TPU v7x, 128 devices: a whole 4x4x4 slice. The times are simulated.
128 devices in a mesh: comp: 2 (over core), dom: 64 (over y, z, x).
Axes of the slice: x: 4, y: 4, z: 4, core: 2. Of those that a mesh axis runs over, the one named last changes fastest.
Arguments:
- column_state: float32 [2, 8, 16, 131072], P('comp', None, None, 'dom'), may hold values from -6 to 6
- vert_rate: float32 [2, 7, 131072], P('comp', None, 'dom'), may hold values from 0.03 to 0.4
- hor_offsets: int32 [2, 6, 131072], P('comp', None, 'dom'), may hold values from -512 to 512, as said below
- hor_coef: float32 [2, 6, 131072], P('comp', None, 'dom'), may hold values from 0.01 to 0.15
- open_mask: int32 [2, 131072], P('comp', 'dom'), may hold values 0 or 1
- couple_rate: float32 [2, 16], P('comp'), may hold values from 0.2 to 0.9
- send_index: int32 [2, 64, 5, 4, 256], P('comp', 'dom'), may hold values from 0 to 2047
- live_slots: int32 [2, 64, 5], P('comp', 'dom'), may hold values from 0 to 4, as said below
- block_source: int32 [2, 64, 8, 2], P('comp', 'dom'), may hold values from 0 to 19
- remap_weight: bfloat16 [2, 64, 8, 2, 256, 256], P('comp', 'dom')
Outputs:
- new_state: float32 [2, 8, 16, 131072], P('comp', None, None, 'dom')
- forcing: float32 [2, 16, 131072], P('comp', None, 'dom')
Inputs may be any that keep to these rules, and one draw needn't show every extreme that they name: `send_index`: entries are column positions within the sending partition's 2048 columns. `hor_offsets`: offsets are nonzero and taken cyclically over the section's 131072 columns. `live_slots`: the pair at offset index 2 always uses all 4 slots.
All inputs are finite; a program needn't handle non-finite values. No bound on the sum of `open_mask` on one device may be relied on, other than what follows from the above.
Results may differ from a plain program's by a relative error of at most 0.0029.
Values may be sent and summed in bfloat16 or wider, within the bound.
No kernel may reach another device: no remote copies, remote signals or barrier semaphores. Data moves between devices by JAX's collectives and lax.ppermute only.
A program may use at most 128 MiB of HBM per device.

v0:
```python
import jax
import jax.numpy as jnp
from jax import lax
from jax.sharding import PartitionSpec as P

RIM = 512
NSUB = 4


def partner(value, axis, apart):
    mask = 2**apart
    pairs = [(source, source ^ mask) for source in range(lax.axis_size(axis))]
    return lax.ppermute(value, axis, pairs)


def passed_along(block, axis, distance):
    devices = range(lax.axis_size(axis))
    route = [((i - distance) % len(devices), i) for i in devices]
    return lax.ppermute(block, axis, route)


def with_halo(block, sides, width):
    for axis, dim in sides:
        count = lax.axis_size(axis)
        forward = [(i, i + 1) for i in range(count - 1)]
        forward.append((count - 1, 0))
        backward = [(target, source) for source, target in forward]
        low = lax.ppermute(
            lax.slice_in_dim(block, block.shape[dim] - width, None, axis=dim), axis, forward
        )
        high = lax.ppermute(lax.slice_in_dim(block, 0, width, axis=dim), axis, backward)
        block = jnp.concatenate([low, block, high], axis=dim)
    return block


def vertical(values, mix_rate):
    interface_flux = mix_rate[:, :, None, :] * (values[:, 1:] - values[:, :-1])
    zero_layer = jnp.zeros_like(values[:, :1])
    return (
        values
        + jnp.concatenate([interface_flux, zero_layer], 1)
        - jnp.concatenate([zero_layer, interface_flux], 1)
    )


def shards(
    column_state,
    vert_rate,
    hor_offsets,
    hor_coef,
    open_mask,
    couple_rate,
    send_index,
    live_slots,
    block_source,
    remap_weight,
):
    levels, fields, columns = (column_state.shape[1], column_state.shape[2], column_state.shape[3])
    partners = live_slots.shape[2]
    radius = partners // 2
    slots = send_index.shape[3]
    width = send_index.shape[4]
    mixed_state = vertical(column_state, vert_rate)
    surface = mixed_state[0, 0]
    flat_index = send_index[0, 0].reshape(-1)
    picked = jnp.take(surface, flat_index, axis=1).reshape(fields, partners, slots, width)
    packed = picked.transpose(1, 2, 0, 3).astype(jnp.bfloat16)
    crossed = partner(packed, "comp", 0)
    pieces = [crossed[k] for k in range(partners)]
    for k in range(partners):
        if k != radius:
            pieces[k] = passed_along(crossed[k], "dom", k - radius)
    received = jnp.stack(pieces, 0)
    received = received.reshape(partners * slots, fields, width)
    slot_valid = (
        (jnp.arange(slots, dtype=jnp.int32)[None, :] < live_slots[0, 0][:, None])
        .astype(jnp.float32)
        .reshape(-1)
    )
    source = block_source[0, 0]
    chosen = received[source]
    source_valid = slot_valid[source]
    weights_here = remap_weight[0, 0]
    product = jnp.einsum(
        "ntib,ntfb->ntfi", weights_here, chosen, preferred_element_type=jnp.float32
    )
    numerator = jnp.sum(product * source_valid[:, :, None, None], axis=1)
    ones_column = jnp.ones((width,), jnp.bfloat16)
    row_sums = jnp.einsum(
        "ntib,b->nti", weights_here, ones_column, preferred_element_type=jnp.float32
    )
    denominator = jnp.maximum(jnp.sum(row_sums * source_valid[:, :, None], axis=1), 1.0)
    blocks = numerator / denominator[:, None, :]
    forcing = blocks.transpose(1, 0, 2).reshape(1, fields, columns)
    open_float = open_mask.astype(jnp.float32)[:, None, :]
    new_top = mixed_state[:, 0] + couple_rate[:, :, None] * open_float * (
        forcing - mixed_state[:, 0]
    )
    current = jnp.concatenate([new_top[:, None], mixed_state[:, 1:]], axis=1)
    channels = levels * fields
    row_state = current.reshape(channels, columns).T
    coef_rows = hor_coef[0].T
    positions = jnp.arange(columns, dtype=jnp.int32) + RIM
    for substep in range(NSUB):
        extended = with_halo(row_state, (("dom", 0),), RIM)
        running = jnp.zeros_like(row_state)
        for j in range(6):
            neighbor = positions + hor_offsets[0, j]
            gathered = jnp.take(extended, neighbor, axis=0)
            running = running + coef_rows[:, j][:, None] * (gathered - row_state)
        row_state = row_state + running
    current = row_state.T.reshape(1, levels, fields, columns)
    return (current, forcing)


def solution(mesh):
    placed = (
        P("comp", None, None, "dom"),
        P("comp", None, "dom"),
        P("comp", None, "dom"),
        P("comp", None, "dom"),
        P("comp", "dom"),
        P("comp", None),
        P("comp", "dom", None, None, None),
        P("comp", "dom", None),
        P("comp", "dom", None, None),
        P("comp", "dom", None, None, None, None),
    )
    return jax.shard_map(
        shards,
        mesh=mesh,
        in_specs=placed,
        out_specs=(P("comp", None, None, "dom"), P("comp", None, "dom")),
        check_vma=False,
    )
```

profile of v0, /device:TPU:0, one launch (start us, length us, event | category | flops | bytes accessed | tf_op | source)
XLA Modules:
  0.0 365.4 jit_solution(992084395934157552)
XLA Ops:
  6.3 18.6 %gather_fusion = bf16[5120,16]{1,0:T(8,128)(2,1)} fusion(bf16[16,2048]{0,1:T(8,128)(2,1)S(1)} %copy.60, s32[5120]{0:T(1024)S(1)} %broadcast_clamp_fusion), kind=kCustom, calls=%fused_computation.24 | custom fusion | bytes 348160 | tf_op jit(solution)/shard_map/jit(_take)/gather | solution.py:66
  30.5 9.1 %collective-permute-start.1 = (bf16[4,16,256]{2,1,0:T(8,128)(2,1)S(1)}, bf16[4,16,256]{2,1,0:T(8,128)(2,1)S(1)}, u32[]{:S(2)}, u32[]{:S(2)}) collective-permute-start(bf16[4,16,256]{2,1,0:T(8,128)(2,1)S(1)} %get-tuple-element.17), channel_id=1, source_target_pairs={{2,0},{3,1},{4,2},{5,3},{6,4},{7,5},{8,6},{9,7},{10,8},{11,9},{12,... | collective-permute-start | bytes 98312 | tf_op jit(solution)/shard_map/ppermute | solution.py:19
  45.5 7.8 %collective-permute-done.3 = bf16[4,16,256]{2,1,0:T(8,128)(2,1)S(1)} collective-permute-done((bf16[4,16,256]{2,1,0:T(8,128)(2,1)S(1)}, bf16[4,16,256]{2,1,0:T(8,128)(2,1)S(1)}, u32[]{:S(2)}, u32[]{:S(2)}) %collective-permute-start.3) | collective-permute-done | bytes 32800 | tf_op jit(solution)/shard_map/ppermute | solution.py:19
  75.2 9.0 %gather_fusion.8 = f32[2048,128]{1,0:T(8,128)} fusion(f32[3072,128]{1,0:T(8,128)} %pad_maximum_fusion, s32[2048]{0:T(1024)S(1)} %get-tuple-element.35), kind=kCustom, calls=%fused_computation.5.clone | custom fusion | bytes 2105344 | tf_op jit(solution)/shard_map/jit(_take)/gather | solution.py:109
  84.2 9.0 %gather_fusion.7 = f32[2048,128]{1,0:T(8,128)} fusion(f32[3072,128]{1,0:T(8,128)} %pad_maximum_fusion, s32[2048]{0:T(1024)S(1)} %get-tuple-element.34), kind=kCustom, calls=%fused_computation.4.clone | custom fusion | bytes 2105344 | tf_op jit(solution)/shard_map/jit(_take)/gather | solution.py:109
  93.2 9.0 %gather_fusion.6 = f32[2048,128]{1,0:T(8,128)} fusion(f32[3072,128]{1,0:T(8,128)} %pad_maximum_fusion, s32[2048]{0:T(1024)S(1)} %get-tuple-element.33), kind=kCustom, calls=%fused_computation.3.clone | custom fusion | bytes 2105344 | tf_op jit(solution)/shard_map/jit(_take)/gather | solution.py:109
  102.1 9.0 %gather_fusion.5 = f32[2048,128]{1,0:T(8,128)} fusion(f32[3072,128]{1,0:T(8,128)} %pad_maximum_fusion, s32[2048]{0:T(1024)S(1)} %get-tuple-element.32), kind=kCustom, calls=%fused_computation.2.clone | custom fusion | bytes 2105344 | tf_op jit(solution)/shard_map/jit(_take)/gather | solution.py:109
  111.1 9.0 %gather_fusion.4 = f32[2048,128]{1,0:T(8,128)} fusion(f32[3072,128]{1,0:T(8,128)} %pad_maximum_fusion, s32[2048]{0:T(1024)S(1)} %get-tuple-element.31), kind=kCustom, calls=%fused_computation.1.clone | custom fusion | bytes 2105344 | tf_op jit(solution)/shard_map/jit(_take)/gather | solution.py:109
  120.0 9.0 %gather_fusion.3 = f32[2048,128]{1,0:T(8,128)} fusion(f32[3072,128]{1,0:T(8,128)} %pad_maximum_fusion, s32[2048]{0:T(1024)S(1)} %get-tuple-element.30), kind=kCustom, calls=%fused_computation.clone | custom fusion | bytes 2105344 | tf_op jit(solution)/shard_map/jit(_take)/gather | solution.py:109
  136.7 7.5 %collective-permute-start.8 = (f32[512,128]{1,0:T(8,128)S(1)}, f32[512,128]{1,0:T(8,128)S(1)}, u32[]{:S(2)}, u32[]{:S(2)}) collective-permute-start(f32[512,128]{1,0:T(8,128)S(1)} %get-tuple-element.10), channel_id=1, source_target_pairs={{1,0},{2,1},{3,2},{4,3},{5,4},{6,5},{7,6},{8,7},{9,8},{10,9},{11,1... | collective-permute-start | bytes 786440 | tf_op jit(solution)/shard_map/ppermute | solution.py:31
  149.7 9.0 %gather_fusion.14 = f32[2048,128]{1,0:T(8,128)} fusion(f32[3072,128]{1,0:T(8,128)} %pad_maximum_fusion.1, s32[2048]{0:T(1024)S(1)} %get-tuple-element.35), kind=kCustom, calls=%fused_computation.11.clone | custom fusion | bytes 2105344 | tf_op jit(solution)/shard_map/jit(_take)/gather | solution.py:109
  158.8 9.0 %gather_fusion.13 = f32[2048,128]{1,0:T(8,128)} fusion(f32[3072,128]{1,0:T(8,128)} %pad_maximum_fusion.1, s32[2048]{0:T(1024)S(1)} %get-tuple-element.34), kind=kCustom, calls=%fused_computation.10.clone | custom fusion | bytes 2105344 | tf_op jit(solution)/shard_map/jit(_take)/gather | solution.py:109
  167.7 9.0 %gather_fusion.12 = f32[2048,128]{1,0:T(8,128)} fusion(f32[3072,128]{1,0:T(8,128)} %pad_maximum_fusion.1, s32[2048]{0:T(1024)S(1)} %get-tuple-element.33), kind=kCustom, calls=%fused_computation.9.clone | custom fusion | bytes 2105344 | tf_op jit(solution)/shard_map/jit(_take)/gather | solution.py:109
  176.7 9.0 %gather_fusion.11 = f32[2048,128]{1,0:T(8,128)} fusion(f32[3072,128]{1,0:T(8,128)} %pad_maximum_fusion.1, s32[2048]{0:T(1024)S(1)} %get-tuple-element.32), kind=kCustom, calls=%fused_computation.8.clone | custom fusion | bytes 2105344 | tf_op jit(solution)/shard_map/jit(_take)/gather | solution.py:109
  185.6 9.0 %gather_fusion.10 = f32[2048,128]{1,0:T(8,128)} fusion(f32[3072,128]{1,0:T(8,128)} %pad_maximum_fusion.1, s32[2048]{0:T(1024)S(1)} %get-tuple-element.31), kind=kCustom, calls=%fused_computation.7.clone | custom fusion | bytes 2105344 | tf_op jit(solution)/shard_map/jit(_take)/gather | solution.py:109
  194.6 9.0 %gather_fusion.9 = f32[2048,128]{1,0:T(8,128)} fusion(f32[3072,128]{1,0:T(8,128)} %pad_maximum_fusion.1, s32[2048]{0:T(1024)S(1)} %get-tuple-element.30), kind=kCustom, calls=%fused_computation.6.clone | custom fusion | bytes 2105344 | tf_op jit(solution)/shard_map/jit(_take)/gather | solution.py:109
  211.0 7.6 %collective-permute-start.10 = (f32[512,128]{1,0:T(8,128)S(1)}, f32[512,128]{1,0:T(8,128)S(1)}, u32[]{:S(2)}, u32[]{:S(2)}) collective-permute-start(f32[512,128]{1,0:T(8,128)S(1)} %get-tuple-element.8), channel_id=1, source_target_pairs={{1,0},{2,1},{3,2},{4,3},{5,4},{6,5},{7,6},{8,7},{9,8},{10,9},{11,1... | collective-permute-start | bytes 786440 | tf_op jit(solution)/shard_map/ppermute | solution.py:31
  224.2 9.0 %gather_fusion.20 = f32[2048,128]{1,0:T(8,128)} fusion(f32[3072,128]{1,0:T(8,128)} %pad_maximum_fusion.2, s32[2048]{0:T(1024)S(1)} %get-tuple-element.35), kind=kCustom, calls=%fused_computation.17.clone | custom fusion | bytes 2105344 | tf_op jit(solution)/shard_map/jit(_take)/gather | solution.py:109
  233.2 9.0 %gather_fusion.19 = f32[2048,128]{1,0:T(8,128)} fusion(f32[3072,128]{1,0:T(8,128)} %pad_maximum_fusion.2, s32[2048]{0:T(1024)S(1)} %get-tuple-element.34), kind=kCustom, calls=%fused_computation.16.clone | custom fusion | bytes 2105344 | tf_op jit(solution)/shard_map/jit(_take)/gather | solution.py:109
  242.1 9.0 %gather_fusion.18 = f32[2048,128]{1,0:T(8,128)} fusion(f32[3072,128]{1,0:T(8,128)} %pad_maximum_fusion.2, s32[2048]{0:T(1024)S(1)} %get-tuple-element.33), kind=kCustom, calls=%fused_computation.15.clone | custom fusion | bytes 2105344 | tf_op jit(solution)/shard_map/jit(_take)/gather | solution.py:109
  251.1 9.0 %gather_fusion.17 = f32[2048,128]{1,0:T(8,128)} fusion(f32[3072,128]{1,0:T(8,128)} %pad_maximum_fusion.2, s32[2048]{0:T(1024)S(1)} %get-tuple-element.32), kind=kCustom, calls=%fused_computation.14.clone | custom fusion | bytes 2105344 | tf_op jit(solution)/shard_map/jit(_take)/gather | solution.py:109
  260.0 9.0 %gather_fusion.16 = f32[2048,128]{1,0:T(8,128)} fusion(f32[3072,128]{1,0:T(8,128)} %pad_maximum_fusion.2, s32[2048]{0:T(1024)S(1)} %get-tuple-element.31), kind=kCustom, calls=%fused_computation.13.clone | custom fusion | bytes 2105344 | tf_op jit(solution)/shard_map/jit(_take)/gather | solution.py:109
  269.0 9.0 %gather_fusion.15 = f32[2048,128]{1,0:T(8,128)} fusion(f32[3072,128]{1,0:T(8,128)} %pad_maximum_fusion.2, s32[2048]{0:T(1024)S(1)} %get-tuple-element.30), kind=kCustom, calls=%fused_computation.12.clone | custom fusion | bytes 2105344 | tf_op jit(solution)/shard_map/jit(_take)/gather | solution.py:109
  278.0 7.5 %fusion.25 = f32[2048,128]{1,0:T(8,128)S(1)} fusion(f32[2048,128]{1,0:T(8,128)} %copy-done.1, f32[2048,128]{1,0:T(8,128)} %gather_fusion.20, f32[2048,128]{1,0:T(8,128)} %gather_fusion.19, f32[2048,128]{1,0:T(8,128)} %gather_fusion.18, f32[2048,128]{1,0:T(8,128)} %gather_fusion.17, f32[2048,128]{1,0:T(8,128)} %gather_fusion.16, ...), kind=kLoop, calls=%fused_computation.60 | loop fusion | flops 6291456 | bytes 8450048 | tf_op jit(solution)/shard_map/add | solution.py:111
  286.4 7.5 %collective-permute-start.12 = (f32[512,128]{1,0:T(8,128)}, f32[512,128]{1,0:T(8,128)}, u32[]{:S(2)}, u32[]{:S(2)}) collective-permute-start(f32[512,128]{1,0:T(8,128)} %get-tuple-element.6), channel_id=1, source_target_pairs={{1,0},{2,1},{3,2},{4,3},{5,4},{6,5},{7,6},{8,7},{9,8},{10,9},{11,1... | collective-permute-start | bytes 786440 | tf_op jit(solution)/shard_map/ppermute | solution.py:31
  300.7 9.0 %gather_fusion.26 = f32[2048,128]{1,0:T(8,128)} fusion(f32[3072,128]{1,0:T(8,128)} %pad_maximum_fusion.3, s32[2048]{0:T(1024)S(1)} %copy-done.25), kind=kCustom, calls=%fused_computation.23.clone | custom fusion | bytes 2105344 | tf_op jit(solution)/shard_map/jit(_take)/gather | solution.py:109
  309.7 9.0 %gather_fusion.25 = f32[2048,128]{1,0:T(8,128)} fusion(f32[3072,128]{1,0:T(8,128)} %pad_maximum_fusion.3, s32[2048]{0:T(1024)S(1)} %copy-done.23), kind=kCustom, calls=%fused_computation.22.clone | custom fusion | bytes 2105344 | tf_op jit(solution)/shard_map/jit(_take)/gather | solution.py:109
  318.7 9.0 %gather_fusion.24 = f32[2048,128]{1,0:T(8,128)} fusion(f32[3072,128]{1,0:T(8,128)} %pad_maximum_fusion.3, s32[2048]{0:T(1024)S(1)} %copy-done.17), kind=kCustom, calls=%fused_computation.21.clone | custom fusion | bytes 2105344 | tf_op jit(solution)/shard_map/jit(_take)/gather | solution.py:109
  327.7 9.0 %gather_fusion.23 = f32[2048,128]{1,0:T(8,128)} fusion(f32[3072,128]{1,0:T(8,128)} %pad_maximum_fusion.3, s32[2048]{0:T(1024)S(1)} %copy-done.15), kind=kCustom, calls=%fused_computation.20.clone | custom fusion | bytes 2105344 | tf_op jit(solution)/shard_map/jit(_take)/gather | solution.py:109
  336.7 9.0 %gather_fusion.22 = f32[2048,128]{1,0:T(8,128)} fusion(f32[3072,128]{1,0:T(8,128)} %pad_maximum_fusion.3, s32[2048]{0:T(1024)S(1)} %copy-done.21), kind=kCustom, calls=%fused_computation.19.clone | custom fusion | bytes 2105344 | tf_op jit(solution)/shard_map/jit(_take)/gather | solution.py:109
  345.7 9.0 %gather_fusion.21 = f32[2048,128]{1,0:T(8,128)} fusion(f32[3072,128]{1,0:T(8,128)} %pad_maximum_fusion.3, s32[2048]{0:T(1024)S(1)} %copy-done.19), kind=kCustom, calls=%fused_computation.18.clone | custom fusion | bytes 2105344 | tf_op jit(solution)/shard_map/jit(_take)/gather | solution.py:109
  354.8 8.1 %fusion.13 = f32[128,2048]{0,1:T(8,128)} fusion(f32[2048,128]{1,0:T(8,128)S(1)} %fusion.25, f32[2048,128]{1,0:T(8,128)} %gather_fusion.26, f32[2048,128]{1,0:T(8,128)} %gather_fusion.25, f32[2048,128]{1,0:T(8,128)} %gather_fusion.24, f32[2048,128]{1,0:T(8,128)} %gather_fusion.23, f32[2048,128]{1,0:T(8,128)} %gather_fusion.22, f32[2048,128]{1,0:T(8,128)} %gather_fusion.21, ...), kind=kLoop, calls=%fused_computation.42 | loop fusion | flops 6291456 | bytes 8450048 | tf_op jit(solution)/shard_map/transpose | solution.py:112
  (173 shorter events, 75.0 us)
Async XLA Ops:
  0.6 29.0 %copy-start = (bf16[1,1,8,2,256,256]{5,4,3,2,1,0:T(8,128)(2,1)S(1)}, bf16[1,1,8,2,256,256]{5,4,3,2,1,0:T(8,128)(2,1)}, u32[]{:S(2)}) copy-start(bf16[1,1,8,2,256,256]{5,4,3,2,1,0:T(8,128)(2,1)} %param.21) | copy-start | bytes 6291460
  6.3 21.0 %copy-start.40 = (s32[1,6,2048]{2,0,1:T(1,128)S(1)}, s32[1,6,2048]{2,0,1:T(1,128)}, u32[]{:S(2)}) copy-start(s32[1,6,2048]{2,0,1:T(1,128)} %param.14) | copy-start | bytes 147460
  6.3 21.6 %copy-start.43 = (s32[1,1,8,2]{2,3,1,0:T(2,128)S(1)}, s32[1,1,8,2]{2,3,1,0:T(2,128)}, u32[]{:S(2)}) copy-start(s32[1,1,8,2]{2,3,1,0:T(2,128)} %param.20) | copy-start | bytes 196
  6.3 21.8 %copy-start.45 = (s32[1,1,5]{2,1,0:T(1,128)S(1)}, s32[1,1,5]{2,1,0:T(1,128)}, u32[]{:S(2)}) copy-start(s32[1,1,5]{2,1,0:T(1,128)} %param.19) | copy-start | bytes 64
  27.3 3.2 collective-permute-start
  27.9 214.2 %copy-start.16 = (s32[2048]{0:T(1024)}, s32[2048]{0:T(1024)S(1)}, u32[]{:S(2)}) copy-start(s32[2048]{0:T(1024)S(1)} %get-tuple-element.33) | copy-start | bytes 24580
  27.9 223.2 %copy-start.14 = (s32[2048]{0:T(1024)}, s32[2048]{0:T(1024)S(1)}, u32[]{:S(2)}) copy-start(s32[2048]{0:T(1024)S(1)} %get-tuple-element.32) | copy-start | bytes 24580
  28.9 15.4 %copy-start.5 = (f32[1,8,16,2048]{3,2,1,0:T(8,128)S(1)}, f32[1,8,16,2048]{3,2,1,0:T(8,128)}, u32[]{:S(2)}) copy-start(f32[1,8,16,2048]{3,2,1,0:T(8,128)} %copy-done.4) | copy-start | bytes 3145732
  30.4 247.6 %copy-start.6 = (f32[2048,1]{0,1:T(1,128)}, f32[2048,1]{0,1:T(1,128)S(1)}, u32[]{:S(2)}) copy-start(f32[2048,1]{0,1:T(1,128)S(1)} %get-tuple-element.20) | copy-start | bytes 24580
  30.4 247.6 %copy-start.8 = (f32[2048,1]{0,1:T(1,128)}, f32[2048,1]{0,1:T(1,128)S(1)}, u32[]{:S(2)}) copy-start(f32[2048,1]{0,1:T(1,128)S(1)} %get-tuple-element.21) | copy-start | bytes 24580
  30.4 247.6 %copy-start.10 = (f32[2048,1]{0,1:T(1,128)}, f32[2048,1]{0,1:T(1,128)S(1)}, u32[]{:S(2)}) copy-start(f32[2048,1]{0,1:T(1,128)S(1)} %get-tuple-element.22) | copy-start | bytes 24580
  30.4 247.6 %copy-start.12 = (f32[2048,1]{0,1:T(1,128)}, f32[2048,1]{0,1:T(1,128)S(1)}, u32[]{:S(2)}) copy-start(f32[2048,1]{0,1:T(1,128)S(1)} %get-tuple-element.23) | copy-start | bytes 24580
  30.5 229.6 %copy-start.20 = (s32[2048]{0:T(1024)}, s32[2048]{0:T(1024)S(1)}, u32[]{:S(2)}) copy-start(s32[2048]{0:T(1024)S(1)} %get-tuple-element.31) | copy-start | bytes 24580
  30.5 238.5 %copy-start.18 = (s32[2048]{0:T(1024)}, s32[2048]{0:T(1024)S(1)}, u32[]{:S(2)}) copy-start(s32[2048]{0:T(1024)S(1)} %get-tuple-element.30) | copy-start | bytes 24580
  30.5 247.5 %copy-start.31 = (pred[2048]{0:T(1024)(128)(4,1)}, pred[2048]{0:T(1024)(128)(4,1)S(1)}, u32[]{:S(2)}) copy-start(pred[2048]{0:T(1024)(128)(4,1)S(1)} %get-tuple-element.40) | copy-start | bytes 6148
  30.5 247.5 %copy-start.33 = (pred[2048]{0:T(1024)(128)(4,1)}, pred[2048]{0:T(1024)(128)(4,1)S(1)}, u32[]{:S(2)}) copy-start(pred[2048]{0:T(1024)(128)(4,1)S(1)} %get-tuple-element.41) | copy-start | bytes 6148
  30.5 10.7 %collective-permute-start.1 = (bf16[4,16,256]{2,1,0:T(8,128)(2,1)S(1)}, bf16[4,16,256]{2,1,0:T(8,128)(2,1)S(1)}, u32[]{:S(2)}, u32[]{:S(2)}) collective-permute-start(bf16[4,16,256]{2,1,0:T(8,128)(2,1)S(1)} %get-tuple-element.17), channel_id=1, source_target_pairs={{2,0},{3,1},{4,2},{5,3},{6,4},{7,5},{8,6},{9,7},{10,8},{11,9},{12,... | collective-permute-start | bytes 98312 | tf_op jit(solution)/shard_map/ppermute | solution.py:19
  39.7 3.9 %collective-permute-start.2 = (bf16[4,16,256]{2,1,0:T(8,128)(2,1)S(1)}, bf16[4,16,256]{2,1,0:T(8,128)(2,1)S(1)}, u32[]{:S(2)}, u32[]{:S(2)}) collective-permute-start(bf16[4,16,256]{2,1,0:T(8,128)(2,1)S(1)} %get-tuple-element.16), channel_id=1, source_target_pairs={{1,0},{2,1},{3,2},{4,3},{5,4},{6,5},{7,6},{8,7},{9,8},{10,9},{11,1... | collective-permute-start | bytes 98312 | tf_op jit(solution)/shard_map/ppermute | solution.py:19
  43.7 9.6 %collective-permute-start.3 = (bf16[4,16,256]{2,1,0:T(8,128)(2,1)S(1)}, bf16[4,16,256]{2,1,0:T(8,128)(2,1)S(1)}, u32[]{:S(2)}, u32[]{:S(2)}) collective-permute-start(bf16[4,16,256]{2,1,0:T(8,128)(2,1)S(1)} %get-tuple-element.14), channel_id=1, source_target_pairs={{63,0},{0,1},{1,2},{2,3},{3,4},{4,5},{5,6},{6,7},{7,8},{8,9},{9,10... | collective-permute-start | bytes 98312 | tf_op jit(solution)/shard_map/ppermute | solution.py:19
  45.4 9.7 %collective-permute-start.4 = (bf16[4,16,256]{2,1,0:T(8,128)(2,1)S(1)}, bf16[4,16,256]{2,1,0:T(8,128)(2,1)S(1)}, u32[]{:S(2)}, u32[]{:S(2)}) collective-permute-start(bf16[4,16,256]{2,1,0:T(8,128)(2,1)S(1)} %get-tuple-element.13), channel_id=1, source_target_pairs={{62,0},{63,1},{0,2},{1,3},{2,4},{3,5},{4,6},{5,7},{6,8},{7,9},{8,1... | collective-permute-start | bytes 98312 | tf_op jit(solution)/shard_map/ppermute | solution.py:19
  62.0 11.9 %collective-permute-start.5 = (f32[512,128]{1,0:T(8,128)S(1)}, f32[512,128]{1,0:T(8,128)S(1)}, u32[]{:S(2)}, u32[]{:S(2)}) collective-permute-start(f32[512,128]{1,0:T(8,128)S(1)} %get-tuple-element.11), channel_id=1, source_target_pairs={{0,1},{1,2},{2,3},{3,4},{4,5},{5,6},{6,7},{7,8},{8,9},{9,10},{10,1... | collective-permute-start | bytes 786440 | tf_op jit(solution)/shard_map/ppermute | solution.py:28
  62.1 11.8 %collective-permute-start.6 = (f32[512,128]{1,0:T(8,128)S(1)}, f32[512,128]{1,0:T(8,128)S(1)}, u32[]{:S(2)}, u32[]{:S(2)}) collective-permute-start(f32[512,128]{1,0:T(8,128)S(1)} %get-tuple-element.12), channel_id=1, source_target_pairs={{1,0},{2,1},{3,2},{4,3},{5,4},{6,5},{7,6},{8,7},{9,8},{10,9},{11,1... | collective-permute-start | bytes 786440 | tf_op jit(solution)/shard_map/ppermute | solution.py:31
  69.6 208.5 %copy-start.35 = (pred[2048]{0:T(1024)(128)(4,1)}, pred[2048]{0:T(1024)(128)(4,1)S(1)}, u32[]{:S(2)}) copy-start(pred[2048]{0:T(1024)(128)(4,1)S(1)} %get-tuple-element.36) | copy-start | bytes 6148
  69.6 208.5 %copy-start.37 = (pred[2048]{0:T(1024)(128)(4,1)}, pred[2048]{0:T(1024)(128)(4,1)S(1)}, u32[]{:S(2)}) copy-start(pred[2048]{0:T(1024)(128)(4,1)S(1)} %get-tuple-element.37) | copy-start | bytes 6148
  69.6 154.6 %copy-start.24 = (s32[2048]{0:T(1024)}, s32[2048]{0:T(1024)S(1)}, u32[]{:S(2)}) copy-start(s32[2048]{0:T(1024)S(1)} %get-tuple-element.35) | copy-start | bytes 24580
  69.6 163.6 %copy-start.22 = (s32[2048]{0:T(1024)}, s32[2048]{0:T(1024)S(1)}, u32[]{:S(2)}) copy-start(s32[2048]{0:T(1024)S(1)} %get-tuple-element.34) | copy-start | bytes 24580
  136.6 11.9 %collective-permute-start.7 = (f32[512,128]{1,0:T(8,128)S(1)}, f32[512,128]{1,0:T(8,128)S(1)}, u32[]{:S(2)}, u32[]{:S(2)}) collective-permute-start(f32[512,128]{1,0:T(8,128)S(1)} %get-tuple-element.9), channel_id=1, source_target_pairs={{0,1},{1,2},{2,3},{3,4},{4,5},{5,6},{6,7},{7,8},{8,9},{9,10},{10,1... | collective-permute-start | bytes 786440 | tf_op jit(solution)/shard_map/ppermute | solution.py:28
  136.7 11.8 %collective-permute-start.8 = (f32[512,128]{1,0:T(8,128)S(1)}, f32[512,128]{1,0:T(8,128)S(1)}, u32[]{:S(2)}, u32[]{:S(2)}) collective-permute-start(f32[512,128]{1,0:T(8,128)S(1)} %get-tuple-element.10), channel_id=1, source_target_pairs={{1,0},{2,1},{3,2},{4,3},{5,4},{6,5},{7,6},{8,7},{9,8},{10,9},{11,1... | collective-permute-start | bytes 786440 | tf_op jit(solution)/shard_map/ppermute | solution.py:31
  211.0 11.9 %collective-permute-start.9 = (f32[512,128]{1,0:T(8,128)S(1)}, f32[512,128]{1,0:T(8,128)S(1)}, u32[]{:S(2)}, u32[]{:S(2)}) collective-permute-start(f32[512,128]{1,0:T(8,128)S(1)} %get-tuple-element.7), channel_id=1, source_target_pairs={{0,1},{1,2},{2,3},{3,4},{4,5},{5,6},{6,7},{7,8},{8,9},{9,10},{10,1... | collective-permute-start | bytes 786440 | tf_op jit(solution)/shard_map/ppermute | solution.py:28
  211.0 11.9 %collective-permute-start.10 = (f32[512,128]{1,0:T(8,128)S(1)}, f32[512,128]{1,0:T(8,128)S(1)}, u32[]{:S(2)}, u32[]{:S(2)}) collective-permute-start(f32[512,128]{1,0:T(8,128)S(1)} %get-tuple-element.8), channel_id=1, source_target_pairs={{1,0},{2,1},{3,2},{4,3},{5,4},{6,5},{7,6},{8,7},{9,8},{10,9},{11,1... | collective-permute-start | bytes 786440 | tf_op jit(solution)/shard_map/ppermute | solution.py:31
  286.4 12.1 %collective-permute-start.11 = (f32[512,128]{1,0:T(8,128)}, f32[512,128]{1,0:T(8,128)S(1)}, u32[]{:S(2)}, u32[]{:S(2)}) collective-permute-start(f32[512,128]{1,0:T(8,128)} %get-tuple-element.5), channel_id=1, source_target_pairs={{0,1},{1,2},{2,3},{3,4},{4,5},{5,6},{6,7},{7,8},{8,9},{9,10},{10,1... | collective-permute-start | bytes 786440 | tf_op jit(solution)/shard_map/ppermute | solution.py:28
  286.4 12.1 %collective-permute-start.12 = (f32[512,128]{1,0:T(8,128)}, f32[512,128]{1,0:T(8,128)}, u32[]{:S(2)}, u32[]{:S(2)}) collective-permute-start(f32[512,128]{1,0:T(8,128)} %get-tuple-element.6), channel_id=1, source_target_pairs={{1,0},{2,1},{3,2},{4,3},{5,4},{6,5},{7,6},{8,7},{9,8},{10,9},{11,1... | collective-permute-start | bytes 786440 | tf_op jit(solution)/shard_map/ppermute | solution.py:31
  (27 other events, 217.8 us)
where the time goes:
time: 367 us; the launch traced here: 365 us
  local copies, waits for them, and re-layouts  249 us (68%)
  other arithmetic  43.1 us (12%)
  starting transfers between devices  41.3 us (11%)
  waiting for transfers between devices  29.1 us (8%)
    gather x24, local copies, waits for them, and re-layouts, shards(): gathered = jnp.take(extended, neighbor, axis=0)  215 us
    ppermute x4, starting transfers between devices, with_halo(): lax.ppermute(lax.slice_in_dim(block, 0, width, axis=dim), axis, backward)  30.1 us
    add x3, other arithmetic, shards(): row_state = row_state + running  22.3 us
    gather x2, local copies, waits for them, and re-layouts, shards(): jnp.take(surface, flat_index, axis=1)  20.3 us
    ppermute x4, waiting for transfers between devices, with_halo(): lax.ppermute(lax.slice_in_dim(block, block.shape[dim] - width, None, axis...  16.7 us
    ppermute x4, waiting for transfers between devices, passed_along(): return lax.ppermute(block, axis, route)  12.4 us
    ppermute x4, starting transfers between devices, passed_along(): return lax.ppermute(block, axis, route)  11 us
    transpose x1, other arithmetic, shards(): current = row_state.T.reshape(1, levels, fields, columns)  8.14 us
  transfers between devices with their start and end apart: 13, of which 8 were waited for; matrix products, arithmetic and copies ran while one was open for 1% of the time, Pallas kernels for 0%

commit v1 on v0

v1 whole, which is shorter than its diff:
```python
import jax
import jax.numpy as jnp
from jax import lax
from jax.experimental import pallas as pl
from jax.experimental.pallas import tpu as pltpu
from jax.sharding import PartitionSpec as P

F32, BF16 = jnp.float32, jnp.bfloat16
RIM = 512
NSUB = 4
TB = 256
WIN = TB + 2 * RIM
LANE = 128
NEVER = 8192.0
FIELDS, LEVELS, COLS = 16, 8, 2048
REST = (LEVELS - 1) * FIELDS
WIDE = COLS - RIM
VMEM_LIMIT = 56 * 2**20


def mix_kernel(state, rate, offs, coef, send, mix0, mixr, bulk, p0, p1, p2, p3, p4, tab_own, tab_low, tab_high):
    packed = (p0, p1, p2, p3, p4)
    for c in range(0, COLS, TB):
        here = slice(c, c + TB)
        v0 = state[0, :, here]
        mix0[:, here] = v0 + rate[0:1, here] * (state[1, :, here] - v0)
    for k in range(5):
        for j in range(4):
            for h in range(2):
                index = send[k, j : j + 1, h * LANE : (h + 1) * LANE]
                low = jnp.broadcast_to(index & (LANE - 1), (FIELDS, LANE))
                high = jnp.broadcast_to(lax.shift_right_logical(index, 7), (FIELDS, LANE))
                total = jnp.zeros((FIELDS, LANE), F32)
                for s in range(COLS // LANE):
                    got = jnp.take_along_axis(
                        mix0[:, s * LANE : (s + 1) * LANE], low, axis=1, mode="promise_in_bounds"
                    )
                    total = jnp.where(high == s, got, total)
                packed[k][j, :, h * LANE : (h + 1) * LANE] = total.astype(BF16)
    for c in range(0, COLS, TB):
        here = slice(c, c + TB)
        lane = lax.broadcasted_iota(jnp.int32, (1, TB), 1).astype(F32) + float(RIM)
        off = [offs[j : j + 1, here].astype(F32) for j in range(6)]
        val = [coef[j : j + 1, here] for j in range(6)]
        whole = jnp.zeros((1, TB), F32)
        rows_c, rows_p = [], []
        for j in range(6):
            merged = val[j]
            first = jnp.ones((1, TB), F32)
            for i in range(6):
                if i != j:
                    same = off[i] == off[j]
                    merged = merged + jnp.where(same, val[i], 0.0)
                    if i < j:
                        first = jnp.where(same, 0.0, first)
            merged = (merged * first).astype(BF16).astype(F32)
            whole = whole + merged
            rows_c.append(merged)
            rows_p.append(jnp.where(first > 0.5, off[j] + lane, NEVER))
        pad = [jnp.zeros((1, TB), F32)] * 3
        block = jnp.concatenate(rows_c + rows_p + [whole] + pad, axis=0)
        tab_own[:, here] = block
        if c < WIDE:
            tab_low[:, here] = block
        if c >= RIM:
            tab_high[:, c - RIM : c - RIM + TB] = block
    for c in range(0, COLS, TB):
        here = slice(c, c + TB)
        before = state[0, :, here]
        mid = state[1, :, here]
        flux = rate[0:1, here] * (mid - before)
        for l in range(1, LEVELS):
            if l < LEVELS - 1:
                after = state[l + 1, :, here]
                below = rate[l : l + 1, here] * (after - mid)
                new = mid + below - flux
                flux, mid = below, after
            else:
                new = mid - flux
            mixr[(l - 1) * FIELDS : l * FIELDS, here] = new
            bulk[(l - 1) * FIELDS : l * FIELDS, here] = new.astype(BF16)


def band_kernel(left, own, right, band, tab):
    b = pl.program_id(0)
    nl = WIDE // TB
    no = COLS // TB

    @pl.when(b < nl)
    def _():
        tab[...] = left[:, pl.ds(pl.multiple_of(b * TB, TB), TB)]

    @pl.when((b >= nl) & (b < nl + no))
    def _():
        tab[...] = own[:, pl.ds(pl.multiple_of((b - nl) * TB, TB), TB)]

    @pl.when(b >= nl + no)
    def _():
        tab[...] = right[:, pl.ds(pl.multiple_of((b - nl - no) * TB, TB), TB)]

    for half in range(TB // LANE):
        lanes = slice(half * LANE, (half + 1) * LANE)
        coefs = [jnp.broadcast_to(tab[j : j + 1, lanes], (16, LANE)).astype(BF16) for j in range(6)]
        first_row = half * LANE
        last_row = first_row + LANE + 2 * RIM
        if first_row:
            band[0, 0:first_row, lanes] = jnp.zeros((first_row, LANE), BF16)
        if last_row < WIN:
            band[0, last_row:WIN, lanes] = jnp.zeros((WIN - last_row, LANE), BF16)
        for base in range(first_row, last_row, LANE):
            rel = [
                jnp.broadcast_to(
                    jnp.clip(tab[6 + j : 7 + j, lanes] - float(base), -1.0, float(LANE)), (16, LANE)
                ).astype(BF16)
                for j in range(6)
            ]
            for r in range(0, LANE, 16):
                row = (lax.broadcasted_iota(jnp.int32, (16, LANE), 0).astype(F32) + float(r)).astype(BF16)
                total = jnp.zeros((16, LANE), BF16)
                for j in range(6):
                    total = jnp.where(rel[j] == row, coefs[j], total)
                band[0, base + r : base + r + 16, lanes] = total


def remap_kernel(live, source, r0, r1, r2, r3, r4, weights, mix0, mask, rate, forcing, top, top_half, got):
    for k, piece in enumerate((r0, r1, r2, r3, r4)):
        got[4 * k : 4 * k + 4] = piece[...]
    ones = jnp.ones((16, TB), BF16)
    for n in range(COLS // TB):
        here = slice(n * TB, (n + 1) * TB)
        num = jnp.zeros((FIELDS, TB), F32)
        den = jnp.zeros((1, TB), F32)
        for m in range(2):
            q = source[n, m]
            valid = jnp.where((q & 3) < live[lax.shift_right_logical(q, 2)], 1.0, 0.0).astype(F32)
            rows = jnp.concatenate([got[q], ones], axis=0)
            both = lax.dot_general(
                rows, weights[n, m], (((1,), (1,)), ((), ())), preferred_element_type=F32
            )
            num = num + valid * both[0:FIELDS]
            den = den + valid * both[FIELDS : FIELDS + 1]
        value = num / jnp.maximum(den, 1.0)
        forcing[:, here] = value
        old = mix0[:, here]
        new = old + rate[...] * mask[0:1, here].astype(F32) * (value - old)
        top[:, here] = new
        top_half[:, here] = new.astype(BF16)


def diffuse_kernel(
    band, mixr, bulk, bulk_l, bulk_r, top, top_half, top_l, top_r, tab_l, tab_o, tab_r,
    out, bands, xa, xb, st, whole, sems, band_sems,
):
    nb = band.shape[0]
    copies = [
        (bulk_l, xa.at[FIELDS:, 0:COLS]),
        (bulk, xa.at[FIELDS:, COLS : 2 * COLS]),
        (bulk_r, xa.at[FIELDS:, 2 * COLS : 3 * COLS]),
        (top_l, xa.at[0:FIELDS, 0:COLS]),
        (top_half, xa.at[0:FIELDS, COLS : 2 * COLS]),
        (top_r, xa.at[0:FIELDS, 2 * COLS : 3 * COLS]),
        (mixr, st.at[FIELDS:, WIDE : WIDE + COLS]),
        (top, st.at[0:FIELDS, WIDE : WIDE + COLS]),
    ]
    copies = [pltpu.make_async_copy(a, b, sems.at[i]) for i, (a, b) in enumerate(copies)]
    for c in copies:
        c.start()
    fetch = [pltpu.make_async_copy(band.at[i], bands.at[i], band_sems.at[i]) for i in range(nb)]
    for c in fetch:
        c.start()
    whole[:, 0:WIDE] = 1.0 - tab_l[12:13]
    whole[:, WIDE : WIDE + COLS] = 1.0 - tab_o[12:13]
    whole[:, WIDE + COLS :] = 1.0 - tab_r[12:13]
    for c in copies:
        c.wait()
    bufs = (xa, xb)
    edge = WIDE // TB
    for step in range(NSUB):
        src, dst = bufs[step % 2], bufs[(step + 1) % 2]
        skip = step * (RIM // TB)
        for b in range(skip, nb - skip):
            if step == 0:
                fetch[b].wait()
            at = slice(b * TB, (b + 1) * TB)
            here = slice(RIM + b * TB, RIM + (b + 1) * TB)
            acc = jnp.dot(src[:, b * TB : b * TB + WIN], bands[b], preferred_element_type=F32)
            if step == 0 and (b < edge or b >= nb - edge):
                old = src[:, here].astype(F32)
            else:
                old = st[:, at]
            new = old * whole[:, at] + acc
            if step < NSUB - 1:
                st[:, at] = new
                dst[:, here] = new.astype(BF16)
            else:
                out[:, (b - edge) * TB : (b - edge + 1) * TB] = new


def neighbour(value, flip, apart):
    size = (lax.axis_size("comp"), lax.axis_size("dom"))
    pairs = [
        (s * size[1] + d, (s ^ flip) * size[1] + (d + apart) % size[1])
        for s in range(size[0])
        for d in range(size[1])
    ]
    return lax.ppermute(value, ("comp", "dom"), pairs)


def spec(n):
    return [pl.BlockSpec(memory_space=pltpu.VMEM)] * n


ANYWHERE = pl.BlockSpec(memory_space=pl.ANY)
SCALARS = pl.BlockSpec(memory_space=pltpu.SMEM)


def params(**more):
    return pltpu.CompilerParams(vmem_limit_bytes=VMEM_LIMIT, **more)


def shards(
    column_state, vert_rate, hor_offsets, hor_coef, open_mask, couple_rate, send_index, live_slots, block_source,
    remap_weight,
):
    shape = jax.ShapeDtypeStruct
    block = shape((4, FIELDS, TB), BF16)
    mix0, mixr, bulk, p0, p1, p2, p3, p4, tab_own, tab_low, tab_high = pl.pallas_call(
        mix_kernel,
        out_shape=[
            shape((FIELDS, COLS), F32),
            shape((REST, COLS), F32),
            shape((REST, COLS), BF16),
            block, block, block, block, block,
            shape((16, COLS), F32),
            shape((16, WIDE), F32),
            shape((16, WIDE), F32),
        ],
        in_specs=spec(5),
        out_specs=spec(11),
        compiler_params=params(),
        name="mix",
    )(column_state[0], vert_rate[0], hor_offsets[0], hor_coef[0], send_index[0, 0])

    tab_left = neighbour(tab_high, 0, 1)
    tab_right = neighbour(tab_low, 0, -1)
    received = [neighbour(p, 1, k - 2) for k, p in enumerate((p0, p1, p2, p3, p4))]
    bulk_left = neighbour(bulk, 0, 1)
    bulk_right = neighbour(bulk, 0, -1)

    nb = (COLS + 2 * WIDE) // TB
    band = pl.pallas_call(
        band_kernel,
        grid=(nb,),
        out_shape=shape((nb, WIN, TB), BF16),
        in_specs=spec(3),
        out_specs=pl.BlockSpec((1, WIN, TB), lambda b: (b, 0, 0)),
        scratch_shapes=[pltpu.VMEM((16, TB), F32)],
        compiler_params=params(),
        cost_estimate=pl.CostEstimate(flops=0, bytes_accessed=30_000_000, transcendentals=0),
        name="band",
    )(tab_left, tab_own, tab_right)

    forcing, top, top_half = pl.pallas_call(
        remap_kernel,
        out_shape=[shape((FIELDS, COLS), F32), shape((FIELDS, COLS), F32), shape((FIELDS, COLS), BF16)],
        in_specs=[SCALARS, SCALARS] + spec(9),
        out_specs=spec(3),
        scratch_shapes=[pltpu.VMEM((20, FIELDS, TB), BF16)],
        compiler_params=params(),
        name="remap",
    )(live_slots[0, 0], block_source[0, 0], *received, remap_weight[0, 0], mix0, open_mask, couple_rate[0][:, None])

    top_left = neighbour(top_half, 0, 1)
    top_right = neighbour(top_half, 0, -1)

    state = pl.pallas_call(
        diffuse_kernel,
        out_shape=shape((LEVELS * FIELDS, COLS), F32),
        in_specs=[ANYWHERE] * 9 + spec(3),
        out_specs=pl.BlockSpec(memory_space=pltpu.VMEM),
        scratch_shapes=[
            pltpu.VMEM((nb, WIN, TB), BF16),
            pltpu.VMEM((LEVELS * FIELDS, 3 * COLS), BF16),
            pltpu.VMEM((LEVELS * FIELDS, 3 * COLS), BF16),
            pltpu.VMEM((LEVELS * FIELDS, COLS + 2 * WIDE), F32),
            pltpu.VMEM((1, COLS + 2 * WIDE), F32),
            pltpu.SemaphoreType.DMA((8,)),
            pltpu.SemaphoreType.DMA((nb,)),
        ],
        compiler_params=params(),
        name="diffuse",
    )(band, mixr, bulk, bulk_left, bulk_right, top, top_half, top_left, top_right, tab_left, tab_own, tab_right)
    return state.reshape(1, LEVELS, FIELDS, COLS), forcing[None]


def solution(mesh):
    placed = (
        P("comp", None, None, "dom"),
        P("comp", None, "dom"),
        P("comp", None, "dom"),
        P("comp", None, "dom"),
        P("comp", "dom"),
        P("comp", None),
        P("comp", "dom", None, None, None),
        P("comp", "dom", None),
        P("comp", "dom", None, None),
        P("comp", "dom", None, None, None, None),
    )
    return jax.shard_map(
        shards,
        mesh=mesh,
        in_specs=placed,
        out_specs=(P("comp", None, None, "dom"), P("comp", None, "dom")),
        check_vma=False,
    )
```

time: 367 us -> 80.9 us (0.22)
  local copies, waits for them, and re-layouts: 249 us -> 9.16 us
  other arithmetic: 43.1 us -> 0 us
  Pallas kernels: 0 us -> 36.9 us
  starting transfers between devices: 41.3 us -> 19.2 us
  waiting for transfers between devices: 29.1 us -> 13.7 us
    gather x30 -> x0, local copies, waits for them, and re-layouts: 238 us -> none  [the longest x24 215 us: shards(): gathered = jnp.take(extended, neighbor, axis=0)]
    pallas_call x0 -> x4, Pallas kernels: none -> 36.9 us  [the longest x1 17 us: shards(): pl.pallas_call(diffuse_kernel, out_shape=shape((LEVELS * FIELDS, COLS), F...]
    add x4 -> x0, other arithmetic: 22.4 us -> none  [the longest x3 22.3 us: shards(): row_state = row_state + running]
    ppermute x13 -> x11, starting transfers between devices: 41.3 us -> 19.2 us  [neighbour(): return lax.ppermute(value, ('comp', 'dom'), pairs)]
    ppermute x13 -> x11, waiting for transfers between devices: 29.1 us -> 13.7 us  [neighbour(): return lax.ppermute(value, ('comp', 'dom'), pairs)]
    concatenate x5 -> x0, other arithmetic: 8.31 us -> none  [the longest x4 6.06 us: with_halo(): block = jnp.concatenate([low, block, high], axis=dim)]
    transpose x1 -> x0, other arithmetic: 8.14 us -> none  [shards(): current = row_state.T.reshape(1, levels, fields, columns)]
    unnamed x97 -> x25, local copies, waits for them, and re-layouts: 2.72 us -> 6.48 us
  transfers between devices with their start and end apart: 13 -> 11, of which waited for: 8 -> 3; matrix products, arithmetic and copies ran while one was open for 1% -> 3% of each run, Pallas kernels for 0% -> 20%
where the time goes in v1:
time: 80.9 us; the launch traced here: 79.8 us
  Pallas kernels  36.9 us (46%)
  starting transfers between devices  19.2 us (24%)
  waiting for transfers between devices  13.7 us (17%)
  local copies, waits for them, and re-layouts  9.16 us (11%)
  between operations  0.91 us (1%)
    ppermute x11, starting transfers between devices, neighbour(): return lax.ppermute(value, ('comp', 'dom'), pairs)  19.2 us
    pallas_call x1, Pallas kernels, shards(): pl.pallas_call(diffuse_kernel, out_shape=shape((LEVELS * FIELDS, COLS), F...  17 us
    ppermute x11, waiting for transfers between devices, neighbour(): return lax.ppermute(value, ('comp', 'dom'), pairs)  13.7 us
    pallas_call x1, Pallas kernels, shards(): pl.pallas_call(band_kernel, grid=(nb,), out_shape=shape((nb, WIN, TB), BF...  13.2 us
    unnamed x25, local copies, waits for them, and re-layouts  6.48 us
    pallas_call x1, Pallas kernels, shards(): pl.pallas_call(mix_kernel, out_shape=[shape((FIELDS, COLS), F32), shape((...  3.51 us
    pallas_call x1, Pallas kernels, shards(): pl.pallas_call(remap_kernel, out_shape=[shape((FIELDS, COLS), F32), shape...  3.09 us
  transfers between devices with their start and end apart: 11, of which 3 were waited for; matrix products, arithmetic and copies ran while one was open for 3% of the time, Pallas kernels for 20%

profile of v1, /device:TPU:0, one launch (start us, length us, event | category | flops | bytes accessed | tf_op | source)
XLA Modules:
  0.0 79.8 jit_solution(6632344476950814846)
XLA Ops:
  0.6 1.5 %copy.22 = f32[1,7,2048]{2,1,0:T(8,128)} copy(f32[1,7,2048]{2,0,1:T(1,128)} %param.11) | data formatting | bytes 114688
  2.1 1.4 %copy.21 = s32[1,6,2048]{2,1,0:T(8,128)} copy(s32[1,6,2048]{2,0,1:T(1,128)} %param.12) | data formatting | bytes 98304
  3.5 1.4 %copy.20 = f32[1,6,2048]{2,1,0:T(8,128)} copy(f32[1,6,2048]{2,0,1:T(1,128)} %param.13) | data formatting | bytes 98304
  5.0 3.5 %mix.1 = (f32[16,2048]{1,0:T(8,128)}, f32[112,2048]{1,0:T(8,128)}, bf16[112,2048]{1,0:T(8,128)(2,1)}, bf16[4,16,256]{2,1,0:T(8,128)(2,1)}, bf16[4,16,256]{2,1,0:...) custom-call(f32[8,16,2048]{2,1,0:T(8,128)} %bitcast.19, ...), custom_call_target="tpu_custom_call" | custom-call | tf_op jit(solution)/shard_map/mix/pallas_call | solution.py:227
  8.5 8.8 %collective-permute-start.3 = (bf16[112,2048]{1,0:T(8,128)(2,1)}, bf16[112,2048]{1,0:T(8,128)(2,1)S(1)}, u32[]{:S(2)}, u32[]{:S(2)}) collective-permute-start(bf16[112,2048]{1,0:T(8,128)(2,1)} %get-tuple-element.20.bulk), channel_id=1, source_target_pairs={{0,63},{1,0},{2,1},{3,2},{4,3},{5,4},{6,5},{7,6},{8,7},{9,8},{10,9... | collective-permute-start | bytes 1376264 | tf_op jit(solution)/shard_map/ppermute | solution.py:206
  17.3 0.0 collective-permute-start.2
  17.3 1.2 %collective-permute-start.4 = (bf16[4,16,256]{2,1,0:T(8,128)(2,1)}, bf16[4,16,256]{2,1,0:T(8,128)(2,1)S(1)}, u32[]{:S(2)}, u32[]{:S(2)}) collective-permute-start(bf16[4,16,256]{2,1,0:T(8,128)(2,1)} %get-tuple-element.21), channel_id=1, source_target_pairs={{0,126},{1,127},{2,64},{3,65},{4,66},{5,67},{6,68},{7,69},{8,70},{... | collective-permute-start | bytes 98312 | tf_op jit(solution)/shard_map/ppermute | solution.py:206
  18.4 5.2 %collective-permute-start.5 = (bf16[4,16,256]{2,1,0:T(8,128)(2,1)}, bf16[4,16,256]{2,1,0:T(8,128)(2,1)S(1)}, u32[]{:S(2)}, u32[]{:S(2)}) collective-permute-start(bf16[4,16,256]{2,1,0:T(8,128)(2,1)} %get-tuple-element.22), channel_id=1, source_target_pairs={{0,127},{1,64},{2,65},{3,66},{4,67},{5,68},{6,69},{7,70},{8,71},{9... | collective-permute-start | bytes 98312 | tf_op jit(solution)/shard_map/ppermute | solution.py:206
  23.6 0.9 %collective-permute-start = (f32[16,1536]{1,0:T(8,128)}, f32[16,1536]{1,0:T(8,128)S(1)}, u32[]{:S(2)}, u32[]{:S(2)}) collective-permute-start(f32[16,1536]{1,0:T(8,128)} %get-tuple-element.16), channel_id=1, source_target_pairs={{0,1},{1,2},{2,3},{3,4},{4,5},{5,6},{6,7},{7,8},{8,9},{9,10},{10,1... | collective-permute-start | bytes 294920 | tf_op jit(solution)/shard_map/ppermute | solution.py:206
  24.5 4.7 %collective-permute-done.4.r0 = bf16[4,16,256]{2,1,0:T(8,128)(2,1)S(1)} collective-permute-done((bf16[4,16,256]{2,1,0:T(8,128)(2,1)}, bf16[4,16,256]{2,1,0:T(8,128)(2,1)S(1)}, u32[]{:S(2)}, u32[]{:S(2)}) %collective-permute-start.4) | collective-permute-done | bytes 32800 | tf_op jit(solution)/shard_map/ppermute | solution.py:206
  29.2 0.1 collective-permute-start.7
  29.2 1.3 %collective-permute-done.6.r2 = bf16[4,16,256]{2,1,0:T(8,128)(2,1)S(1)} collective-permute-done((bf16[4,16,256]{2,1,0:T(8,128)(2,1)}, bf16[4,16,256]{2,1,0:T(8,128)(2,1)S(1)}, u32[]{:S(2)}, u32[]{:S(2)}) %collective-permute-start.6) | collective-permute-done | bytes 32800 | tf_op jit(solution)/shard_map/ppermute | solution.py:206
  30.6 0.0 collective-permute-start.8
  30.6 7.6 %collective-permute-done.7.r3 = bf16[4,16,256]{2,1,0:T(8,128)(2,1)S(1)} collective-permute-done((bf16[4,16,256]{2,1,0:T(8,128)(2,1)}, bf16[4,16,256]{2,1,0:T(8,128)(2,1)S(1)}, u32[]{:S(2)}, u32[]{:S(2)}) %collective-permute-start.7) | collective-permute-done | bytes 32800 | tf_op jit(solution)/shard_map/ppermute | solution.py:206
  38.2 1.0 %collective-permute-start.1 = (f32[16,1536]{1,0:T(8,128)}, f32[16,1536]{1,0:T(8,128)S(1)}, u32[]{:S(2)}, u32[]{:S(2)}) collective-permute-start(f32[16,1536]{1,0:T(8,128)} %get-tuple-element.18), channel_id=1, source_target_pairs={{0,63},{1,0},{2,1},{3,2},{4,3},{5,4},{6,5},{7,6},{8,7},{9,8},{10,9... | collective-permute-start | bytes 294920 | tf_op jit(solution)/shard_map/ppermute | solution.py:206
  39.2 1.3 %copy.12.source = s32[8,2]{1,0:T(8,128)} copy(s32[8,2]{0,1:T(2,128)} %bitcast.24) | data formatting | bytes 128 | tf_op jit(solution)/shard_map/squeeze | solution.py:271
  40.6 1.3 %copy.13.rate = f32[16,1]{1,0:T(8,128)} copy(f32[16,1]{0,1:T(1,128)} %bitcast.25) | data formatting | bytes 128 | tf_op jit(solution)/shard_map/broadcast_in_dim;squeeze | solution.py:271
  42.0 0.6 copy-done.10
  42.5 3.1 %remap.1 = (f32[16,2048]{1,0:T(8,128)}, f32[16,2048]{1,0:T(8,128)}, bf16[16,2048]{1,0:T(8,128)(2,1)}) custom-call(s32[5]{0:T(128)} %bitcast.26, s32[8,2]{1,0:T(8,128)} %copy.12.source, bf16[4,16,256]{2,1,0:T(8,128)(2,1)} %copy-done.6, bf16[4,16,256]{2,1,0:T(8,128)(2,1)} %copy-done.7, bf16[4,16,256]{2,1,0:T(8,128)(2,1)} %copy-done.8, ...), custom_call_target="tpu_custom_call" | custom-call | tf_op jit(solution)/shard_map/remap/pallas_call | solution.py:263
  45.6 2.1 %collective-permute-start.10 = (bf16[16,2048]{1,0:T(8,128)(2,1)}, bf16[16,2048]{1,0:T(8,128)(2,1)S(1)}, u32[]{:S(2)}, u32[]{:S(2)}) collective-permute-start(bf16[16,2048]{1,0:T(8,128)(2,1)} %get-tuple-element.28.top_half), channel_id=1, source_target_pairs={{0,63},{1,0},{2,1},{3,2},{4,3},{5,4},{6,5},{7,6},{8,7},{9,8},{10,9... | collective-permute-start | bytes 196616 | tf_op jit(solution)/shard_map/ppermute | solution.py:206
  47.8 0.0 collective-permute-done.left.tab_l
  47.8 0.0 collective-permute-start.9
  47.8 0.0 collective-permute-done.1.right.tab_r
  47.8 0.6 copy-done.2
  48.4 0.0 copy-done.3
  48.4 13.2 %band.1 = bf16[20,1280,256]{2,1,0:T(8,128)(2,1)} custom-call(f32[16,1536]{1,0:T(8,128)} %copy-done.2, f32[16,2048]{1,0:T(8,128)} %get-tuple-element.17.own.tab_o, f32[16,1536]{1,0:T(8,128)} %copy-done.3), custom_call_target="tpu_custom_call" | custom-call | bytes 30000000 | tf_op jit(solution)/shard_map/band/pallas_call | solution.py:251
  61.7 0.0 collective-permute-done.3.bulk_r
  61.7 0.6 copy-done.4
  62.3 0.0 copy-done.5
  62.3 0.2 copy-done
  62.5 0.1 copy-done.1
  62.6 17.0 %diffuse.1 = f32[128,2048]{1,0:T(8,128)} custom-call(bf16[20,1280,256]{2,1,0:T(8,128)(2,1)} %band.1, f32[112,2048]{1,0:T(8,128)} %get-tuple-element.19.mixr, bf16[112,2048]{1,0:T(8,128)(2,1)} %get-tuple-element.20.bulk, bf16[112,2048]{1,0:T(8,128)(2,1)} %copy-done.1, bf16[112,2048]{1,0:T(8,128)(2,1)} %copy-done, f32[16,2048]{1,0:T(8,128)} %get-tuple-element.27.top, ...), custom_call_target="tpu_custom_call" | custom-call | tf_op jit(solution)/shard_map/diffuse/pallas_call | solution.py:276
  (21 shorter events, 0.0 us)
Async XLA Ops:
  8.5 53.2 %collective-permute-start.3 = (bf16[112,2048]{1,0:T(8,128)(2,1)}, bf16[112,2048]{1,0:T(8,128)(2,1)S(1)}, u32[]{:S(2)}, u32[]{:S(2)}) collective-permute-start(bf16[112,2048]{1,0:T(8,128)(2,1)} %get-tuple-element.20.bulk), channel_id=1, source_target_pairs={{0,63},{1,0},{2,1},{3,2},{4,3},{5,4},{6,5},{7,6},{8,7},{9,8},{10,9... | collective-permute-start | bytes 1376264 | tf_op jit(solution)/shard_map/ppermute | solution.py:206
  17.3 44.4 %collective-permute-start.2 = (bf16[112,2048]{1,0:T(8,128)(2,1)}, bf16[112,2048]{1,0:T(8,128)(2,1)S(1)}, u32[]{:S(2)}, u32[]{:S(2)}) collective-permute-start(bf16[112,2048]{1,0:T(8,128)(2,1)} %get-tuple-element.20.bulk), channel_id=1, source_target_pairs={{0,1},{1,2},{2,3},{3,4},{4,5},{5,6},{6,7},{7,8},{8,9},{9,10},{10,1... | collective-permute-start | bytes 1376264 | tf_op jit(solution)/shard_map/ppermute | solution.py:206
  17.3 11.9 %collective-permute-start.4 = (bf16[4,16,256]{2,1,0:T(8,128)(2,1)}, bf16[4,16,256]{2,1,0:T(8,128)(2,1)S(1)}, u32[]{:S(2)}, u32[]{:S(2)}) collective-permute-start(bf16[4,16,256]{2,1,0:T(8,128)(2,1)} %get-tuple-element.21), channel_id=1, source_target_pairs={{0,126},{1,127},{2,64},{3,65},{4,66},{5,67},{6,68},{7,69},{8,70},{... | collective-permute-start | bytes 98312 | tf_op jit(solution)/shard_map/ppermute | solution.py:206
  18.4 10.7 %collective-permute-start.5 = (bf16[4,16,256]{2,1,0:T(8,128)(2,1)}, bf16[4,16,256]{2,1,0:T(8,128)(2,1)S(1)}, u32[]{:S(2)}, u32[]{:S(2)}) collective-permute-start(bf16[4,16,256]{2,1,0:T(8,128)(2,1)} %get-tuple-element.22), channel_id=1, source_target_pairs={{0,127},{1,64},{2,65},{3,66},{4,67},{5,68},{6,69},{7,70},{8,71},{9... | collective-permute-start | bytes 98312 | tf_op jit(solution)/shard_map/ppermute | solution.py:206
  23.6 24.2 %collective-permute-start = (f32[16,1536]{1,0:T(8,128)}, f32[16,1536]{1,0:T(8,128)S(1)}, u32[]{:S(2)}, u32[]{:S(2)}) collective-permute-start(f32[16,1536]{1,0:T(8,128)} %get-tuple-element.16), channel_id=1, source_target_pairs={{0,1},{1,2},{2,3},{3,4},{4,5},{5,6},{6,7},{7,8},{8,9},{9,10},{10,1... | collective-permute-start | bytes 294920 | tf_op jit(solution)/shard_map/ppermute | solution.py:206
  29.1 12.8 %copy-start.6 = (bf16[4,16,256]{2,1,0:T(8,128)(2,1)}, bf16[4,16,256]{2,1,0:T(8,128)(2,1)S(1)}, u32[]{:S(2)}) copy-start(bf16[4,16,256]{2,1,0:T(8,128)(2,1)S(1)} %collective-permute-done.4.r0) | copy-start | bytes 98308
  29.2 1.4 %collective-permute-start.6 = (bf16[4,16,256]{2,1,0:T(8,128)(2,1)}, bf16[4,16,256]{2,1,0:T(8,128)(2,1)S(1)}, u32[]{:S(2)}, u32[]{:S(2)}) collective-permute-start(bf16[4,16,256]{2,1,0:T(8,128)(2,1)} %get-tuple-element.23), channel_id=1, source_target_pairs={{0,64},{1,65},{2,66},{3,67},{4,68},{5,69},{6,70},{7,71},{8,72},{9,... | collective-permute-start | bytes 98312 | tf_op jit(solution)/shard_map/ppermute | solution.py:206
  29.2 12.8 %copy-start.7 = (bf16[4,16,256]{2,1,0:T(8,128)(2,1)}, bf16[4,16,256]{2,1,0:T(8,128)(2,1)S(1)}, u32[]{:S(2)}) copy-start(bf16[4,16,256]{2,1,0:T(8,128)(2,1)S(1)} %collective-permute-done.5.r1) | copy-start | bytes 98308
  29.2 9.0 %collective-permute-start.7 = (bf16[4,16,256]{2,1,0:T(8,128)(2,1)}, bf16[4,16,256]{2,1,0:T(8,128)(2,1)S(1)}, u32[]{:S(2)}, u32[]{:S(2)}) collective-permute-start(bf16[4,16,256]{2,1,0:T(8,128)(2,1)} %get-tuple-element.24), channel_id=1, source_target_pairs={{0,65},{1,66},{2,67},{3,68},{4,69},{5,70},{6,71},{7,72},{8,73},{9,... | collective-permute-start | bytes 98312 | tf_op jit(solution)/shard_map/ppermute | solution.py:206
  30.6 11.4 %copy-start.8 = (bf16[4,16,256]{2,1,0:T(8,128)(2,1)}, bf16[4,16,256]{2,1,0:T(8,128)(2,1)S(1)}, u32[]{:S(2)}) copy-start(bf16[4,16,256]{2,1,0:T(8,128)(2,1)S(1)} %collective-permute-done.6.r2) | copy-start | bytes 98308
  30.6 11.3 %collective-permute-start.8 = (bf16[4,16,256]{2,1,0:T(8,128)(2,1)}, bf16[4,16,256]{2,1,0:T(8,128)(2,1)S(1)}, u32[]{:S(2)}, u32[]{:S(2)}) collective-permute-start(bf16[4,16,256]{2,1,0:T(8,128)(2,1)} %get-tuple-element.25), channel_id=1, source_target_pairs={{0,66},{1,67},{2,68},{3,69},{4,70},{5,71},{6,72},{7,73},{8,74},{9,... | collective-permute-start | bytes 98312 | tf_op jit(solution)/shard_map/ppermute | solution.py:206
  38.2 3.7 %copy-start.9 = (bf16[4,16,256]{2,1,0:T(8,128)(2,1)}, bf16[4,16,256]{2,1,0:T(8,128)(2,1)S(1)}, u32[]{:S(2)}) copy-start(bf16[4,16,256]{2,1,0:T(8,128)(2,1)S(1)} %collective-permute-done.7.r3) | copy-start | bytes 98308
  38.2 9.6 %collective-permute-start.1 = (f32[16,1536]{1,0:T(8,128)}, f32[16,1536]{1,0:T(8,128)S(1)}, u32[]{:S(2)}, u32[]{:S(2)}) collective-permute-start(f32[16,1536]{1,0:T(8,128)} %get-tuple-element.18), channel_id=1, source_target_pairs={{0,63},{1,0},{2,1},{3,2},{4,3},{5,4},{6,5},{7,6},{8,7},{9,8},{10,9... | collective-permute-start | bytes 294920 | tf_op jit(solution)/shard_map/ppermute | solution.py:206
  41.9 0.6 copy-start.10
  45.6 16.1 %collective-permute-start.10 = (bf16[16,2048]{1,0:T(8,128)(2,1)}, bf16[16,2048]{1,0:T(8,128)(2,1)S(1)}, u32[]{:S(2)}, u32[]{:S(2)}) collective-permute-start(bf16[16,2048]{1,0:T(8,128)(2,1)} %get-tuple-element.28.top_half), channel_id=1, source_target_pairs={{0,63},{1,0},{2,1},{3,2},{4,3},{5,4},{6,5},{7,6},{8,7},{9,8},{10,9... | collective-permute-start | bytes 196616 | tf_op jit(solution)/shard_map/ppermute | solution.py:206
  47.8 0.6 copy-start.2
  47.8 13.9 %collective-permute-start.9 = (bf16[16,2048]{1,0:T(8,128)(2,1)}, bf16[16,2048]{1,0:T(8,128)(2,1)S(1)}, u32[]{:S(2)}, u32[]{:S(2)}) collective-permute-start(bf16[16,2048]{1,0:T(8,128)(2,1)} %get-tuple-element.28.top_half), channel_id=1, source_target_pairs={{0,1},{1,2},{2,3},{3,4},{4,5},{5,6},{6,7},{7,8},{8,9},{9,10},{10,1... | collective-permute-start | bytes 196616 | tf_op jit(solution)/shard_map/ppermute | solution.py:206
  47.8 0.6 copy-start.3
  61.7 0.6 copy-start.4
  61.7 0.6 copy-start.5
  61.7 0.8 %copy-start = (bf16[112,2048]{1,0:T(8,128)(2,1)}, bf16[112,2048]{1,0:T(8,128)(2,1)S(1)}, u32[]{:S(2)}) copy-start(bf16[112,2048]{1,0:T(8,128)(2,1)S(1)} %collective-permute-done.3.bulk_r) | copy-start | bytes 1376260
  61.7 0.9 %copy-start.1 = (bf16[112,2048]{1,0:T(8,128)(2,1)}, bf16[112,2048]{1,0:T(8,128)(2,1)S(1)}, u32[]{:S(2)}) copy-start(bf16[112,2048]{1,0:T(8,128)(2,1)S(1)} %collective-permute-done.2.bulk_l) | copy-start | bytes 1376260

commit v2 on v1

v2 whole, which is shorter than its diff:
```python
import jax
import jax.numpy as jnp
from jax import lax
from jax.experimental import pallas as pl
from jax.experimental.pallas import tpu as pltpu
from jax.sharding import PartitionSpec as P

F32, BF16 = jnp.float32, jnp.bfloat16
RIM = 512
NSUB = 4
TB = 256
WIN = TB + 2 * RIM
LANE = 128
NEVER = 64.0
FIELDS, LEVELS, COLS = 16, 8, 2048
REST = (LEVELS - 1) * FIELDS
WIDE = COLS - RIM
TABLE = 32


def pick_kernel(state, rate, send, mix0, p0, p1, p2, p3, p4):
    packed = (p0, p1, p2, p3, p4)
    for c in range(0, COLS, TB):
        here = slice(c, c + TB)
        v0 = state[0, 0, :, here]
        mix0[:, here] = v0 + rate[0, :, here] * (state[0, 1, :, here] - v0)
    for k in range(5):
        for j in range(4):
            for h in range(2):
                index = send[k, j : j + 1, h * LANE : (h + 1) * LANE]
                low = jnp.broadcast_to(index & (LANE - 1), (FIELDS, LANE))
                high = jnp.broadcast_to(lax.shift_right_logical(index, 7), (FIELDS, LANE))
                total = jnp.zeros((FIELDS, LANE), F32)
                for s in range(COLS // LANE):
                    got = jnp.take_along_axis(
                        mix0[:, s * LANE : (s + 1) * LANE], low, axis=1, mode="promise_in_bounds"
                    )
                    total = jnp.where(high == s, got, total)
                packed[k][j, :, h * LANE : (h + 1) * LANE] = total.astype(BF16)


def rest_kernel(state, rate, offs, coef, after, mixr, bulk):
    del after
    for c in range(0, COLS, TB):
        here = slice(c, c + TB)
        before = state[0, 0, :, here]
        mid = state[0, 1, :, here]
        flux = rate[0, :, here] * (mid - before)
        for l in range(1, LEVELS):
            if l < LEVELS - 1:
                after = state[0, l + 1, :, here]
                below = rate[l, :, here] * (after - mid)
                new = mid + below - flux
                flux, mid = below, after
            else:
                new = mid - flux
            mixr[(l - 1) * FIELDS : l * FIELDS, here] = new
            bulk[(l - 1) * FIELDS : l * FIELDS, here] = new.astype(BF16)
        lane = lax.broadcasted_iota(jnp.int32, (1, TB), 1) + RIM
        off = [offs[j, :, here] for j in range(6)]
        val = [coef[j, :, here] for j in range(6)]
        zero = jnp.zeros((1, TB), F32)
        rows_c, rows_h, rows_l = [], [], []
        for j in range(6):
            merged = val[j]
            repeated = zero
            for i in range(6):
                if i != j:
                    same = off[i] == off[j]
                    merged = merged + jnp.where(same, val[i], 0.0)
                    if i < j:
                        repeated = jnp.where(same, 1.0, repeated)
            place = off[j] + lane
            rows_c.append(jnp.where(repeated > 0.5, 0.0, merged))
            rows_h.append(jnp.where(repeated > 0.5, NEVER, lax.shift_right_logical(place, 7).astype(F32)))
            rows_l.append((place & (LANE - 1)).astype(F32))
        block = jnp.concatenate(rows_c + [zero] * 2 + rows_h + [zero] * 2 + rows_l + [zero] * 10, axis=0)
        bulk[REST : REST + TABLE, here] = block.astype(BF16)


def build_bands(tab, rel, band, first, count, source):
    columns = count * TB
    tab[0:8, 0:columns] = source[0:16, 0:columns].astype(F32)[0:8]
    high = source[0:16, 0:columns].astype(F32)[8:16]
    low = source[16:32, 0:columns].astype(F32)[0:8]
    tab[8:16, 0:columns] = high * float(LANE) + low
    rows = [
        (lax.broadcasted_iota(jnp.int32, (16, LANE), 0) + r).astype(F32).astype(BF16) for r in range(0, LANE, 16)
    ]

    @pl.loop(0, count)
    def _(b):
        for half in range(TB // LANE):
            start = pl.multiple_of(b * TB + half * LANE, LANE)
            lanes = slice(half * LANE, (half + 1) * LANE)
            coefs = [
                jnp.broadcast_to(tab[j : j + 1, pl.ds(start, LANE)], (16, LANE)).astype(BF16) for j in range(6)
            ]
            first_row = half * LANE
            last_row = first_row + LANE + 2 * RIM
            if first_row:
                band[first + b, 0:first_row, lanes] = jnp.zeros((first_row, LANE), BF16)
            if last_row < WIN:
                band[first + b, last_row:WIN, lanes] = jnp.zeros((WIN - last_row, LANE), BF16)
            for base in range(first_row, last_row, LANE):
                slot = 8 * (half * (WIN // LANE) + base // LANE)
                rel[slot : slot + 8, :] = tab[8:16, pl.ds(start, LANE)] - float(base)
                there = [
                    jnp.broadcast_to(rel[slot + j : slot + j + 1, :], (16, LANE)).astype(BF16) for j in range(6)
                ]
                for r in range(0, LANE, 16):
                    total = jnp.zeros((16, LANE), BF16)
                    for j in range(6):
                        total = jnp.where(there[j] == rows[r // 16], coefs[j], total)
                    band[first + b, base + r : base + r + 16, lanes] = total


def own_band_kernel(bulk, band, raw, tab, rel, sem):
    copy = pltpu.make_async_copy(bulk.at[REST : REST + TABLE], raw, sem)
    copy.start()
    copy.wait()
    build_bands(tab, rel, band, 0, COLS // TB, raw)


def side_band_kernel(bulk_l, bulk, bulk_r, band, wide, keep, raw_l, raw_o, raw_r, tab, rel, sems):
    tables = [
        pltpu.make_async_copy(bulk_l.at[REST : REST + TABLE, RIM:COLS], raw_l, sems.at[0]),
        pltpu.make_async_copy(bulk.at[REST : REST + TABLE], raw_o, sems.at[1]),
        pltpu.make_async_copy(bulk_r.at[REST : REST + TABLE, 0:WIDE], raw_r, sems.at[2]),
    ]
    fields = [
        pltpu.make_async_copy(piece.at[0:REST], wide.at[:, i * COLS : (i + 1) * COLS], sems.at[3 + i])
        for i, piece in enumerate((bulk_l, bulk, bulk_r))
    ]
    for c in tables + fields:
        c.start()
    for c in tables:
        c.wait()
    at = 0
    for raw, columns in ((raw_l, WIDE), (raw_o, COLS), (raw_r, WIDE)):
        coefs = raw[0:16, :].astype(F32)[0:8]
        keep[:, at : at + columns] = 1.0 - jnp.sum(coefs, axis=0, keepdims=True)
        at += columns
    build_bands(tab, rel, band, 0, WIDE // TB, raw_l)
    build_bands(tab, rel, band, WIDE // TB, WIDE // TB, raw_r)
    for c in fields:
        c.wait()


def remap_kernel(live, source, r0, r1, r2, r3, r4, weights, mix0, mask, rate, after, forcing, top, top_half, got):
    del after
    for k, piece in enumerate((r0, r1, r2, r3, r4)):
        got[4 * k : 4 * k + 4] = piece[...]
    ones = jnp.ones((16, TB), BF16)
    eye = lax.broadcasted_iota(jnp.int32, (FIELDS, FIELDS), 0) == lax.broadcasted_iota(
        jnp.int32, (FIELDS, FIELDS), 1
    )
    rate_column = jnp.sum(
        jnp.where(eye, jnp.broadcast_to(rate[...], (FIELDS, FIELDS)), 0.0), axis=1, keepdims=True
    )
    for n in range(COLS // TB):
        here = slice(n * TB, (n + 1) * TB)
        num = jnp.zeros((FIELDS, TB), F32)
        den = jnp.zeros((1, TB), F32)
        for m in range(2):
            q = source[m, n]
            valid = jnp.where((q & 3) < live[0, lax.shift_right_logical(q, 2)], 1.0, 0.0).astype(F32)
            rows = jnp.concatenate([got[q], ones], axis=0)
            both = lax.dot_general(
                rows, weights[n, m], (((1,), (1,)), ((), ())), preferred_element_type=F32
            )
            num = num + valid * both[0:FIELDS]
            den = den + valid * both[FIELDS : FIELDS + 1]
        value = num / jnp.maximum(den, 1.0)
        forcing[:, here] = value
        old = mix0[:, here]
        new = old + rate_column * mask[0:1, here].astype(F32) * (value - old)
        top[:, here] = new
        top_half[:, here] = new.astype(BF16)


def diffuse_kernel(
    band_own, band_side, wide, keep, mixr, top, top_half, top_l, top_r, out, xt, xa, xb, st,
):
    xt[:, 0:COLS] = top_l[...]
    xt[:, COLS : 2 * COLS] = top_half[...]
    xt[:, 2 * COLS : 3 * COLS] = top_r[...]
    edge = WIDE // TB
    own = COLS // TB
    nb = own + 2 * edge
    bufs = (xa, xb)
    for step in range(NSUB):
        src, dst = bufs[(step + 1) % 2], bufs[step % 2]
        skip = step * (RIM // TB)
        for b in range(skip, nb - skip):
            at = slice(b * TB, (b + 1) * TB)
            here = slice(RIM + b * TB, RIM + (b + 1) * TB)
            window = slice(b * TB, b * TB + WIN)
            inside = edge <= b < edge + own
            mine = slice((b - edge) * TB, (b - edge + 1) * TB)
            if inside:
                matrix = band_own[b - edge]
            else:
                matrix = band_side[b if b < edge else b - own]
            if step == 0:
                rows = jnp.concatenate([xt[:, window], wide[:, window]], axis=0)
                if inside:
                    old = jnp.concatenate([top[:, mine], mixr[:, mine]], axis=0)
                else:
                    old = jnp.concatenate([xt[:, here], wide[:, here]], axis=0).astype(F32)
            else:
                rows = src[:, window]
                old = st[:, at]
            new = old * keep[:, at] + jnp.dot(rows, matrix, preferred_element_type=F32)
            if step < NSUB - 1:
                st[:, at] = new
                dst[:, here] = new.astype(BF16)
            else:
                out[:, mine] = new


def neighbour(value, flip, apart):
    size = (lax.axis_size("comp"), lax.axis_size("dom"))
    pairs = [
        (s * size[1] + d, (s ^ flip) * size[1] + (d + apart) % size[1])
        for s in range(size[0])
        for d in range(size[1])
    ]
    return lax.ppermute(value, ("comp", "dom"), pairs)


def spec(n):
    return [pl.BlockSpec(memory_space=pltpu.VMEM)] * n


ANYWHERE = pl.BlockSpec(memory_space=pl.ANY)
SCALARS = pl.BlockSpec(memory_space=pltpu.SMEM)


def params(mib):
    return pltpu.CompilerParams(vmem_limit_bytes=mib * 2**20)


def cost(us):
    return pl.CostEstimate(flops=0, bytes_accessed=us * 3_000_000, transcendentals=0)


def shards(
    column_state, vert_rate, hor_offsets, hor_coef, open_mask, couple_rate, send_index, live_slots, block_source,
    remap_weight,
):
    shape = jax.ShapeDtypeStruct
    block = shape((4, FIELDS, TB), BF16)
    rate = vert_rate.transpose(1, 0, 2)
    mix0, p0, p1, p2, p3, p4 = pl.pallas_call(
        pick_kernel,
        grid=(1,),
        out_shape=[shape((FIELDS, COLS), F32)] + [block] * 5,
        in_specs=[
            pl.BlockSpec((1, 2, FIELDS, COLS), lambda i: (0, 0, 0, 0)),
            pl.BlockSpec((1, 1, COLS), lambda i: (0, 0, 0)),
        ]
        + spec(1),
        out_specs=spec(6),
        compiler_params=params(8),
        cost_estimate=cost(2),
        name="pick",
    )(column_state, rate, send_index[0, 0])
    received = [neighbour(p, 1, k - 2) for k, p in enumerate((p0, p1, p2, p3, p4))]

    mixr, bulk = pl.pallas_call(
        rest_kernel,
        out_shape=[shape((REST, COLS), F32), shape((REST + TABLE, COLS), BF16)],
        in_specs=spec(4) + [ANYWHERE],
        out_specs=spec(2),
        compiler_params=params(8),
        cost_estimate=cost(2),
        name="rest",
    )(column_state, rate, hor_offsets.transpose(1, 0, 2), hor_coef.transpose(1, 0, 2), p4)
    bulk_left = neighbour(bulk, 0, 1)
    bulk_right = neighbour(bulk, 0, -1)

    raw = pltpu.VMEM((TABLE, COLS), BF16)
    raw_side = pltpu.VMEM((TABLE, WIDE), BF16)
    tab = pltpu.VMEM((16, COLS), F32)
    rel = pltpu.VMEM((16 * (WIN // LANE), LANE), F32)
    band_own = pl.pallas_call(
        own_band_kernel,
        out_shape=shape((COLS // TB, WIN, TB), BF16),
        in_specs=[ANYWHERE],
        out_specs=pl.BlockSpec(memory_space=pltpu.VMEM),
        scratch_shapes=[raw, tab, rel, pltpu.SemaphoreType.DMA],
        compiler_params=params(8),
        cost_estimate=cost(3),
        name="own_band",
    )(bulk)

    forcing, top, top_half = pl.pallas_call(
        remap_kernel,
        out_shape=[shape((FIELDS, COLS), F32), shape((FIELDS, COLS), F32), shape((FIELDS, COLS), BF16)],
        in_specs=[SCALARS, SCALARS] + spec(9) + [ANYWHERE],
        out_specs=spec(3),
        scratch_shapes=[pltpu.VMEM((20, FIELDS, TB), BF16)],
        compiler_params=params(8),
        cost_estimate=cost(2),
        name="remap",
    )(live_slots[0], block_source[0, 0].T, *received, remap_weight[0, 0], mix0, open_mask, couple_rate, band_own)
    top_left = neighbour(top_half, 0, 1)
    top_right = neighbour(top_half, 0, -1)

    band_side, wide, keep = pl.pallas_call(
        side_band_kernel,
        out_shape=[
            shape((2 * WIDE // TB, WIN, TB), BF16),
            shape((REST, 3 * COLS), BF16),
            shape((1, COLS + 2 * WIDE), F32),
        ],
        in_specs=[ANYWHERE] * 3,
        out_specs=spec(3),
        scratch_shapes=[raw_side, raw, raw_side, tab, rel, pltpu.SemaphoreType.DMA((6,))],
        compiler_params=params(8),
        cost_estimate=cost(4),
        name="side_band",
    )(bulk_left, bulk, bulk_right)

    half = pltpu.VMEM((LEVELS * FIELDS, 3 * COLS), BF16)
    state = pl.pallas_call(
        diffuse_kernel,
        out_shape=shape((LEVELS * FIELDS, COLS), F32),
        in_specs=spec(9),
        out_specs=pl.BlockSpec(memory_space=pltpu.VMEM),
        scratch_shapes=[
            pltpu.VMEM((FIELDS, 3 * COLS), BF16),
            half,
            half,
            pltpu.VMEM((LEVELS * FIELDS, COLS + 2 * WIDE), F32),
        ],
        compiler_params=params(16),
        cost_estimate=cost(6),
        name="diffuse",
    )(band_own, band_side, wide, keep, mixr, top, top_half, top_left, top_right)
    return state.reshape(1, LEVELS, FIELDS, COLS), forcing[None]


def solution(mesh):
    placed = (
        P("comp", None, None, "dom"),
        P("comp", None, "dom"),
        P("comp", None, "dom"),
        P("comp", None, "dom"),
        P("comp", "dom"),
        P("comp", None),
        P("comp", "dom", None, None, None),
        P("comp", "dom", None),
        P("comp", "dom", None, None),
        P("comp", "dom", None, None, None, None),
    )
    return jax.shard_map(
        shards,
        mesh=mesh,
        in_specs=placed,
        out_specs=(P("comp", None, None, "dom"), P("comp", None, "dom")),
        check_vma=False,
    )
```

time: 80.9 us -> 58.8 us (0.73)
  Pallas kernels: 36.9 us -> 16.6 us
  local copies, waits for them, and re-layouts: 9.16 us -> 4.39 us
  starting transfers between devices: 19.2 us -> 21.6 us
  waiting for transfers between devices: 13.7 us -> 15.1 us
    pallas_call x1, Pallas kernels: 17 us -> 6.35 us  [shards(): pl.pallas_call(diffuse_kernel, out_shape=shape((LEVELS * FIELDS, COLS), F...]
    pallas_call x2 -> x4, Pallas kernels: 16.7 us -> 8.33 us  [the longest x1 4.32 us: shards(): pl.pallas_call(side_band_kernel, out_shape=[shape((2 * WIDE // TB, WIN, T...]
    ppermute x11 -> x9, starting transfers between devices: 19.2 us -> 21.6 us  [neighbour(): return lax.ppermute(value, ('comp', 'dom'), pairs)]
    unnamed x25 -> x20, local copies, waits for them, and re-layouts: 6.48 us -> 4.39 us
    ppermute x11 -> x9, waiting for transfers between devices: 13.7 us -> 15.1 us  [neighbour(): return lax.ppermute(value, ('comp', 'dom'), pairs)]
    squeeze x1 -> x0, local copies, waits for them, and re-layouts: 1.34 us -> none  [shards(): block_source[0, 0]]
    another operation x1 -> x0, local copies, waits for them, and re-layouts: 1.33 us -> none  [shards(): couple_rate[0][:, None]]
    pallas_call x1, Pallas kernels: 3.09 us -> 1.95 us  [shards(): pl.pallas_call(remap_kernel, out_shape=[shape((FIELDS, COLS), F32), shape...]
  transfers between devices with their start and end apart: 11 -> 9, of which waited for: 3 -> 4; matrix products, arithmetic and copies ran while one was open for 3% -> 0% of each run, Pallas kernels for 20% -> 15%
where the time goes in v2:
time: 58.8 us; the launch traced here: 58.4 us
  starting transfers between devices  21.6 us (37%)
  Pallas kernels  16.6 us (28%)
  waiting for transfers between devices  15.1 us (26%)
  local copies, waits for them, and re-layouts  4.39 us (7%)
  between operations  0.76 us (1%)
    ppermute x9, starting transfers between devices, neighbour(): return lax.ppermute(value, ('comp', 'dom'), pairs)  21.6 us
    ppermute x9, waiting for transfers between devices, neighbour(): return lax.ppermute(value, ('comp', 'dom'), pairs)  15.1 us
    pallas_call x1, Pallas kernels, shards(): pl.pallas_call(diffuse_kernel, out_shape=shape((LEVELS * FIELDS, COLS), F...  6.35 us
    unnamed x20, local copies, waits for them, and re-layouts  4.39 us
    pallas_call x1, Pallas kernels, shards(): pl.pallas_call(side_band_kernel, out_shape=[shape((2 * WIDE // TB, WIN, T...  4.32 us
    pallas_call x1, Pallas kernels, shards(): pl.pallas_call(own_band_kernel, out_shape=shape((COLS // TB, WIN, TB), BF...  2.75 us
    pallas_call x1, Pallas kernels, shards(): pl.pallas_call(remap_kernel, out_shape=[shape((FIELDS, COLS), F32), shape...  1.95 us
  transfers between devices with their start and end apart: 9, of which 4 were waited for; matrix products, arithmetic and copies ran while one was open for 0% of the time, Pallas kernels for 15%

profile of v2, /device:TPU:0, one launch (start us, length us, event | category | flops | bytes accessed | tf_op | source)
XLA Modules:
  0.0 58.4 jit_solution(6975784900137023425)
XLA Ops:
  0.6 0.0 copy-start.8
  0.6 0.0 copy-start.7
  0.7 1.2 %copy-done = f32[1,8,16,2048]{3,2,1,0:T(8,128)S(1)} copy-done((f32[1,8,16,2048]{3,2,1,0:T(8,128)S(1)}, f32[1,8,16,2048]{3,2,1,0:T(8,128)}, u32[]{:S(2)}) %copy-start) | copy-done | bytes 1048600
  1.9 0.8 %copy-done.2 = f32[1,7,2048]{2,0,1:T(1,128)S(1)} copy-done((f32[1,7,2048]{2,0,1:T(1,128)S(1)}, f32[1,7,2048]{2,0,1:T(1,128)}, u32[]{:S(2)}) %copy-start.2) | copy-done | bytes 57368
  2.7 0.7 %copy-done.5 = s32[1,1,5,4,256]{4,3,2,1,0:T(4,128)S(1)} copy-done((s32[1,1,5,4,256]{4,3,2,1,0:T(4,128)S(1)}, s32[1,1,5,4,256]{4,3,2,1,0:T(4,128)}, u32[]{:S(2)}) %copy-start.5) | copy-done | bytes 20504
  3.5 0.9 %pick.1 = (f32[16,2048]{1,0:T(8,128)S(1)}, bf16[4,16,256]{2,1,0:T(8,128)(2,1)S(1)}, bf16[4,16,256]{2,1,0:T(8,128)(2,1)S(1)}, bf16[4,16,256]{2,1,0:T(8,128)(2,1)S...) custom-call(f32[1,8,16,2048]{3,2,1,0:T(8,128)S(1)} %copy-done, f32[7,1,2048]{2,1,0:T(1,128)S(1)} %bitcast.12, ...), custom_call_target="tpu_custom_call" | custom-call | bytes 6000000 | tf_op jit(solution)/shard_map/pick/pallas_call | solution.py:255
  4.3 0.0 copy-start.3
  4.3 0.8 %copy-done.3 = s32[1,6,2048]{2,0,1:T(1,128)S(1)} copy-done((s32[1,6,2048]{2,0,1:T(1,128)S(1)}, s32[1,6,2048]{2,0,1:T(1,128)}, u32[]{:S(2)}) %copy-start.3) | copy-done | bytes 49176
  5.1 0.8 %copy-done.4 = f32[1,6,2048]{2,0,1:T(1,128)S(1)} copy-done((f32[1,6,2048]{2,0,1:T(1,128)S(1)}, f32[1,6,2048]{2,0,1:T(1,128)}, u32[]{:S(2)}) %copy-start.4) | copy-done | bytes 49176
  5.9 0.4 rest.1
  6.3 1.6 %collective-permute-start = (bf16[144,2048]{1,0:T(8,128)(2,1)S(1)}, bf16[144,2048]{1,0:T(8,128)(2,1)S(1)}, u32[]{:S(2)}, u32[]{:S(2)}) collective-permute-start(bf16[144,2048]{1,0:T(8,128)(2,1)S(1)} %get-tuple-element.17.bulk), channel_id=1, source_target_pairs={{0,1},{1,2},{2,3},{3,4},{4,5},{5,6},{6,7},{7,8},{8,9},{9,10},{10,1... | collective-permute-start | bytes 1769480 | tf_op jit(solution)/shard_map/ppermute | solution.py:229
  8.0 7.3 %collective-permute-start.1 = (bf16[144,2048]{1,0:T(8,128)(2,1)S(1)}, bf16[144,2048]{1,0:T(8,128)(2,1)S(1)}, u32[]{:S(2)}, u32[]{:S(2)}) collective-permute-start(bf16[144,2048]{1,0:T(8,128)(2,1)S(1)} %get-tuple-element.17.bulk), channel_id=1, source_target_pairs={{0,63},{1,0},{2,1},{3,2},{4,3},{5,4},{6,5},{7,6},{8,7},{9,8},{10,9... | collective-permute-start | bytes 1769480 | tf_op jit(solution)/shard_map/ppermute | solution.py:229
  15.3 1.1 %collective-permute-start.2 = (bf16[4,16,256]{2,1,0:T(8,128)(2,1)S(1)}, bf16[4,16,256]{2,1,0:T(8,128)(2,1)S(1)}, u32[]{:S(2)}, u32[]{:S(2)}) collective-permute-start(bf16[4,16,256]{2,1,0:T(8,128)(2,1)S(1)} %get-tuple-element.22), channel_id=1, source_target_pairs={{0,126},{1,127},{2,64},{3,65},{4,66},{5,67},{6,68},{7,69},{8,70},{... | collective-permute-start | bytes 98312 | tf_op jit(solution)/shard_map/ppermute | solution.py:229
  16.3 2.0 %collective-permute-start.3 = (bf16[4,16,256]{2,1,0:T(8,128)(2,1)S(1)}, bf16[4,16,256]{2,1,0:T(8,128)(2,1)S(1)}, u32[]{:S(2)}, u32[]{:S(2)}) collective-permute-start(bf16[4,16,256]{2,1,0:T(8,128)(2,1)S(1)} %get-tuple-element.23), channel_id=1, source_target_pairs={{0,127},{1,64},{2,65},{3,66},{4,67},{5,68},{6,69},{7,70},{8,71},{9... | collective-permute-start | bytes 98312 | tf_op jit(solution)/shard_map/ppermute | solution.py:229
  18.3 0.0 collective-permute-start.4
  18.3 5.0 %collective-permute-done.2.r0 = bf16[4,16,256]{2,1,0:T(8,128)(2,1)S(1)} collective-permute-done((bf16[4,16,256]{2,1,0:T(8,128)(2,1)S(1)}, bf16[4,16,256]{2,1,0:T(8,128)(2,1)S(1)}, u32[]{:S(2)}, u32[]{:S(2)}) %collective-permute-start.2) | collective-permute-done | bytes 32800 | tf_op jit(solution)/shard_map/ppermute | solution.py:229
  23.3 2.2 %collective-permute-start.5 = (bf16[4,16,256]{2,1,0:T(8,128)(2,1)S(1)}, bf16[4,16,256]{2,1,0:T(8,128)(2,1)S(1)}, u32[]{:S(2)}, u32[]{:S(2)}) collective-permute-start(bf16[4,16,256]{2,1,0:T(8,128)(2,1)S(1)} %get-tuple-element.25), channel_id=1, source_target_pairs={{0,65},{1,66},{2,67},{3,68},{4,69},{5,70},{6,71},{7,72},{8,73},{9,... | collective-permute-start | bytes 98312 | tf_op jit(solution)/shard_map/ppermute | solution.py:229
  25.5 3.8 %collective-permute-done.3.r1 = bf16[4,16,256]{2,1,0:T(8,128)(2,1)S(1)} collective-permute-done((bf16[4,16,256]{2,1,0:T(8,128)(2,1)S(1)}, bf16[4,16,256]{2,1,0:T(8,128)(2,1)S(1)}, u32[]{:S(2)}, u32[]{:S(2)}) %collective-permute-start.3) | collective-permute-done | bytes 32800 | tf_op jit(solution)/shard_map/ppermute | solution.py:229
  29.2 0.0 collective-permute-start.6
  29.2 2.7 %own_band.1.after.band_own = bf16[8,1280,256]{2,1,0:T(8,128)(2,1)S(1)} custom-call(bf16[144,2048]{1,0:T(8,128)(2,1)S(1)} %get-tuple-element.17.bulk), custom_call_target="tpu_custom_call" | custom-call | bytes 9000000 | tf_op jit(solution)/shard_map/own_band/pallas_call | solution.py:287
  32.0 0.0 collective-permute-done.4.r2
  32.0 0.1 collective-permute-done.5.r3
  32.1 6.2 %collective-permute-done.6.r4 = bf16[4,16,256]{2,1,0:T(8,128)(2,1)S(1)} collective-permute-done((bf16[4,16,256]{2,1,0:T(8,128)(2,1)S(1)}, bf16[4,16,256]{2,1,0:T(8,128)(2,1)S(1)}, u32[]{:S(2)}, u32[]{:S(2)}) %collective-permute-start.6) | collective-permute-done | bytes 32800 | tf_op jit(solution)/shard_map/ppermute | solution.py:229
  38.3 1.9 %remap.1 = (f32[16,2048]{1,0:T(8,128)}, f32[16,2048]{1,0:T(8,128)S(1)}, bf16[16,2048]{1,0:T(8,128)(2,1)S(1)}) custom-call(s32[1,5]{1,0:T(1,128)S(1)} %bitcast.18, s32[2,8]{1,0:T(2,128)S(1)} %bitcast.17, bf16[4,16,256]{2,1,0:T(8,128)(2,1)S(1)} %collective-permute-done.2.r0, bf16[4,16,256]{2,1,0:T(8,128)(2,1)S(1)} %collective-permute-done.3.r1, ...), custom_call_target="tpu_custom_call" | custom-call | bytes 6000000 | tf_op jit(solution)/shard_map/remap/pallas_call | solution.py:298
  40.3 0.8 %collective-permute-start.7 = (bf16[16,2048]{1,0:T(8,128)(2,1)S(1)}, bf16[16,2048]{1,0:T(8,128)(2,1)S(1)}, u32[]{:S(2)}, u32[]{:S(2)}) collective-permute-start(bf16[16,2048]{1,0:T(8,128)(2,1)S(1)} %get-tuple-element.28.top_half), channel_id=1, source_target_pairs={{0,1},{1,2},{2,3},{3,4},{4,5},{5,6},{6,7},{7,8},{8,9},{9,10},{10,1... | collective-permute-start | bytes 196616 | tf_op jit(solution)/shard_map/ppermute | solution.py:229
  41.1 6.7 %collective-permute-start.8 = (bf16[16,2048]{1,0:T(8,128)(2,1)S(1)}, bf16[16,2048]{1,0:T(8,128)(2,1)S(1)}, u32[]{:S(2)}, u32[]{:S(2)}) collective-permute-start(bf16[16,2048]{1,0:T(8,128)(2,1)S(1)} %get-tuple-element.28.top_half), channel_id=1, source_target_pairs={{0,63},{1,0},{2,1},{3,2},{4,3},{5,4},{6,5},{7,6},{8,7},{9,8},{10,9... | collective-permute-start | bytes 196616 | tf_op jit(solution)/shard_map/ppermute | solution.py:229
  47.7 0.0 collective-permute-done.bulk_l
  47.7 0.0 collective-permute-done.1.bulk_r
  47.8 4.3 %side_band.1 = (bf16[12,1280,256]{2,1,0:T(8,128)(2,1)S(1)}, bf16[112,6144]{1,0:T(8,128)(2,1)S(1)}, f32[1,5120]{1,0:T(1,128)S(1)}) custom-call(bf16[144,2048]{1,0:T(8,128)(2,1)S(1)} %collective-permute-done.bulk_l, bf16[144,2048]{1,0:T(8,128)(2,1)S(1)} %get-tuple-element.17.bulk, bf16[144,2048]{1,0:T(8,128)(2,1)S(1)} %collective-permute-done.1.bulk_r), custom_call_target="tpu_custom_call" | custom-call | bytes 12000000 | tf_op jit(solution)/shard_map/side_band/pallas_call | solution.py:311
  52.1 0.0 collective-permute-done.7.top_l
  52.1 0.0 collective-permute-done.8.top_r
  52.1 6.4 %diffuse.1 = f32[128,2048]{1,0:T(8,128)} custom-call(bf16[8,1280,256]{2,1,0:T(8,128)(2,1)S(1)} %own_band.1.after.band_own, bf16[12,1280,256]{2,1,0:T(8,128)(2,1)S(1)} %get-tuple-element.18.band_side, bf16[112,6144]{1,0:T(8,128)(2,1)S(1)} %get-tuple-element.19.wide, f32[1,5120]{1,0:T(1,128)S(1)} %get-tuple-element.20.keep, ...), custom_call_target="tpu_custom_call" | custom-call | bytes 18000000 | tf_op jit(solution)/shard_map/diffuse/pallas_call | solution.py:327
  (12 shorter events, 0.0 us)
Async XLA Ops:
  0.6 37.7 %copy-start.8 = (s32[1,1,5]{2,1,0:T(1,128)S(1)}, s32[1,1,5]{2,1,0:T(1,128)}, u32[]{:S(2)}) copy-start(s32[1,1,5]{2,1,0:T(1,128)} %param.17) | copy-start | bytes 64
  0.6 37.7 %copy-start.7 = (s32[1,1,8,2]{2,3,1,0:T(2,128)S(1)}, s32[1,1,8,2]{2,3,1,0:T(2,128)}, u32[]{:S(2)}) copy-start(s32[1,1,8,2]{2,3,1,0:T(2,128)} %param.18) | copy-start | bytes 196
  0.7 37.7 %copy-start.9 = (f32[1,16]{1,0:T(1,128)S(1)}, f32[1,16]{1,0:T(1,128)}, u32[]{:S(2)}) copy-start(f32[1,16]{1,0:T(1,128)} %rate.1) | copy-start | bytes 196
  0.7 1.2 %copy-start = (f32[1,8,16,2048]{3,2,1,0:T(8,128)S(1)}, f32[1,8,16,2048]{3,2,1,0:T(8,128)}, u32[]{:S(2)}) copy-start(f32[1,8,16,2048]{3,2,1,0:T(8,128)} %state.3) | copy-start | bytes 3145732
  1.9 0.8 %copy-start.2 = (f32[1,7,2048]{2,0,1:T(1,128)S(1)}, f32[1,7,2048]{2,0,1:T(1,128)}, u32[]{:S(2)}) copy-start(f32[1,7,2048]{2,0,1:T(1,128)} %param.11) | copy-start | bytes 172036
  2.7 0.7 %copy-start.5 = (s32[1,1,5,4,256]{4,3,2,1,0:T(4,128)S(1)}, s32[1,1,5,4,256]{4,3,2,1,0:T(4,128)}, u32[]{:S(2)}) copy-start(s32[1,1,5,4,256]{4,3,2,1,0:T(4,128)} %param.16) | copy-start | bytes 61444
  3.5 34.9 %copy-start.1 = (bf16[1,1,8,2,256,256]{5,4,3,2,1,0:T(8,128)(2,1)S(1)}, bf16[1,1,8,2,256,256]{5,4,3,2,1,0:T(8,128)(2,1)}, u32[]{:S(2)}) copy-start(bf16[1,1,8,2,256,256]{5,4,3,2,1,0:T(8,128)(2,1)} %param.19) | copy-start | bytes 6291460
  4.3 0.8 %copy-start.3 = (s32[1,6,2048]{2,0,1:T(1,128)S(1)}, s32[1,6,2048]{2,0,1:T(1,128)}, u32[]{:S(2)}) copy-start(s32[1,6,2048]{2,0,1:T(1,128)} %param.12) | copy-start | bytes 147460
  5.1 0.8 %copy-start.4 = (f32[1,6,2048]{2,0,1:T(1,128)S(1)}, f32[1,6,2048]{2,0,1:T(1,128)}, u32[]{:S(2)}) copy-start(f32[1,6,2048]{2,0,1:T(1,128)} %param.13) | copy-start | bytes 147460
  5.9 32.4 %copy-start.6 = (s32[1,2048]{1,0:T(1,128)S(1)}, s32[1,2048]{1,0:T(1,128)}, u32[]{:S(2)}) copy-start(s32[1,2048]{1,0:T(1,128)} %mask.1) | copy-start | bytes 24580
  6.3 41.4 %collective-permute-start = (bf16[144,2048]{1,0:T(8,128)(2,1)S(1)}, bf16[144,2048]{1,0:T(8,128)(2,1)S(1)}, u32[]{:S(2)}, u32[]{:S(2)}) collective-permute-start(bf16[144,2048]{1,0:T(8,128)(2,1)S(1)} %get-tuple-element.17.bulk), channel_id=1, source_target_pairs={{0,1},{1,2},{2,3},{3,4},{4,5},{5,6},{6,7},{7,8},{8,9},{9,10},{10,1... | collective-permute-start | bytes 1769480 | tf_op jit(solution)/shard_map/ppermute | solution.py:229
  8.0 39.8 %collective-permute-start.1 = (bf16[144,2048]{1,0:T(8,128)(2,1)S(1)}, bf16[144,2048]{1,0:T(8,128)(2,1)S(1)}, u32[]{:S(2)}, u32[]{:S(2)}) collective-permute-start(bf16[144,2048]{1,0:T(8,128)(2,1)S(1)} %get-tuple-element.17.bulk), channel_id=1, source_target_pairs={{0,63},{1,0},{2,1},{3,2},{4,3},{5,4},{6,5},{7,6},{8,7},{9,8},{10,9... | collective-permute-start | bytes 1769480 | tf_op jit(solution)/shard_map/ppermute | solution.py:229
  15.3 8.1 %collective-permute-start.2 = (bf16[4,16,256]{2,1,0:T(8,128)(2,1)S(1)}, bf16[4,16,256]{2,1,0:T(8,128)(2,1)S(1)}, u32[]{:S(2)}, u32[]{:S(2)}) collective-permute-start(bf16[4,16,256]{2,1,0:T(8,128)(2,1)S(1)} %get-tuple-element.22), channel_id=1, source_target_pairs={{0,126},{1,127},{2,64},{3,65},{4,66},{5,67},{6,68},{7,69},{8,70},{... | collective-permute-start | bytes 98312 | tf_op jit(solution)/shard_map/ppermute | solution.py:229
  16.3 12.9 %collective-permute-start.3 = (bf16[4,16,256]{2,1,0:T(8,128)(2,1)S(1)}, bf16[4,16,256]{2,1,0:T(8,128)(2,1)S(1)}, u32[]{:S(2)}, u32[]{:S(2)}) collective-permute-start(bf16[4,16,256]{2,1,0:T(8,128)(2,1)S(1)} %get-tuple-element.23), channel_id=1, source_target_pairs={{0,127},{1,64},{2,65},{3,66},{4,67},{5,68},{6,69},{7,70},{8,71},{9... | collective-permute-start | bytes 98312 | tf_op jit(solution)/shard_map/ppermute | solution.py:229
  18.3 13.7 %collective-permute-start.4 = (bf16[4,16,256]{2,1,0:T(8,128)(2,1)S(1)}, bf16[4,16,256]{2,1,0:T(8,128)(2,1)S(1)}, u32[]{:S(2)}, u32[]{:S(2)}) collective-permute-start(bf16[4,16,256]{2,1,0:T(8,128)(2,1)S(1)} %get-tuple-element.24), channel_id=1, source_target_pairs={{0,64},{1,65},{2,66},{3,67},{4,68},{5,69},{6,70},{7,71},{8,72},{9,... | collective-permute-start | bytes 98312 | tf_op jit(solution)/shard_map/ppermute | solution.py:229
  23.3 8.8 %collective-permute-start.5 = (bf16[4,16,256]{2,1,0:T(8,128)(2,1)S(1)}, bf16[4,16,256]{2,1,0:T(8,128)(2,1)S(1)}, u32[]{:S(2)}, u32[]{:S(2)}) collective-permute-start(bf16[4,16,256]{2,1,0:T(8,128)(2,1)S(1)} %get-tuple-element.25), channel_id=1, source_target_pairs={{0,65},{1,66},{2,67},{3,68},{4,69},{5,70},{6,71},{7,72},{8,73},{9,... | collective-permute-start | bytes 98312 | tf_op jit(solution)/shard_map/ppermute | solution.py:229
  29.2 9.1 %collective-permute-start.6 = (bf16[4,16,256]{2,1,0:T(8,128)(2,1)S(1)}, bf16[4,16,256]{2,1,0:T(8,128)(2,1)S(1)}, u32[]{:S(2)}, u32[]{:S(2)}) collective-permute-start(bf16[4,16,256]{2,1,0:T(8,128)(2,1)S(1)} %get-tuple-element.16.after), channel_id=1, source_target_pairs={{0,66},{1,67},{2,68},{3,69},{4,70},{5,71},{6,72},{7,73},{8,74},{9,... | collective-permute-start | bytes 98312 | tf_op jit(solution)/shard_map/ppermute | solution.py:229
  40.3 11.8 %collective-permute-start.7 = (bf16[16,2048]{1,0:T(8,128)(2,1)S(1)}, bf16[16,2048]{1,0:T(8,128)(2,1)S(1)}, u32[]{:S(2)}, u32[]{:S(2)}) collective-permute-start(bf16[16,2048]{1,0:T(8,128)(2,1)S(1)} %get-tuple-element.28.top_half), channel_id=1, source_target_pairs={{0,1},{1,2},{2,3},{3,4},{4,5},{5,6},{6,7},{7,8},{8,9},{9,10},{10,1... | collective-permute-start | bytes 196616 | tf_op jit(solution)/shard_map/ppermute | solution.py:229
  41.1 11.0 %collective-permute-start.8 = (bf16[16,2048]{1,0:T(8,128)(2,1)S(1)}, bf16[16,2048]{1,0:T(8,128)(2,1)S(1)}, u32[]{:S(2)}, u32[]{:S(2)}) collective-permute-start(bf16[16,2048]{1,0:T(8,128)(2,1)S(1)} %get-tuple-element.28.top_half), channel_id=1, source_target_pairs={{0,63},{1,0},{2,1},{3,2},{4,3},{5,4},{6,5},{7,6},{8,7},{9,8},{10,9... | collective-permute-start | bytes 196616 | tf_op jit(solution)/shard_map/ppermute | solution.py:229

commit v3 on v2

v3 whole, which is shorter than its diff:
```python
import jax
import jax.numpy as jnp
from jax import lax
from jax.experimental import pallas as pl
from jax.experimental.pallas import tpu as pltpu
from jax.sharding import PartitionSpec as P

F32, BF16 = jnp.float32, jnp.bfloat16
RIM = 512
NSUB = 4
TB = 256
WIN = TB + 2 * RIM
LANE = 128
NEVER = 64.0
FIELDS, LEVELS, COLS = 16, 8, 2048
REST = (LEVELS - 1) * FIELDS
WIDE = COLS - RIM
PICK_MIB = 63
PAY = 4 + 2 * WIDE // TB


def mix_kernel(
    state_hbm, rate_hbm, send_hbm, offs_hbm, coef_hbm, mask_hbm, couple_hbm, packed, mix0, mixr, bulk, tabs, gate,
    state, rate, send, offs, coef, mask, couple, sems,
):
    pairs = (
        (state_hbm.at[0, 0:2], state.at[0:2]),
        (rate_hbm, rate),
        (send_hbm, send),
        (offs_hbm, offs),
        (coef_hbm, coef),
        (mask_hbm, mask),
        (couple_hbm, couple),
        (state_hbm.at[0, 2:LEVELS], state.at[2:LEVELS]),
    )
    copies = [pltpu.make_async_copy(a, b, sems.at[i]) for i, (a, b) in enumerate(pairs)]
    for copy in copies:
        copy.start()
    for copy in copies[:3]:
        copy.wait()
    for c in range(0, COLS, TB):
        here = slice(c, c + TB)
        v0 = state[0, :, here]
        mix0[:, here] = v0 + rate[0, :, here] * (state[1, :, here] - v0)
    for k in range(5):
        for j in range(4):
            for h in range(2):
                index = send[k, j : j + 1, h * LANE : (h + 1) * LANE]
                low = jnp.broadcast_to(index & (LANE - 1), (FIELDS, LANE))
                high = jnp.broadcast_to(lax.shift_right_logical(index, 7), (FIELDS, LANE))
                total = jnp.zeros((FIELDS, LANE), F32)
                for p in range(COLS // LANE):
                    got = jnp.take_along_axis(
                        mix0[:, p * LANE : (p + 1) * LANE], low, axis=1, mode="promise_in_bounds"
                    )
                    total = jnp.where(high == p, got, total)
                packed[k, j, :, h * LANE : (h + 1) * LANE] = total.astype(BF16)
    for copy in copies[3:]:
        copy.wait()
    eye = lax.broadcasted_iota(jnp.int32, (FIELDS, FIELDS), 0) == lax.broadcasted_iota(
        jnp.int32, (FIELDS, FIELDS), 1
    )
    couple_column = jnp.sum(
        jnp.where(eye, jnp.broadcast_to(couple[...], (FIELDS, FIELDS)), 0.0), axis=1, keepdims=True
    )
    for n in range(COLS // TB):
        here = slice(n * TB, (n + 1) * TB)
        gate[:, here] = couple_column * mask[0:1, here].astype(F32)
        before = state[0, :, here]
        mid = state[1, :, here]
        flux = rate[0, :, here] * (mid - before)
        for l in range(1, LEVELS):
            if l < LEVELS - 1:
                after_mid = state[l + 1, :, here]
                below = rate[l, :, here] * (after_mid - mid)
                new = mid + below - flux
                flux, mid = below, after_mid
            else:
                new = mid - flux
            mixr[(l - 1) * FIELDS : l * FIELDS, here] = new
            bulk[(l - 1) * FIELDS : l * FIELDS, here] = new.astype(BF16)
        lane = lax.broadcasted_iota(jnp.int32, (1, TB), 1) + RIM
        off = [offs[j, :, here] for j in range(6)]
        val = [coef[j, :, here] for j in range(6)]
        zero = jnp.zeros((1, TB), F32)
        rows_c, rows_h, rows_l = [], [], []
        for j in range(6):
            merged = val[j]
            repeated = zero
            for i in range(6):
                if i != j:
                    same = off[i] == off[j]
                    merged = merged + jnp.where(same, val[i], 0.0)
                    if i < j:
                        repeated = jnp.where(same, 1.0, repeated)
            place = off[j] + lane
            rows_c.append(jnp.where(repeated > 0.5, 0.0, merged))
            rows_h.append(jnp.where(repeated > 0.5, NEVER, lax.shift_right_logical(place, 7).astype(F32)))
            rows_l.append((place & (LANE - 1)).astype(F32))
        tabs[2 * n] = jnp.concatenate(rows_c + [zero] * 2 + rows_h + [zero] * 2, axis=0).astype(BF16)
        tabs[2 * n + 1] = jnp.concatenate(rows_l + [zero] * 10, axis=0).astype(BF16)


def parities():
    d = lax.axis_index("dom")
    return (d & 1) == 0, (d & 2) == 0


def stage_kernel(swapped, tabs, e1, o1, e2, o2, kept):
    near, far = parities()
    e1[0:4] = swapped[jnp.where(near, 3, 1)]
    e1[4:PAY] = tabs[pl.ds(jnp.where(near, 2 * COLS // TB - (PAY - 4), 0), PAY - 4)]
    o1[0:4] = swapped[jnp.where(near, 1, 3)]
    o1[4:PAY] = tabs[pl.ds(jnp.where(near, 0, 2 * COLS // TB - (PAY - 4)), PAY - 4)]
    kept[...] = tabs[...]
    e2[...] = swapped[jnp.where(far, 4, 0)]
    o2[...] = swapped[jnp.where(far, 0, 4)]


def build_bands(tab, rel, band, into, count, tabs, start):
    rows = [
        (lax.broadcasted_iota(jnp.int32, (16, LANE), 0) + r).astype(F32).astype(BF16) for r in range(0, LANE, 16)
    ]

    @pl.loop(0, count)
    def _(b):
        first = tabs[start + 2 * b].astype(F32)
        second = tabs[start + 2 * b + 1].astype(F32)
        tab[0:8] = first[0:8]
        tab[8:16] = first[8:16] * float(LANE) + second[0:8]
        for half in range(TB // LANE):
            lanes = slice(half * LANE, (half + 1) * LANE)
            coefs = [jnp.broadcast_to(tab[j : j + 1, lanes], (16, LANE)).astype(BF16) for j in range(6)]
            first_row = half * LANE
            last_row = first_row + LANE + 2 * RIM
            if first_row:
                band[into + b, 0:first_row, lanes] = jnp.zeros((first_row, LANE), BF16)
            if last_row < WIN:
                band[into + b, last_row:WIN, lanes] = jnp.zeros((WIN - last_row, LANE), BF16)
            for base in range(first_row, last_row, LANE):
                slot = 8 * (half * (WIN // LANE) + base // LANE)
                rel[slot : slot + 8, :] = tab[8:16, lanes] - float(base)
                there = [
                    jnp.broadcast_to(rel[slot + j : slot + j + 1, :], (16, LANE)).astype(BF16) for j in range(6)
                ]
                for r in range(0, LANE, 16):
                    total = jnp.zeros((16, LANE), BF16)
                    for j in range(6):
                        total = jnp.where(there[j] == rows[r // 16], coefs[j], total)
                    band[into + b, base + r : base + r + 16, lanes] = total


def own_band_kernel(tabs, after, band, tab, rel):
    del after
    build_bands(tab, rel, band, 0, COLS // TB, tabs, 0)


def side_band_kernel(e1, tabs, o1, after, band, keep, tab, rel):
    del after
    near, _ = parities()
    side = WIDE // TB
    places = (
        (e1, 4, side, jnp.where(near, WIDE + COLS, 0)),
        (tabs, 0, COLS // TB, WIDE),
        (o1, 4, side, jnp.where(near, 0, WIDE + COLS)),
    )
    for ref, start, count, base in places:
        for b in range(count):
            coefs = ref[start + 2 * b].astype(F32)[0:8]
            at = base + b * TB
            at = at if isinstance(at, int) else pl.multiple_of(at, TB)
            keep[:, pl.ds(at, TB)] = 1.0 - jnp.sum(coefs, axis=0, keepdims=True)
    build_bands(tab, rel, band, jnp.where(near, side, 0), side, e1, 4)
    build_bands(tab, rel, band, jnp.where(near, 0, side), side, o1, 4)


def remap_kernel(live, source, e1, o1, e2, o2, swapped, weights, mix0, gate, after, forcing, top, top_half, got):
    del after
    near, far = parities()
    got[pl.ds(jnp.where(far, 0, 16), 4)] = e2[...]
    got[pl.ds(jnp.where(near, 4, 12), 4)] = e1[0:4]
    got[8:12] = swapped[2]
    got[pl.ds(jnp.where(near, 12, 4), 4)] = o1[0:4]
    got[pl.ds(jnp.where(far, 16, 0), 4)] = o2[...]
    ones = jnp.ones((16, TB), BF16)
    for n in range(COLS // TB):
        here = slice(n * TB, (n + 1) * TB)
        num = jnp.zeros((FIELDS, TB), F32)
        den = jnp.zeros((1, TB), F32)
        for m in range(2):
            q = source[m, n]
            valid = jnp.where((q & 3) < live[0, lax.shift_right_logical(q, 2)], 1.0, 0.0).astype(F32)
            rows = jnp.concatenate([got[q], ones], axis=0)
            both = lax.dot_general(
                rows, weights[n, m], (((1,), (1,)), ((), ())), preferred_element_type=F32
            )
            num = num + valid * both[0:FIELDS]
            den = den + valid * both[FIELDS : FIELDS + 1]
        value = num / jnp.maximum(den, 1.0)
        forcing[:, here] = value
        old = mix0[:, here]
        new = old + gate[:, here] * (value - old)
        top[:, here] = new
        top_half[:, here] = new.astype(BF16)


def columns_of(parts, start, size):
    pieces = []
    while size:
        which, at = divmod(start, COLS)
        step = min(size, COLS - at)
        pieces.append(parts[which][:, at : at + step])
        start, size = start + step, size - step
    return pieces[0] if len(pieces) == 1 else jnp.concatenate(pieces, axis=1)


def diffuse_kernel(
    band_own, band_side, keep, mixr, bulk_e, bulk, bulk_o, top, top_e, top_half, top_o, out, xa, xb, st,
):
    edge = WIDE // TB
    own = COLS // TB
    nb = own + 2 * edge
    bufs = (xa, xb)

    def matrix(b):
        if edge <= b < edge + own:
            return band_own[b - edge]
        return band_side[b if b < edge else b - own]

    def first_step(tops, rests):
        for b in range(nb):
            at = slice(b * TB, (b + 1) * TB)
            mine = slice((b - edge) * TB, (b - edge + 1) * TB)
            rows = jnp.concatenate([columns_of(tops, b * TB, WIN), columns_of(rests, b * TB, WIN)], axis=0)
            if edge <= b < edge + own:
                old = jnp.concatenate([top[:, mine], mixr[:, mine]], axis=0)
            else:
                start = RIM + b * TB
                old = jnp.concatenate([columns_of(tops, start, TB), columns_of(rests, start, TB)], axis=0).astype(F32)
            new = old * keep[:, at] + jnp.dot(rows, matrix(b), preferred_element_type=F32)
            st[:, at] = new
            xa[:, at] = new.astype(BF16)

    near, _ = parities()

    @pl.when(near)
    def _():
        first_step((top_o, top_half, top_e), (bulk_o, bulk, bulk_e))

    @pl.when(jnp.logical_not(near))
    def _():
        first_step((top_e, top_half, top_o), (bulk_e, bulk, bulk_o))

    for step in range(1, NSUB):
        src, dst = bufs[(step + 1) % 2], bufs[step % 2]
        skip = step * (RIM // TB)
        for b in range(skip, nb - skip):
            at = slice(b * TB, (b + 1) * TB)
            rows = src[:, b * TB - RIM : b * TB - RIM + WIN]
            new = st[:, at] * keep[:, at] + jnp.dot(rows, matrix(b), preferred_element_type=F32)
            if step < NSUB - 1:
                st[:, at] = new
                dst[:, at] = new.astype(BF16)
            else:
                out[:, (b - edge) * TB : (b - edge + 1) * TB] = new


def crossed(value):
    size = (lax.axis_size("comp"), lax.axis_size("dom"))
    pairs = [(s * size[1] + d, (1 - s) * size[1] + d) for s in range(size[0]) for d in range(size[1])]
    return lax.ppermute(value, ("comp", "dom"), pairs)


def paired(value, apart, odd):
    count = lax.axis_size("dom")
    pairs = [(d, (d + (apart if bool(d & apart) == odd else -apart)) % count) for d in range(count)]
    return lax.ppermute(value, "dom", pairs)


def spec(n):
    return [pl.BlockSpec(memory_space=pltpu.VMEM)] * n


ANYWHERE = pl.BlockSpec(memory_space=pl.ANY)
SCALARS = pl.BlockSpec(memory_space=pltpu.SMEM)


def params(mib):
    return pltpu.CompilerParams(vmem_limit_bytes=mib * 2**20)


def cost(us):
    return pl.CostEstimate(flops=0, bytes_accessed=us * 3_000_000, transcendentals=0)


def shards(
    column_state, vert_rate, hor_offsets, hor_coef, open_mask, couple_rate, send_index, live_slots, block_source,
    remap_weight,
):
    shape = jax.ShapeDtypeStruct
    rate = vert_rate.transpose(1, 0, 2)
    packed, mix0, mixr, bulk, tabs, gate = pl.pallas_call(
        mix_kernel,
        out_shape=[
            shape((5, 4, FIELDS, TB), BF16),
            shape((FIELDS, COLS), F32),
            shape((REST, COLS), F32),
            shape((REST, COLS), BF16),
            shape((2 * COLS // TB, 16, TB), BF16),
            shape((FIELDS, COLS), F32),
        ],
        in_specs=[pl.BlockSpec(memory_space=pltpu.HBM)] * 7,
        out_specs=spec(6),
        scratch_shapes=[
            pltpu.VMEM((LEVELS, FIELDS, COLS), F32),
            pltpu.VMEM((LEVELS - 1, 1, COLS), F32),
            pltpu.VMEM((5, 4, TB), jnp.int32),
            pltpu.VMEM((6, 1, COLS), jnp.int32),
            pltpu.VMEM((6, 1, COLS), F32),
            pltpu.VMEM((1, COLS), jnp.int32),
            pltpu.VMEM((1, FIELDS), F32),
            pltpu.SemaphoreType.DMA((8,)),
        ],
        compiler_params=params(PICK_MIB),
        cost_estimate=cost(3),
        name="mix",
    )(
        column_state, rate, send_index[0, 0], hor_offsets.transpose(1, 0, 2), hor_coef.transpose(1, 0, 2), open_mask,
        couple_rate,
    )
    swapped = crossed(packed)

    pair = shape((4, FIELDS, TB), BF16)
    payload = shape((PAY, 16, TB), BF16)
    e1, o1, e2, o2, tabs = pl.pallas_call(
        stage_kernel,
        out_shape=[payload, payload, pair, pair, shape(tabs.shape, BF16)],
        in_specs=spec(2),
        out_specs=spec(5),
        compiler_params=params(4),
        cost_estimate=cost(1),
        name="stage",
    )(swapped, tabs)
    staged = e1
    e1, e2, o1, o2 = paired(e1, 1, False), paired(e2, 2, False), paired(o1, 1, True), paired(o2, 2, True)

    tab = pltpu.VMEM((16, TB), F32)
    rel = pltpu.VMEM((16 * (WIN // LANE), LANE), F32)
    band_own = pl.pallas_call(
        own_band_kernel,
        out_shape=shape((COLS // TB, WIN, TB), BF16),
        in_specs=spec(1) + [ANYWHERE],
        out_specs=spec(1)[0],
        scratch_shapes=[tab, rel],
        compiler_params=params(8),
        cost_estimate=cost(3),
        name="own_band",
    )(tabs, staged)
    bulk_later, band_own, e1, e2, o1, o2 = lax.optimization_barrier((bulk, band_own, e1, e2, o1, o2))
    bulk_e, bulk_o = paired(bulk_later, 1, False), paired(bulk_later, 1, True)

    forcing, top, top_half = pl.pallas_call(
        remap_kernel,
        out_shape=[shape((FIELDS, COLS), F32), shape((FIELDS, COLS), F32), shape((FIELDS, COLS), BF16)],
        in_specs=[SCALARS, SCALARS] + spec(8) + [ANYWHERE],
        out_specs=spec(3),
        scratch_shapes=[pltpu.VMEM((20, FIELDS, TB), BF16)],
        compiler_params=params(8),
        cost_estimate=cost(2),
        name="remap",
    )(
        live_slots[0], block_source[0, 0].T, e1, o1, e2, o2, swapped, remap_weight[0, 0], mix0, gate, band_own,
    )
    top_e, top_o = paired(top_half, 1, False), paired(top_half, 1, True)

    band_side, keep = pl.pallas_call(
        side_band_kernel,
        out_shape=[shape((2 * WIDE // TB, WIN, TB), BF16), shape((1, COLS + 2 * WIDE), F32)],
        in_specs=spec(3) + [ANYWHERE],
        out_specs=spec(2),
        scratch_shapes=[tab, rel],
        compiler_params=params(8),
        cost_estimate=cost(4),
        name="side_band",
    )(e1, tabs, o1, top_half)

    half = pltpu.VMEM((LEVELS * FIELDS, COLS + 2 * WIDE), BF16)
    state = pl.pallas_call(
        diffuse_kernel,
        out_shape=shape((LEVELS * FIELDS, COLS), F32),
        in_specs=spec(11),
        out_specs=pl.BlockSpec(memory_space=pltpu.VMEM),
        scratch_shapes=[half, half, pltpu.VMEM((LEVELS * FIELDS, COLS + 2 * WIDE), F32)],
        compiler_params=params(16),
        cost_estimate=cost(6),
        name="diffuse",
    )(band_own, band_side, keep, mixr, bulk_e, bulk, bulk_o, top, top_e, top_half, top_o)
    return state.reshape(1, LEVELS, FIELDS, COLS), forcing[None]


def solution(mesh):
    placed = (
        P("comp", None, None, "dom"),
        P("comp", None, "dom"),
        P("comp", None, "dom"),
        P("comp", None, "dom"),
        P("comp", "dom"),
        P("comp", None),
        P("comp", "dom", None, None, None),
        P("comp", "dom", None),
        P("comp", "dom", None, None),
        P("comp", "dom", None, None, None, None),
    )
    return jax.shard_map(
        shards,
        mesh=mesh,
        in_specs=placed,
        out_specs=(P("comp", None, None, "dom"), P("comp", None, "dom")),
        check_vma=False,
    )
```

time: 58.8 us -> 49.9 us (0.85)
  waiting for transfers between devices: 15.1 us -> 9.44 us
  local copies, waits for them, and re-layouts: 4.39 us -> 0.94 us
  Pallas kernels: 16.6 us -> 18.4 us
  starting transfers between devices: 21.6 us -> 20.2 us
    ppermute x9, waiting for transfers between devices: 15.1 us -> 9.44 us  [the longest x8 7.85 us: paired(): return lax.ppermute(value, 'dom', pairs)]
    unnamed x20 -> x16, local copies, waits for them, and re-layouts: 4.39 us -> 0.94 us
    pallas_call x2, Pallas kernels: 1.27 us -> 3.32 us  [the longest x1 3.29 us: shards(): pl.pallas_call(mix_kernel, out_shape=[shape((5, 4, FIELDS, TB), BF16), sh...]
    ppermute x9, starting transfers between devices: 21.6 us -> 20.2 us  [the longest x8 20.1 us: paired(): return lax.ppermute(value, 'dom', pairs)]
  transfers between devices with their start and end apart: 9 -> 9, of which waited for: 4 -> 3; matrix products, arithmetic and copies ran while one was open for 0% -> 0% of each run, Pallas kernels for 15% -> 17%
where the time goes in v3:
time: 49.9 us; the launch traced here: 49.8 us
  starting transfers between devices  20.2 us (40%)
  Pallas kernels  18.4 us (37%)
  waiting for transfers between devices  9.44 us (19%)
  local copies, waits for them, and re-layouts  0.94 us (2%)
  between operations  0.78 us (2%)
    ppermute x8, starting transfers between devices, paired(): return lax.ppermute(value, 'dom', pairs)  20.1 us
    ppermute x8, waiting for transfers between devices, paired(): return lax.ppermute(value, 'dom', pairs)  7.85 us
    pallas_call x1, Pallas kernels, shards(): pl.pallas_call(diffuse_kernel, out_shape=shape((LEVELS * FIELDS, COLS), F...  6.6 us
    pallas_call x1, Pallas kernels, shards(): pl.pallas_call(side_band_kernel, out_shape=[shape((2 * WIDE // TB, WIN, T...  3.95 us
    pallas_call x1, Pallas kernels, shards(): pl.pallas_call(mix_kernel, out_shape=[shape((5, 4, FIELDS, TB), BF16), sh...  3.29 us
    pallas_call x1, Pallas kernels, shards(): pl.pallas_call(own_band_kernel, out_shape=shape((COLS // TB, WIN, TB), BF...  2.59 us
    pallas_call x1, Pallas kernels, shards(): pl.pallas_call(remap_kernel, out_shape=[shape((FIELDS, COLS), F32), shape...  1.95 us
    ppermute x1, waiting for transfers between devices, crossed(): return lax.ppermute(value, ('comp', 'dom'), pairs)  1.59 us
  transfers between devices with their start and end apart: 9, of which 3 were waited for; matrix products, arithmetic and copies ran while one was open for 0% of the time, Pallas kernels for 17%

profile of v3, /device:TPU:0, one launch (start us, length us, event | category | flops | bytes accessed | tf_op | source)
XLA Modules:
  0.0 49.8 jit_solution(2508232165220357205)
XLA Ops:
  0.6 0.0 copy-start.6
  0.6 0.0 copy-start.7
  0.7 3.3 %mix.1 = (bf16[5,4,16,256]{3,2,1,0:T(8,128)(2,1)}, f32[16,2048]{1,0:T(8,128)}, f32[112,2048]{1,0:T(8,128)}, bf16[112,2048]{1,0:T(8,128)(2,1)}, bf16[16,16,256]{2,1,0:T(8,128)(2,1)}, /*index=5*/f32[16,2048]{1,0:T(8,128)}) custom-call(f32[1,8,16,2048]{3,2,1,0:T(8,128)} %state_hbm.1, f32[7,1,2048]{2,1,0:T(1,128)} %bitcast.15, s32[5,4,256]{2,1,0:T(4,128)} %bitcast.18, ...), custom_call_target="tpu_custom_call" | custom-call | bytes 9000000 | tf_op jit(solution)/shard_map/mix/pallas_call | solution.py:302
  3.9 0.0 copy-start.2
  4.0 0.0 copy-start
  4.0 0.0 copy-start.3
  4.0 0.0 copy-start.4
  4.0 0.1 collective-permute-start
  4.1 1.6 %collective-permute-done.swapped = bf16[5,4,16,256]{3,2,1,0:T(8,128)(2,1)S(1)} collective-permute-done((bf16[5,4,16,256]{3,2,1,0:T(8,128)(2,1)}, bf16[5,4,16,256]{3,2,1,0:T(8,128)(2,1)S(1)}, u32[]{:S(2)}, u32[]{:S(2)}) %collective-permute-start) | collective-permute-done | bytes 163872 | tf_op jit(solution)/shard_map/ppermute | solution.py:271
  5.7 0.9 %copy-done.5 = bf16[16,16,256]{2,1,0:T(8,128)(2,1)S(1)} copy-done((bf16[16,16,256]{2,1,0:T(8,128)(2,1)S(1)}, bf16[16,16,256]{2,1,0:T(8,128)(2,1)}, u32[]{:S(2)}) %copy-start.5) | copy-done | bytes 131096
  6.6 8.8 %collective-permute-start.3 = (bf16[16,16,256]{2,1,0:T(8,128)(2,1)S(1)}, bf16[16,16,256]{2,1,0:T(8,128)(2,1)S(1)}, u32[]{:S(2)}, u32[]{:S(2)}) collective-permute-start(bf16[16,16,256]{2,1,0:T(8,128)(2,1)S(1)} %get-tuple-element.30), channel_id=1, source_target_pairs={{0,63},{1,2},{2,1},{3,4},{4,3},{5,6},{6,5},{7,8},{8,7},{9,10},{10,... | collective-permute-start | bytes 393224 | tf_op jit(solution)/shard_map/ppermute | solution.py:277
  15.5 0.0 collective-permute-start.1
  15.5 0.0 collective-permute-start.2
  15.5 3.7 %collective-permute-start.4 = (bf16[4,16,256]{2,1,0:T(8,128)(2,1)S(1)}, bf16[4,16,256]{2,1,0:T(8,128)(2,1)S(1)}, u32[]{:S(2)}, u32[]{:S(2)}) collective-permute-start(bf16[4,16,256]{2,1,0:T(8,128)(2,1)S(1)} %get-tuple-element.31), channel_id=1, source_target_pairs={{0,62},{1,63},{2,4},{3,5},{4,2},{5,3},{6,8},{7,9},{8,6},{9,7},{10,... | collective-permute-start | bytes 98312 | tf_op jit(solution)/shard_map/ppermute | solution.py:277
  19.2 2.6 %own_band.1.after.band_own = bf16[8,1280,256]{2,1,0:T(8,128)(2,1)S(1)} custom-call(bf16[16,16,256]{2,1,0:T(8,128)(2,1)S(1)} %get-tuple-element.27.tabs, bf16[16,16,256]{2,1,0:T(8,128)(2,1)S(1)} %get-tuple-element.28.after), custom_call_target="tpu_custom_call" | custom-call | bytes 9000000 | tf_op jit(solution)/shard_map/own_band/pallas_call | solution.py:349
  21.8 0.0 copy-start.1
  21.8 0.0 collective-permute-done.2.e2
  21.8 3.3 %collective-permute-done.4.o2 = bf16[4,16,256]{2,1,0:T(8,128)(2,1)S(1)} collective-permute-done((bf16[4,16,256]{2,1,0:T(8,128)(2,1)S(1)}, bf16[4,16,256]{2,1,0:T(8,128)(2,1)S(1)}, u32[]{:S(2)}, u32[]{:S(2)}) %collective-permute-start.4) | collective-permute-done | bytes 32800 | tf_op jit(solution)/shard_map/ppermute | solution.py:277
  25.1 0.0 collective-permute-done.3.o1
  25.1 0.0 collective-permute-done.1.e1
  25.1 0.0 copy-done.2
  25.1 4.6 %collective-permute-start.6 = (bf16[112,2048]{1,0:T(8,128)(2,1)S(1)}, bf16[112,2048]{1,0:T(8,128)(2,1)S(1)}, u32[]{:S(2)}, u32[]{:S(2)}) collective-permute-start(bf16[112,2048]{1,0:T(8,128)(2,1)S(1)} %copy-done.2), channel_id=1, source_target_pairs={{0,63},{1,2},{2,1},{3,4},{4,3},{5,6},{6,5},{7,8},{8,7},{9,10},{10,... | collective-permute-start | bytes 1376264 | tf_op jit(solution)/shard_map/ppermute | solution.py:277
  29.7 0.0 collective-permute-start.5
  29.8 2.0 %remap.1 = (f32[16,2048]{1,0:T(8,128)}, f32[16,2048]{1,0:T(8,128)S(1)}, bf16[16,2048]{1,0:T(8,128)(2,1)S(1)}) custom-call(s32[1,5]{1,0:T(1,128)S(1)} %bitcast.13, s32[2,8]{1,0:T(2,128)S(1)} %bitcast.12, bf16[16,16,256]{2,1,0:T(8,128)(2,1)S(1)} %collective-permute-done.1.e1, bf16[16,16,256]{2,1,0:T(8,128)(2,1)S(1)} %collective-permute-done.3.o1, ...), custom_call_target="tpu_custom_call" | custom-call | bytes 6000000 | tf_op jit(solution)/shard_map/remap/pallas_call | solution.py:362
  31.7 2.9 %collective-permute-start.8 = (bf16[16,2048]{1,0:T(8,128)(2,1)S(1)}, bf16[16,2048]{1,0:T(8,128)(2,1)S(1)}, u32[]{:S(2)}, u32[]{:S(2)}) collective-permute-start(bf16[16,2048]{1,0:T(8,128)(2,1)S(1)} %get-tuple-element.39.after.top_half), channel_id=1, source_target_pairs={{0,63},{1,2},{2,1},{3,4},{4,3},{5,6},{6,5},{7,8},{8,7},{9,10},{10,... | collective-permute-start | bytes 196616 | tf_op jit(solution)/shard_map/ppermute | solution.py:277
  34.7 0.0 collective-permute-start.7
  34.7 4.0 %side_band.1 = (bf16[12,1280,256]{2,1,0:T(8,128)(2,1)S(1)}, f32[1,5120]{1,0:T(1,128)S(1)}) custom-call(bf16[16,16,256]{2,1,0:T(8,128)(2,1)S(1)} %collective-permute-done.1.e1, bf16[16,16,256]{2,1,0:T(8,128)(2,1)S(1)} %get-tuple-element.27.tabs, bf16[16,16,256]{2,1,0:T(8,128)(2,1)S(1)} %collective-permute-done.3.o1, ...), custom_call_target="tpu_custom_call" | custom-call | bytes 12000000 | tf_op jit(solution)/shard_map/side_band/pallas_call | solution.py:376
  38.6 4.6 %collective-permute-done.8.top_o = bf16[16,2048]{1,0:T(8,128)(2,1)S(1)} collective-permute-done((bf16[16,2048]{1,0:T(8,128)(2,1)S(1)}, bf16[16,2048]{1,0:T(8,128)(2,1)S(1)}, u32[]{:S(2)}, u32[]{:S(2)}) %collective-permute-start.8) | collective-permute-done | bytes 65568 | tf_op jit(solution)/shard_map/ppermute | solution.py:277
  43.2 0.0 collective-permute-done.7.top_e
  43.2 0.0 collective-permute-done.6.bulk_o
  43.2 0.0 collective-permute-done.5.bulk_e
  43.2 6.6 %diffuse.1 = f32[128,2048]{1,0:T(8,128)} custom-call(bf16[8,1280,256]{2,1,0:T(8,128)(2,1)S(1)} %own_band.1.after.band_own, bf16[12,1280,256]{2,1,0:T(8,128)(2,1)S(1)} %get-tuple-element.40.band_side, f32[1,5120]{1,0:T(1,128)S(1)} %get-tuple-element.41.keep, f32[112,2048]{1,0:T(8,128)S(1)} %copy-done.1, bf16[112,2048]{1,0:T(8,128)(2,1)S(1)} %collective-permute-done.5.bulk_e, ...), custom_call_target="tpu_custom_call" | custom-call | bytes 18000000 | tf_op jit(solution)/shard_map/diffuse/pallas_call | solution.py:388
  (8 shorter events, 0.0 us)
Async XLA Ops:
  0.6 29.1 %copy-start.6 = (s32[1,1,8,2]{2,3,1,0:T(2,128)S(1)}, s32[1,1,8,2]{2,3,1,0:T(2,128)}, u32[]{:S(2)}) copy-start(s32[1,1,8,2]{2,3,1,0:T(2,128)} %param.18) | copy-start | bytes 196
  0.6 29.1 %copy-start.7 = (s32[1,1,5]{2,1,0:T(1,128)S(1)}, s32[1,1,5]{2,1,0:T(1,128)}, u32[]{:S(2)}) copy-start(s32[1,1,5]{2,1,0:T(1,128)} %param.17) | copy-start | bytes 64
  3.9 21.2 %copy-start.2 = (bf16[112,2048]{1,0:T(8,128)(2,1)S(1)}, bf16[112,2048]{1,0:T(8,128)(2,1)}, u32[]{:S(2)}) copy-start(bf16[112,2048]{1,0:T(8,128)(2,1)} %get-tuple-element.43.bulk) | copy-start | bytes 1376260
  4.0 25.8 %copy-start = (bf16[1,1,8,2,256,256]{5,4,3,2,1,0:T(8,128)(2,1)S(1)}, bf16[1,1,8,2,256,256]{5,4,3,2,1,0:T(8,128)(2,1)}, u32[]{:S(2)}) copy-start(bf16[1,1,8,2,256,256]{5,4,3,2,1,0:T(8,128)(2,1)} %param.19) | copy-start | bytes 6291460
  4.0 25.8 %copy-start.3 = (f32[16,2048]{1,0:T(8,128)S(1)}, f32[16,2048]{1,0:T(8,128)}, u32[]{:S(2)}) copy-start(f32[16,2048]{1,0:T(8,128)} %get-tuple-element.37.mix0) | copy-start | bytes 393220
  4.0 25.8 %copy-start.4 = (f32[16,2048]{1,0:T(8,128)S(1)}, f32[16,2048]{1,0:T(8,128)}, u32[]{:S(2)}) copy-start(f32[16,2048]{1,0:T(8,128)} %get-tuple-element.38.gate) | copy-start | bytes 393220
  4.0 1.7 %collective-permute-start = (bf16[5,4,16,256]{3,2,1,0:T(8,128)(2,1)}, bf16[5,4,16,256]{3,2,1,0:T(8,128)(2,1)S(1)}, u32[]{:S(2)}, u32[]{:S(2)}) collective-permute-start(bf16[5,4,16,256]{3,2,1,0:T(8,128)(2,1)} %get-tuple-element.25), channel_id=1, source_target_pairs={{0,64},{1,65},{2,66},{3,67},{4,68},{5,69},{6,70},{7,71},{8,72},{9,... | collective-permute-start | bytes 491528 | tf_op jit(solution)/shard_map/ppermute | solution.py:271
  5.7 0.9 %copy-start.5 = (bf16[16,16,256]{2,1,0:T(8,128)(2,1)S(1)}, bf16[16,16,256]{2,1,0:T(8,128)(2,1)}, u32[]{:S(2)}) copy-start(bf16[16,16,256]{2,1,0:T(8,128)(2,1)} %get-tuple-element.26.tabs) | copy-start | bytes 393220
  6.6 18.5 %collective-permute-start.3 = (bf16[16,16,256]{2,1,0:T(8,128)(2,1)S(1)}, bf16[16,16,256]{2,1,0:T(8,128)(2,1)S(1)}, u32[]{:S(2)}, u32[]{:S(2)}) collective-permute-start(bf16[16,16,256]{2,1,0:T(8,128)(2,1)S(1)} %get-tuple-element.30), channel_id=1, source_target_pairs={{0,63},{1,2},{2,1},{3,4},{4,3},{5,6},{6,5},{7,8},{8,7},{9,10},{10,... | collective-permute-start | bytes 393224 | tf_op jit(solution)/shard_map/ppermute | solution.py:277
  15.5 9.7 %collective-permute-start.1 = (bf16[16,16,256]{2,1,0:T(8,128)(2,1)S(1)}, bf16[16,16,256]{2,1,0:T(8,128)(2,1)S(1)}, u32[]{:S(2)}, u32[]{:S(2)}) collective-permute-start(bf16[16,16,256]{2,1,0:T(8,128)(2,1)S(1)} %get-tuple-element.28.after), channel_id=1, source_target_pairs={{0,1},{1,0},{2,3},{3,2},{4,5},{5,4},{6,7},{7,6},{8,9},{9,8},{10,11... | collective-permute-start | bytes 393224 | tf_op jit(solution)/shard_map/ppermute | solution.py:277
  15.5 6.4 %collective-permute-start.2 = (bf16[4,16,256]{2,1,0:T(8,128)(2,1)S(1)}, bf16[4,16,256]{2,1,0:T(8,128)(2,1)S(1)}, u32[]{:S(2)}, u32[]{:S(2)}) collective-permute-start(bf16[4,16,256]{2,1,0:T(8,128)(2,1)S(1)} %get-tuple-element.29), channel_id=1, source_target_pairs={{0,2},{1,3},{2,0},{3,1},{4,6},{5,7},{6,4},{7,5},{8,10},{9,11},{10,... | collective-permute-start | bytes 98312 | tf_op jit(solution)/shard_map/ppermute | solution.py:277
  15.5 9.6 %collective-permute-start.4 = (bf16[4,16,256]{2,1,0:T(8,128)(2,1)S(1)}, bf16[4,16,256]{2,1,0:T(8,128)(2,1)S(1)}, u32[]{:S(2)}, u32[]{:S(2)}) collective-permute-start(bf16[4,16,256]{2,1,0:T(8,128)(2,1)S(1)} %get-tuple-element.31), channel_id=1, source_target_pairs={{0,62},{1,63},{2,4},{3,5},{4,2},{5,3},{6,8},{7,9},{8,6},{9,7},{10,... | collective-permute-start | bytes 98312 | tf_op jit(solution)/shard_map/ppermute | solution.py:277
  21.8 21.4 %copy-start.1 = (f32[112,2048]{1,0:T(8,128)S(1)}, f32[112,2048]{1,0:T(8,128)}, u32[]{:S(2)}) copy-start(f32[112,2048]{1,0:T(8,128)} %get-tuple-element.42.mixr) | copy-start | bytes 2752516
  25.1 18.1 %collective-permute-start.6 = (bf16[112,2048]{1,0:T(8,128)(2,1)S(1)}, bf16[112,2048]{1,0:T(8,128)(2,1)S(1)}, u32[]{:S(2)}, u32[]{:S(2)}) collective-permute-start(bf16[112,2048]{1,0:T(8,128)(2,1)S(1)} %copy-done.2), channel_id=1, source_target_pairs={{0,63},{1,2},{2,1},{3,4},{4,3},{5,6},{6,5},{7,8},{8,7},{9,10},{10,... | collective-permute-start | bytes 1376264 | tf_op jit(solution)/shard_map/ppermute | solution.py:277
  29.7 13.4 %collective-permute-start.5 = (bf16[112,2048]{1,0:T(8,128)(2,1)S(1)}, bf16[112,2048]{1,0:T(8,128)(2,1)S(1)}, u32[]{:S(2)}, u32[]{:S(2)}) collective-permute-start(bf16[112,2048]{1,0:T(8,128)(2,1)S(1)} %copy-done.2), channel_id=1, source_target_pairs={{0,1},{1,0},{2,3},{3,2},{4,5},{5,4},{6,7},{7,6},{8,9},{9,8},{10,11... | collective-permute-start | bytes 1376264 | tf_op jit(solution)/shard_map/ppermute | solution.py:277
  31.7 11.4 %collective-permute-start.8 = (bf16[16,2048]{1,0:T(8,128)(2,1)S(1)}, bf16[16,2048]{1,0:T(8,128)(2,1)S(1)}, u32[]{:S(2)}, u32[]{:S(2)}) collective-permute-start(bf16[16,2048]{1,0:T(8,128)(2,1)S(1)} %get-tuple-element.39.after.top_half), channel_id=1, source_target_pairs={{0,63},{1,2},{2,1},{3,4},{4,3},{5,6},{6,5},{7,8},{8,7},{9,10},{10,... | collective-permute-start | bytes 196616 | tf_op jit(solution)/shard_map/ppermute | solution.py:277
  34.7 8.5 %collective-permute-start.7 = (bf16[16,2048]{1,0:T(8,128)(2,1)S(1)}, bf16[16,2048]{1,0:T(8,128)(2,1)S(1)}, u32[]{:S(2)}, u32[]{:S(2)}) collective-permute-start(bf16[16,2048]{1,0:T(8,128)(2,1)S(1)} %get-tuple-element.39.after.top_half), channel_id=1, source_target_pairs={{0,1},{1,0},{2,3},{3,2},{4,5},{5,4},{6,7},{7,6},{8,9},{9,8},{10,11... | collective-permute-start | bytes 196616 | tf_op jit(solution)/shard_map/ppermute | solution.py:277

commit v4 on v3

--- a/solution.py
+++ b/solution.py
@@ -20,7 +20,7 @@
 
 
 def mix_kernel(
-    state_hbm, rate_hbm, send_hbm, offs_hbm, coef_hbm, mask_hbm, couple_hbm, packed, mix0, mixr, bulk, tabs, gate,
+    state_hbm, rate_hbm, send_hbm, offs_hbm, coef_hbm, mask_hbm, couple_hbm, packed, mix0, mixr, tabs, gate,
     state, rate, send, offs, coef, mask, couple, sems,
 ):
     pairs = (
@@ -78,7 +78,6 @@
             else:
                 new = mid - flux
             mixr[(l - 1) * FIELDS : l * FIELDS, here] = new
-            bulk[(l - 1) * FIELDS : l * FIELDS, here] = new.astype(BF16)
         lane = lax.broadcasted_iota(jnp.int32, (1, TB), 1) + RIM
         off = [offs[j, :, here] for j in range(6)]
         val = [coef[j, :, here] for j in range(6)]
@@ -150,8 +149,10 @@
                     band[into + b, base + r : base + r + 16, lanes] = total
 
 
-def own_band_kernel(tabs, after, band, tab, rel):
+def own_band_kernel(tabs, mixr, after, band, bulk, tab, rel):
     del after
+    for c in range(0, COLS, TB):
+        bulk[:, c : c + TB] = mixr[:, c : c + TB].astype(BF16)
     build_bands(tab, rel, band, 0, COLS // TB, tabs, 0)
 
 
@@ -170,8 +171,8 @@
             at = base + b * TB
             at = at if isinstance(at, int) else pl.multiple_of(at, TB)
             keep[:, pl.ds(at, TB)] = 1.0 - jnp.sum(coefs, axis=0, keepdims=True)
-    build_bands(tab, rel, band, jnp.where(near, side, 0), side, e1, 4)
-    build_bands(tab, rel, band, jnp.where(near, 0, side), side, o1, 4)
+    build_bands(tab, rel, band, 0, side, e1, 4)
+    build_bands(tab, rel, band, side, side, o1, 4)
 
 
 def remap_kernel(live, source, e1, o1, e2, o2, swapped, weights, mix0, gate, after, forcing, top, top_half, got):
@@ -204,65 +205,116 @@
         top_half[:, here] = new.astype(BF16)
 
 
-def columns_of(parts, start, size):
-    pieces = []
-    while size:
-        which, at = divmod(start, COLS)
-        step = min(size, COLS - at)
-        pieces.append(parts[which][:, at : at + step])
-        start, size = start + step, size - step
-    return pieces[0] if len(pieces) == 1 else jnp.concatenate(pieces, axis=1)
-
-
-def diffuse_kernel(
-    band_own, band_side, keep, mixr, bulk_e, bulk, bulk_o, top, top_e, top_half, top_o, out, xa, xb, st,
-):
-    edge = WIDE // TB
-    own = COLS // TB
-    nb = own + 2 * edge
-    bufs = (xa, xb)
-
-    def matrix(b):
-        if edge <= b < edge + own:
-            return band_own[b - edge]
-        return band_side[b if b < edge else b - own]
-
-    def first_step(tops, rests):
-        for b in range(nb):
-            at = slice(b * TB, (b + 1) * TB)
-            mine = slice((b - edge) * TB, (b - edge + 1) * TB)
-            rows = jnp.concatenate([columns_of(tops, b * TB, WIN), columns_of(rests, b * TB, WIN)], axis=0)
-            if edge <= b < edge + own:
-                old = jnp.concatenate([top[:, mine], mixr[:, mine]], axis=0)
-            else:
-                start = RIM + b * TB
-                old = jnp.concatenate([columns_of(tops, start, TB), columns_of(rests, start, TB)], axis=0).astype(F32)
-            new = old * keep[:, at] + jnp.dot(rows, matrix(b), preferred_element_type=F32)
-            st[:, at] = new
-            xa[:, at] = new.astype(BF16)
-
+EDGE = WIDE // TB
+OWN = COLS // TB
+
+
+def part(blocks, source, bands, keep, old, new):
+    for b, band in blocks:
+        rows = source[:, b * TB : b * TB + WIN]
+        at = slice(b * TB, (b + 1) * TB)
+        new(b, old(b) * keep[:, at] + jnp.dot(rows, bands(band), preferred_element_type=F32))
+
+
+def blocks_of(own, side, on_right):
+    return [(EDGE + n, ("own", n)) for n in own] + [((EDGE + OWN if on_right else 0) + n, ("side", n)) for n in side]
+
+
+def per_order(run):
     near, _ = parities()
 
     @pl.when(near)
     def _():
-        first_step((top_o, top_half, top_e), (bulk_o, bulk, bulk_e))
+        run(True)
 
     @pl.when(jnp.logical_not(near))
     def _():
-        first_step((top_e, top_half, top_o), (bulk_e, bulk, bulk_o))
-
-    for step in range(1, NSUB):
-        src, dst = bufs[(step + 1) % 2], bufs[step % 2]
-        skip = step * (RIM // TB)
-        for b in range(skip, nb - skip):
-            at = slice(b * TB, (b + 1) * TB)
-            rows = src[:, b * TB - RIM : b * TB - RIM + WIN]
-            new = st[:, at] * keep[:, at] + jnp.dot(rows, matrix(b), preferred_element_type=F32)
-            if step < NSUB - 1:
-                st[:, at] = new
-                dst[:, at] = new.astype(BF16)
+        run(False)
+
+
+def begin_kernel(band_own, band_side, keep, mixr, bulk, bulk_e, top, top_half, top_e, st, xa, xb, x0):
+    x0[0:FIELDS, COLS : 2 * COLS] = top_half[...]
+    x0[FIELDS:, COLS : 2 * COLS] = bulk[...]
+
+    def run(right):
+        there = slice(2 * COLS, 3 * COLS) if right else slice(0, COLS)
+        x0[0:FIELDS, there] = top_e[...]
+        x0[FIELDS:, there] = bulk_e[...]
+
+        def bands(band):
+            return band_own[band[1]] if band[0] == "own" else band_side[band[1]]
+
+        for step in range(1, NSUB):
+            count = OWN - 2 * step
+            own = range(2 * step, OWN) if right else range(0, count)
+            side = range(0, count) if right else range(2 * step - 2, EDGE)
+            dst = xa if step % 2 else xb
+
+            def old(b):
+                if step > 1:
+                    return st[:, b * TB : (b + 1) * TB]
+                if EDGE <= b < EDGE + OWN:
+                    mine = slice((b - EDGE) * TB, (b - EDGE + 1) * TB)
+                    return jnp.concatenate([top[:, mine], mixr[:, mine]], axis=0)
+                return x0[:, RIM + b * TB : RIM + (b + 1) * TB].astype(F32)
+
+            def new(b, value):
+                st[:, b * TB : (b + 1) * TB] = value
+                dst[:, RIM + b * TB : RIM + (b + 1) * TB] = value.astype(BF16)
+
+            src = x0 if step == 1 else (xb if step % 2 else xa)
+            part(blocks_of(own, side, right), src, bands, keep, old, new)
+
+    per_order(run)
+
+
+def finish_kernel(
+    band_own, band_side, keep, mixr, bulk, bulk_o, top, top_half, top_o, st_in, xa_in, xb_in, out, st, xa, xb, x0,
+):
+    x0[0:FIELDS, COLS : 2 * COLS] = top_half[...]
+    x0[FIELDS:, COLS : 2 * COLS] = bulk[...]
+
+    def run(right):
+        there = slice(0, COLS) if right else slice(2 * COLS, 3 * COLS)
+        x0[0:FIELDS, there] = top_o[...]
+        x0[FIELDS:, there] = bulk_o[...]
+
+        def bands(band):
+            return band_own[band[1]] if band[0] == "own" else band_side[EDGE + band[1]]
+
+        for step in range(1, NSUB):
+            first = EDGE + (2 * step if right else OWN - 2 * step - 4)
+            at = slice(RIM + first * TB, RIM + (first + 4) * TB)
+            if step % 2:
+                xa[:, at] = xa_in[:, at]
             else:
-                out[:, (b - edge) * TB : (b - edge + 1) * TB] = new
+                xb[:, at] = xb_in[:, at]
+        for step in range(1, NSUB + 1):
+            own = range(0, 2 * step) if right else range(OWN - 2 * step, OWN)
+            side = range(2 * step - 2, EDGE) if right else range(0, OWN - 2 * step)
+            before = range(2 * step - 2, 2 * step) if right else range(OWN - 2 * step, OWN - 2 * step + 2)
+            dst = xa if step % 2 else xb
+
+            def old(b):
+                n = b - EDGE
+                if step > 1:
+                    return (st_in if n in before else st)[:, b * TB : (b + 1) * TB]
+                if 0 <= n < OWN:
+                    mine = slice(n * TB, (n + 1) * TB)
+                    return jnp.concatenate([top[:, mine], mixr[:, mine]], axis=0)
+                return x0[:, RIM + b * TB : RIM + (b + 1) * TB].astype(F32)
+
+            def new(b, value):
+                if step == NSUB:
+                    out[:, (b - EDGE) * TB : (b - EDGE + 1) * TB] = value
+                else:
+                    st[:, b * TB : (b + 1) * TB] = value
+                    dst[:, RIM + b * TB : RIM + (b + 1) * TB] = value.astype(BF16)
+
+            src = x0 if step == 1 else (xb if step % 2 else xa)
+            part(blocks_of(own, side, not right), src, bands, keep, old, new)
+
+    per_order(run)
 
 
 def crossed(value):
@@ -290,7 +342,7 @@
 
 
 def cost(us):
-    return pl.CostEstimate(flops=0, bytes_accessed=us * 3_000_000, transcendentals=0)
+    return pl.CostEstimate(flops=us * 1_000_000_000, bytes_accessed=us * 3_000_000, transcendentals=0)
 
 
 def shards(
@@ -299,18 +351,17 @@
 ):
     shape = jax.ShapeDtypeStruct
     rate = vert_rate.transpose(1, 0, 2)
-    packed, mix0, mixr, bulk, tabs, gate = pl.pallas_call(
+    packed, mix0, mixr, tabs, gate = pl.pallas_call(
         mix_kernel,
         out_shape=[
             shape((5, 4, FIELDS, TB), BF16),
             shape((FIELDS, COLS), F32),
             shape((REST, COLS), F32),
-            shape((REST, COLS), BF16),
             shape((2 * COLS // TB, 16, TB), BF16),
             shape((FIELDS, COLS), F32),
         ],
         in_specs=[pl.BlockSpec(memory_space=pltpu.HBM)] * 7,
-        out_specs=spec(6),
+        out_specs=spec(5),
         scratch_shapes=[
             pltpu.VMEM((LEVELS, FIELDS, COLS), F32),
             pltpu.VMEM((LEVELS - 1, 1, COLS), F32),
@@ -346,17 +397,17 @@
 
     tab = pltpu.VMEM((16, TB), F32)
     rel = pltpu.VMEM((16 * (WIN // LANE), LANE), F32)
-    band_own = pl.pallas_call(
+    band_own, bulk = pl.pallas_call(
         own_band_kernel,
-        out_shape=shape((COLS // TB, WIN, TB), BF16),
-        in_specs=spec(1) + [ANYWHERE],
-        out_specs=spec(1)[0],
+        out_shape=[shape((COLS // TB, WIN, TB), BF16), shape((REST, COLS), BF16)],
+        in_specs=spec(2) + [ANYWHERE],
+        out_specs=spec(2),
         scratch_shapes=[tab, rel],
         compiler_params=params(8),
         cost_estimate=cost(3),
         name="own_band",
-    )(tabs, staged)
-    bulk_later, band_own, e1, e2, o1, o2 = lax.optimization_barrier((bulk, band_own, e1, e2, o1, o2))
+    )(tabs, mixr, staged)
+    bulk_later, e1, e2 = lax.optimization_barrier((bulk, e1, e2))
     bulk_e, bulk_o = paired(bulk_later, 1, False), paired(bulk_later, 1, True)
 
     forcing, top, top_half = pl.pallas_call(
@@ -366,7 +417,7 @@
         out_specs=spec(3),
         scratch_shapes=[pltpu.VMEM((20, FIELDS, TB), BF16)],
         compiler_params=params(8),
-        cost_estimate=cost(2),
+        cost_estimate=cost(20),
         name="remap",
     )(
         live_slots[0], block_source[0, 0].T, e1, o1, e2, o2, swapped, remap_weight[0, 0], mix0, gate, band_own,
@@ -380,21 +431,34 @@
         out_specs=spec(2),
         scratch_shapes=[tab, rel],
         compiler_params=params(8),
-        cost_estimate=cost(4),
+        cost_estimate=cost(1),
         name="side_band",
     )(e1, tabs, o1, top_half)
 
-    half = pltpu.VMEM((LEVELS * FIELDS, COLS + 2 * WIDE), BF16)
+    wide = (LEVELS * FIELDS, 3 * COLS)
+    narrow = (LEVELS * FIELDS, COLS + 2 * WIDE)
+    st, xa, xb = pl.pallas_call(
+        begin_kernel,
+        out_shape=[shape(narrow, F32), shape(wide, BF16), shape(wide, BF16)],
+        in_specs=spec(9),
+        out_specs=spec(3),
+        scratch_shapes=[pltpu.VMEM(wide, BF16)],
+        compiler_params=params(8),
+        cost_estimate=cost(1),
+        name="begin",
+    )(band_own, band_side, keep, mixr, bulk, bulk_e, top, top_half, top_e)
     state = pl.pallas_call(
-        diffuse_kernel,
+        finish_kernel,
         out_shape=shape((LEVELS * FIELDS, COLS), F32),
-        in_specs=spec(11),
+        in_specs=spec(12),
         out_specs=pl.BlockSpec(memory_space=pltpu.VMEM),
-        scratch_shapes=[half, half, pltpu.VMEM((LEVELS * FIELDS, COLS + 2 * WIDE), F32)],
+        scratch_shapes=[
+            pltpu.VMEM(narrow, F32), pltpu.VMEM(wide, BF16), pltpu.VMEM(wide, BF16), pltpu.VMEM(wide, BF16),
+        ],
         compiler_params=params(16),
-        cost_estimate=cost(6),
-        name="diffuse",
-    )(band_own, band_side, keep, mixr, bulk_e, bulk, bulk_o, top, top_e, top_half, top_o)
+        cost_estimate=cost(4),
+        name="finish",
+    )(band_own, band_side, keep, mixr, bulk, bulk_o, top, top_half, top_o, st, xa, xb)
     return state.reshape(1, LEVELS, FIELDS, COLS), forcing[None]
 
 

time: 49.9 us -> 45.6 us (0.914)
  waiting for transfers between devices: 9.44 us -> 5.35 us
  starting transfers between devices: 20.2 us -> 19.5 us
    ppermute x8, waiting for transfers between devices: 7.85 us -> 3.76 us  [paired(): return lax.ppermute(value, 'dom', pairs)]
    ppermute x8, starting transfers between devices: 20.1 us -> 19.5 us  [paired(): return lax.ppermute(value, 'dom', pairs)]
    pallas_call x2 -> x3, Pallas kernels: 9.19 us -> 9.67 us  [the longest x1 4.66 us: shards(): pl.pallas_call(finish_kernel, out_shape=shape((LEVELS * FIELDS, COLS), F3...]
  transfers between devices with their start and end apart: 9 -> 9, of which waited for: 3 -> 3; matrix products, arithmetic and copies ran while one was open for 0% -> 0% of each run, Pallas kernels for 17% -> 24%
where the time goes in v4:
time: 45.6 us; the launch traced here: 45.4 us
  starting transfers between devices  19.5 us (43%)
  Pallas kernels  18.8 us (41%)
  waiting for transfers between devices  5.35 us (12%)
  local copies, waits for them, and re-layouts  0.93 us (2%)
  between operations  0.77 us (2%)
    ppermute x8, starting transfers between devices, paired(): return lax.ppermute(value, 'dom', pairs)  19.5 us
    pallas_call x1, Pallas kernels, shards(): pl.pallas_call(finish_kernel, out_shape=shape((LEVELS * FIELDS, COLS), F3...  4.66 us
    pallas_call x1, Pallas kernels, shards(): pl.pallas_call(side_band_kernel, out_shape=[shape((2 * WIDE // TB, WIN, T...  3.94 us
    ppermute x8, waiting for transfers between devices, paired(): return lax.ppermute(value, 'dom', pairs)  3.76 us
    pallas_call x1, Pallas kernels, shards(): pl.pallas_call(mix_kernel, out_shape=[shape((5, 4, FIELDS, TB), BF16), sh...  3.24 us
    pallas_call x1, Pallas kernels, shards(): pl.pallas_call(own_band_kernel, out_shape=[shape((COLS // TB, WIN, TB), B...  2.64 us
    pallas_call x1, Pallas kernels, shards(): pl.pallas_call(begin_kernel, out_shape=[shape(narrow, F32), shape(wide, B...  2.37 us
    pallas_call x1, Pallas kernels, shards(): pl.pallas_call(remap_kernel, out_shape=[shape((FIELDS, COLS), F32), shape...  1.94 us
  transfers between devices with their start and end apart: 9, of which 3 were waited for; matrix products, arithmetic and copies ran while one was open for 0% of the time, Pallas kernels for 24%

profile of v4, /device:TPU:0, one launch (start us, length us, event | category | flops | bytes accessed | tf_op | source)
XLA Modules:
  0.0 45.4 jit_solution(5971785481194996518)
XLA Ops:
  0.6 3.2 %mix.1 = (bf16[5,4,16,256]{3,2,1,0:T(8,128)(2,1)}, f32[16,2048]{1,0:T(8,128)}, f32[112,2048]{1,0:T(8,128)}, bf16[16,16,256]{2,1,0:T(8,128)(2,1)}, f32[16,2048]{1,0:T(8,128)}) custom-call(f32[1,8,16,2048]{3,2,1,0:T(8,128)} %state_hbm.1, f32[7,1,2048]{2,1,0:T(1,128)} %bitcast.15, s32[5,4,256]{2,1,0:T(4,128)} %bitcast.18, s32[6,1,2048]{2,1,0:T(1,128)} %bitcast.16, ...), custom_call_target="tpu_custom_call" | custom-call | flops 3000000000 | bytes 9000000 | tf_op jit(solution)/shard_map/mix/pallas_call | solution.py:354
  3.9 0.0 copy-start
  3.9 0.1 collective-permute-start
  4.0 1.6 %collective-permute-done.swapped = bf16[5,4,16,256]{3,2,1,0:T(8,128)(2,1)S(1)} collective-permute-done((bf16[5,4,16,256]{3,2,1,0:T(8,128)(2,1)}, bf16[5,4,16,256]{3,2,1,0:T(8,128)(2,1)S(1)}, u32[]{:S(2)}, u32[]{:S(2)}) %collective-permute-start) | collective-permute-done | bytes 163872 | tf_op jit(solution)/shard_map/ppermute | solution.py:323
  5.6 0.9 %copy-done.4 = bf16[16,16,256]{2,1,0:T(8,128)(2,1)S(1)} copy-done((bf16[16,16,256]{2,1,0:T(8,128)(2,1)S(1)}, bf16[16,16,256]{2,1,0:T(8,128)(2,1)}, u32[]{:S(2)}) %copy-start.4) | copy-done | bytes 131096
  6.5 3.2 %collective-permute-start.2 = (bf16[4,16,256]{2,1,0:T(8,128)(2,1)S(1)}, bf16[4,16,256]{2,1,0:T(8,128)(2,1)S(1)}, u32[]{:S(2)}, u32[]{:S(2)}) collective-permute-start(bf16[4,16,256]{2,1,0:T(8,128)(2,1)S(1)} %get-tuple-element.32), channel_id=1, source_target_pairs={{0,2},{1,3},{2,0},{3,1},{4,6},{5,7},{6,4},{7,5},{8,10},{9,11},{10,... | collective-permute-start | bytes 98312 | tf_op jit(solution)/shard_map/ppermute | solution.py:329
  9.7 6.4 %collective-permute-start.4 = (bf16[4,16,256]{2,1,0:T(8,128)(2,1)S(1)}, bf16[4,16,256]{2,1,0:T(8,128)(2,1)S(1)}, u32[]{:S(2)}, u32[]{:S(2)}) collective-permute-start(bf16[4,16,256]{2,1,0:T(8,128)(2,1)S(1)} %get-tuple-element.36), channel_id=1, source_target_pairs={{0,62},{1,63},{2,4},{3,5},{4,2},{5,3},{6,8},{7,9},{8,6},{9,7},{10,... | collective-permute-start | bytes 98312 | tf_op jit(solution)/shard_map/ppermute | solution.py:329
  16.1 1.1 %collective-permute-start.3 = (bf16[16,16,256]{2,1,0:T(8,128)(2,1)S(1)}, bf16[16,16,256]{2,1,0:T(8,128)(2,1)S(1)}, u32[]{:S(2)}, u32[]{:S(2)}) collective-permute-start(bf16[16,16,256]{2,1,0:T(8,128)(2,1)S(1)} %get-tuple-element.34), channel_id=1, source_target_pairs={{0,63},{1,2},{2,1},{3,4},{4,3},{5,6},{6,5},{7,8},{8,7},{9,10},{10,... | collective-permute-start | bytes 393224 | tf_op jit(solution)/shard_map/ppermute | solution.py:329
  17.2 0.4 collective-permute-start.1
  17.6 0.0 copy-start.5
  17.7 0.0 copy-start.6
  17.7 2.6 %own_band.1 = (bf16[8,1280,256]{2,1,0:T(8,128)(2,1)S(1)}, bf16[112,2048]{1,0:T(8,128)(2,1)S(1)}) custom-call(bf16[16,16,256]{2,1,0:T(8,128)(2,1)S(1)} %get-tuple-element.27.tabs, f32[112,2048]{1,0:T(8,128)S(1)} %copy-done, bf16[16,16,256]{2,1,0:T(8,128)(2,1)S(1)} %get-tuple-element.29.after), custom_call_target="tpu_custom_call" | custom-call | flops 3000000000 | bytes 9000000 | tf_op jit(solution)/shard_map/own_band/pallas_call | solution.py:400
  20.3 0.0 collective-permute-done.2.e2
  20.3 1.9 %collective-permute-done.1.e1 = bf16[16,16,256]{2,1,0:T(8,128)(2,1)S(1)} collective-permute-done((bf16[16,16,256]{2,1,0:T(8,128)(2,1)S(1)}, bf16[16,16,256]{2,1,0:T(8,128)(2,1)S(1)}, u32[]{:S(2)}, u32[]{:S(2)}) %collective-permute-start.1) | collective-permute-done | bytes 131104 | tf_op jit(solution)/shard_map/ppermute | solution.py:329
  22.2 0.6 %collective-permute-start.7 = (bf16[112,2048]{1,0:T(8,128)(2,1)S(1)}, bf16[112,2048]{1,0:T(8,128)(2,1)S(1)}, u32[]{:S(2)}, u32[]{:S(2)}) collective-permute-start(bf16[112,2048]{1,0:T(8,128)(2,1)S(1)} %get-tuple-element.42.bulk), channel_id=1, source_target_pairs={{0,1},{1,0},{2,3},{3,2},{4,5},{5,4},{6,7},{7,6},{8,9},{9,8},{10,11... | collective-permute-start | bytes 1376264 | tf_op jit(solution)/shard_map/ppermute | solution.py:329
  22.9 5.7 %collective-permute-start.5 = (bf16[112,2048]{1,0:T(8,128)(2,1)S(1)}, bf16[112,2048]{1,0:T(8,128)(2,1)S(1)}, u32[]{:S(2)}, u32[]{:S(2)}) collective-permute-start(bf16[112,2048]{1,0:T(8,128)(2,1)S(1)} %get-tuple-element.42.bulk), channel_id=1, source_target_pairs={{0,63},{1,2},{2,1},{3,4},{4,3},{5,6},{6,5},{7,8},{8,7},{9,10},{10,... | collective-permute-start | bytes 1376264 | tf_op jit(solution)/shard_map/ppermute | solution.py:329
  28.6 0.0 collective-permute-done.4.o2
  28.6 0.0 collective-permute-done.3.o1
  28.6 0.0 copy-done.1
  28.6 0.0 copy-done.2
  28.6 0.0 copy-done.3
  28.6 0.0 copy-done.5
  28.6 1.9 %remap.1 = (f32[16,2048]{1,0:T(8,128)}, f32[16,2048]{1,0:T(8,128)S(1)}, bf16[16,2048]{1,0:T(8,128)(2,1)S(1)}) custom-call(s32[1,5]{1,0:T(1,128)S(1)} %bitcast.13, s32[2,8]{1,0:T(2,128)S(1)} %bitcast.12, bf16[16,16,256]{2,1,0:T(8,128)(2,1)S(1)} %collective-permute-done.1.e1, bf16[16,16,256]{2,1,0:T(8,128)(2,1)S(1)} %collective-permute-done.3.o1, ...), custom_call_target="tpu_custom_call" | custom-call | flops 20000000000 | bytes 60000000 | tf_op jit(solution)/shard_map/remap/pallas_call | solution.py:413
  30.6 0.0 collective-permute-start.8
  30.6 2.0 %collective-permute-start.6 = (bf16[16,2048]{1,0:T(8,128)(2,1)S(1)}, bf16[16,2048]{1,0:T(8,128)(2,1)S(1)}, u32[]{:S(2)}, u32[]{:S(2)}) collective-permute-start(bf16[16,2048]{1,0:T(8,128)(2,1)S(1)} %get-tuple-element.39.after.top_half), channel_id=1, source_target_pairs={{0,63},{1,2},{2,1},{3,4},{4,3},{5,6},{6,5},{7,8},{8,7},{9,10},{10,... | collective-permute-start | bytes 196616 | tf_op jit(solution)/shard_map/ppermute | solution.py:329
  32.6 3.9 %side_band.1 = (bf16[12,1280,256]{2,1,0:T(8,128)(2,1)S(1)}, f32[1,5120]{1,0:T(1,128)S(1)}) custom-call(bf16[16,16,256]{2,1,0:T(8,128)(2,1)S(1)} %collective-permute-done.1.e1, bf16[16,16,256]{2,1,0:T(8,128)(2,1)S(1)} %get-tuple-element.27.tabs, bf16[16,16,256]{2,1,0:T(8,128)(2,1)S(1)} %collective-permute-done.3.o1, ...), custom_call_target="tpu_custom_call" | custom-call | flops 1000000000 | bytes 3000000 | tf_op jit(solution)/shard_map/side_band/pallas_call | solution.py:427
  36.5 0.0 collective-permute-done.8.top_e
  36.5 0.0 collective-permute-done.7.bulk_e
  36.6 2.4 %begin.1 = (f32[128,5120]{1,0:T(8,128)S(1)}, bf16[128,6144]{1,0:T(8,128)(2,1)S(1)}, bf16[128,6144]{1,0:T(8,128)(2,1)S(1)}) custom-call(bf16[8,1280,256]{2,1,0:T(8,128)(2,1)S(1)} %get-tuple-element.30.after.band_own, bf16[12,1280,256]{2,1,0:T(8,128)(2,1)S(1)} %get-tuple-element.40.band_side, f32[1,5120]{1,0:T(1,128)S(1)} %get-tuple-element.41.keep, ...), custom_call_target="tpu_custom_call" | custom-call | flops 1000000000 | bytes 3000000 | tf_op jit(solution)/shard_map/begin/pallas_call | solution.py:440
  38.9 1.8 %collective-permute-done.6.top_o = bf16[16,2048]{1,0:T(8,128)(2,1)S(1)} collective-permute-done((bf16[16,2048]{1,0:T(8,128)(2,1)S(1)}, bf16[16,2048]{1,0:T(8,128)(2,1)S(1)}, u32[]{:S(2)}, u32[]{:S(2)}) %collective-permute-start.6) | collective-permute-done | bytes 65568 | tf_op jit(solution)/shard_map/ppermute | solution.py:329
  40.8 0.0 collective-permute-done.5.bulk_o
  40.8 4.7 %finish.1 = f32[128,2048]{1,0:T(8,128)} custom-call(bf16[8,1280,256]{2,1,0:T(8,128)(2,1)S(1)} %get-tuple-element.30.after.band_own, bf16[12,1280,256]{2,1,0:T(8,128)(2,1)S(1)} %get-tuple-element.40.band_side, f32[1,5120]{1,0:T(1,128)S(1)} %get-tuple-element.41.keep, f32[112,2048]{1,0:T(8,128)S(1)} %copy-done, bf16[112,2048]{1,0:T(8,128)(2,1)S(1)} %get-tuple-element.42.bulk, ...), custom_call_target="tpu_custom_call" | custom-call | flops 4000000000 | bytes 12000000 | tf_op jit(solution)/shard_map/finish/pallas_call | solution.py:450
  (7 shorter events, 0.0 us)
Async XLA Ops:
  3.9 13.8 %copy-start = (f32[112,2048]{1,0:T(8,128)S(1)}, f32[112,2048]{1,0:T(8,128)}, u32[]{:S(2)}) copy-start(f32[112,2048]{1,0:T(8,128)} %get-tuple-element.28.mixr) | copy-start | bytes 2752516
  3.9 1.7 %collective-permute-start = (bf16[5,4,16,256]{3,2,1,0:T(8,128)(2,1)}, bf16[5,4,16,256]{3,2,1,0:T(8,128)(2,1)S(1)}, u32[]{:S(2)}, u32[]{:S(2)}) collective-permute-start(bf16[5,4,16,256]{3,2,1,0:T(8,128)(2,1)} %get-tuple-element.25), channel_id=1, source_target_pairs={{0,64},{1,65},{2,66},{3,67},{4,68},{5,69},{6,70},{7,71},{8,72},{9,... | collective-permute-start | bytes 491528 | tf_op jit(solution)/shard_map/ppermute | solution.py:323
  5.6 0.9 %copy-start.4 = (bf16[16,16,256]{2,1,0:T(8,128)(2,1)S(1)}, bf16[16,16,256]{2,1,0:T(8,128)(2,1)}, u32[]{:S(2)}) copy-start(bf16[16,16,256]{2,1,0:T(8,128)(2,1)} %get-tuple-element.26.tabs) | copy-start | bytes 393220
  6.5 13.8 %collective-permute-start.2 = (bf16[4,16,256]{2,1,0:T(8,128)(2,1)S(1)}, bf16[4,16,256]{2,1,0:T(8,128)(2,1)S(1)}, u32[]{:S(2)}, u32[]{:S(2)}) collective-permute-start(bf16[4,16,256]{2,1,0:T(8,128)(2,1)S(1)} %get-tuple-element.32), channel_id=1, source_target_pairs={{0,2},{1,3},{2,0},{3,1},{4,6},{5,7},{6,4},{7,5},{8,10},{9,11},{10,... | collective-permute-start | bytes 98312 | tf_op jit(solution)/shard_map/ppermute | solution.py:329
  9.7 18.9 %collective-permute-start.4 = (bf16[4,16,256]{2,1,0:T(8,128)(2,1)S(1)}, bf16[4,16,256]{2,1,0:T(8,128)(2,1)S(1)}, u32[]{:S(2)}, u32[]{:S(2)}) collective-permute-start(bf16[4,16,256]{2,1,0:T(8,128)(2,1)S(1)} %get-tuple-element.36), channel_id=1, source_target_pairs={{0,62},{1,63},{2,4},{3,5},{4,2},{5,3},{6,8},{7,9},{8,6},{9,7},{10,... | collective-permute-start | bytes 98312 | tf_op jit(solution)/shard_map/ppermute | solution.py:329
  16.1 12.5 %collective-permute-start.3 = (bf16[16,16,256]{2,1,0:T(8,128)(2,1)S(1)}, bf16[16,16,256]{2,1,0:T(8,128)(2,1)S(1)}, u32[]{:S(2)}, u32[]{:S(2)}) collective-permute-start(bf16[16,16,256]{2,1,0:T(8,128)(2,1)S(1)} %get-tuple-element.34), channel_id=1, source_target_pairs={{0,63},{1,2},{2,1},{3,4},{4,3},{5,6},{6,5},{7,8},{8,7},{9,10},{10,... | collective-permute-start | bytes 393224 | tf_op jit(solution)/shard_map/ppermute | solution.py:329
  17.2 5.1 %collective-permute-start.1 = (bf16[16,16,256]{2,1,0:T(8,128)(2,1)S(1)}, bf16[16,16,256]{2,1,0:T(8,128)(2,1)S(1)}, u32[]{:S(2)}, u32[]{:S(2)}) collective-permute-start(bf16[16,16,256]{2,1,0:T(8,128)(2,1)S(1)} %get-tuple-element.29.after), channel_id=1, source_target_pairs={{0,1},{1,0},{2,3},{3,2},{4,5},{5,4},{6,7},{7,6},{8,9},{9,8},{10,11... | collective-permute-start | bytes 393224 | tf_op jit(solution)/shard_map/ppermute | solution.py:329
  17.6 11.0 %copy-start.1 = (bf16[1,1,8,2,256,256]{5,4,3,2,1,0:T(8,128)(2,1)S(1)}, bf16[1,1,8,2,256,256]{5,4,3,2,1,0:T(8,128)(2,1)}, u32[]{:S(2)}) copy-start(bf16[1,1,8,2,256,256]{5,4,3,2,1,0:T(8,128)(2,1)} %param.19) | copy-start | bytes 6291460
  17.6 11.0 %copy-start.2 = (s32[1,1,8,2]{2,3,1,0:T(2,128)S(1)}, s32[1,1,8,2]{2,3,1,0:T(2,128)}, u32[]{:S(2)}) copy-start(s32[1,1,8,2]{2,3,1,0:T(2,128)} %param.18) | copy-start | bytes 196
  17.6 11.0 %copy-start.3 = (s32[1,1,5]{2,1,0:T(1,128)S(1)}, s32[1,1,5]{2,1,0:T(1,128)}, u32[]{:S(2)}) copy-start(s32[1,1,5]{2,1,0:T(1,128)} %param.17) | copy-start | bytes 64
  17.6 11.0 %copy-start.5 = (f32[16,2048]{1,0:T(8,128)S(1)}, f32[16,2048]{1,0:T(8,128)}, u32[]{:S(2)}) copy-start(f32[16,2048]{1,0:T(8,128)} %get-tuple-element.37.mix0) | copy-start | bytes 393220
  17.7 11.0 %copy-start.6 = (f32[16,2048]{1,0:T(8,128)S(1)}, f32[16,2048]{1,0:T(8,128)}, u32[]{:S(2)}) copy-start(f32[16,2048]{1,0:T(8,128)} %get-tuple-element.38.gate) | copy-start | bytes 393220
  22.2 14.3 %collective-permute-start.7 = (bf16[112,2048]{1,0:T(8,128)(2,1)S(1)}, bf16[112,2048]{1,0:T(8,128)(2,1)S(1)}, u32[]{:S(2)}, u32[]{:S(2)}) collective-permute-start(bf16[112,2048]{1,0:T(8,128)(2,1)S(1)} %get-tuple-element.42.bulk), channel_id=1, source_target_pairs={{0,1},{1,0},{2,3},{3,2},{4,5},{5,4},{6,7},{7,6},{8,9},{9,8},{10,11... | collective-permute-start | bytes 1376264 | tf_op jit(solution)/shard_map/ppermute | solution.py:329
  22.9 17.9 %collective-permute-start.5 = (bf16[112,2048]{1,0:T(8,128)(2,1)S(1)}, bf16[112,2048]{1,0:T(8,128)(2,1)S(1)}, u32[]{:S(2)}, u32[]{:S(2)}) collective-permute-start(bf16[112,2048]{1,0:T(8,128)(2,1)S(1)} %get-tuple-element.42.bulk), channel_id=1, source_target_pairs={{0,63},{1,2},{2,1},{3,4},{4,3},{5,6},{6,5},{7,8},{8,7},{9,10},{10,... | collective-permute-start | bytes 1376264 | tf_op jit(solution)/shard_map/ppermute | solution.py:329
  30.6 6.0 %collective-permute-start.8 = (bf16[16,2048]{1,0:T(8,128)(2,1)S(1)}, bf16[16,2048]{1,0:T(8,128)(2,1)S(1)}, u32[]{:S(2)}, u32[]{:S(2)}) collective-permute-start(bf16[16,2048]{1,0:T(8,128)(2,1)S(1)} %get-tuple-element.39.after.top_half), channel_id=1, source_target_pairs={{0,1},{1,0},{2,3},{3,2},{4,5},{5,4},{6,7},{7,6},{8,9},{9,8},{10,11... | collective-permute-start | bytes 196616 | tf_op jit(solution)/shard_map/ppermute | solution.py:329
  30.6 10.2 %collective-permute-start.6 = (bf16[16,2048]{1,0:T(8,128)(2,1)S(1)}, bf16[16,2048]{1,0:T(8,128)(2,1)S(1)}, u32[]{:S(2)}, u32[]{:S(2)}) collective-permute-start(bf16[16,2048]{1,0:T(8,128)(2,1)S(1)} %get-tuple-element.39.after.top_half), channel_id=1, source_target_pairs={{0,63},{1,2},{2,1},{3,4},{4,3},{5,6},{6,5},{7,8},{8,7},{9,10},{10,... | collective-permute-start | bytes 196616 | tf_op jit(solution)/shard_map/ppermute | solution.py:329

commit v5 on v4

--- a/solution.py
+++ b/solution.py
@@ -105,13 +105,16 @@
     return (d & 1) == 0, (d & 2) == 0
 
 
-def stage_kernel(swapped, tabs, e1, o1, e2, o2, kept):
+def hold_kernel(tabs, kept):
+    kept[...] = tabs[...]
+
+
+def stage_kernel(swapped, tabs, e1, o1, e2, o2):
     near, far = parities()
     e1[0:4] = swapped[jnp.where(near, 3, 1)]
     e1[4:PAY] = tabs[pl.ds(jnp.where(near, 2 * COLS // TB - (PAY - 4), 0), PAY - 4)]
     o1[0:4] = swapped[jnp.where(near, 1, 3)]
     o1[4:PAY] = tabs[pl.ds(jnp.where(near, 0, 2 * COLS // TB - (PAY - 4)), PAY - 4)]
-    kept[...] = tabs[...]
     e2[...] = swapped[jnp.where(far, 4, 0)]
     o2[...] = swapped[jnp.where(far, 0, 4)]
 
@@ -269,7 +272,8 @@
 
 
 def finish_kernel(
-    band_own, band_side, keep, mixr, bulk, bulk_o, top, top_half, top_o, st_in, xa_in, xb_in, out, st, xa, xb, x0,
+    band_own, band_side, keep, mixr, bulk, bulk_o, top, top_half, top_o, st_in, xa_in, xb_in, out, st, xa, xb, x0, result,
+    sems,
 ):
     x0[0:FIELDS, COLS : 2 * COLS] = top_half[...]
     x0[FIELDS:, COLS : 2 * COLS] = bulk[...]
@@ -306,7 +310,9 @@
 
             def new(b, value):
                 if step == NSUB:
-                    out[:, (b - EDGE) * TB : (b - EDGE + 1) * TB] = value
+                    mine = slice((b - EDGE) * TB, (b - EDGE + 1) * TB)
+                    result[:, mine] = value
+                    pltpu.make_async_copy(result.at[:, mine], out.at[:, mine], sems.at[b - EDGE]).start()
                 else:
                     st[:, b * TB : (b + 1) * TB] = value
                     dst[:, RIM + b * TB : RIM + (b + 1) * TB] = value.astype(BF16)
@@ -315,6 +321,9 @@
             part(blocks_of(own, side, not right), src, bands, keep, old, new)
 
     per_order(run)
+    for n in range(OWN):
+        mine = slice(n * TB, (n + 1) * TB)
+        pltpu.make_async_copy(result.at[:, mine], out.at[:, mine], sems.at[n]).wait()
 
 
 def crossed(value):
@@ -381,13 +390,22 @@
     )
     swapped = crossed(packed)
 
+    tabs = pl.pallas_call(
+        hold_kernel,
+        out_shape=shape(tabs.shape, BF16),
+        in_specs=spec(1),
+        out_specs=spec(1)[0],
+        compiler_params=params(4),
+        cost_estimate=cost(1),
+        name="hold",
+    )(tabs)
     pair = shape((4, FIELDS, TB), BF16)
     payload = shape((PAY, 16, TB), BF16)
-    e1, o1, e2, o2, tabs = pl.pallas_call(
+    e1, o1, e2, o2 = pl.pallas_call(
         stage_kernel,
-        out_shape=[payload, payload, pair, pair, shape(tabs.shape, BF16)],
+        out_shape=[payload, payload, pair, pair],
         in_specs=spec(2),
-        out_specs=spec(5),
+        out_specs=spec(4),
         compiler_params=params(4),
         cost_estimate=cost(1),
         name="stage",
@@ -407,7 +425,7 @@
         cost_estimate=cost(3),
         name="own_band",
     )(tabs, mixr, staged)
-    bulk_later, e1, e2 = lax.optimization_barrier((bulk, e1, e2))
+    bulk_later, e2 = lax.optimization_barrier((bulk, e2))
     bulk_e, bulk_o = paired(bulk_later, 1, False), paired(bulk_later, 1, True)
 
     forcing, top, top_half = pl.pallas_call(
@@ -451,9 +469,10 @@
         finish_kernel,
         out_shape=shape((LEVELS * FIELDS, COLS), F32),
         in_specs=spec(12),
-        out_specs=pl.BlockSpec(memory_space=pltpu.VMEM),
+        out_specs=ANYWHERE,
         scratch_shapes=[
             pltpu.VMEM(narrow, F32), pltpu.VMEM(wide, BF16), pltpu.VMEM(wide, BF16), pltpu.VMEM(wide, BF16),
+            pltpu.VMEM((LEVELS * FIELDS, COLS), F32), pltpu.SemaphoreType.DMA((OWN,)),
         ],
         compiler_params=params(16),
         cost_estimate=cost(4),

time: 45.6 us -> 44 us (0.965)
  waiting for transfers between devices: 5.35 us -> 2.98 us
  starting transfers between devices: 19.5 us -> 20.3 us
    ppermute x8, waiting for transfers between devices: 3.76 us -> 2.32 us  [paired(): return lax.ppermute(value, 'dom', pairs)]
    ppermute x1, waiting for transfers between devices: 1.59 us -> 0.66 us  [crossed(): return lax.ppermute(value, ('comp', 'dom'), pairs)]
    ppermute x8, starting transfers between devices: 19.5 us -> 20.2 us  [paired(): return lax.ppermute(value, 'dom', pairs)]
  transfers between devices with their start and end apart: 9 -> 9, of which waited for: 3 -> 2; matrix products, arithmetic and copies ran while one was open for 0% -> 0% of each run, Pallas kernels for 24% -> 25%
where the time goes in v5:
time: 44 us; the launch traced here: 43.8 us
  starting transfers between devices  20.3 us (46%)
  Pallas kernels  18.7 us (42%)
  waiting for transfers between devices  2.98 us (7%)
  between operations  0.95 us (2%)
  local copies, waits for them, and re-layouts  0.93 us (2%)
    ppermute x8, starting transfers between devices, paired(): return lax.ppermute(value, 'dom', pairs)  20.2 us
    pallas_call x1, Pallas kernels, shards(): pl.pallas_call(finish_kernel, out_shape=shape((LEVELS * FIELDS, COLS), F3...  4.49 us
    pallas_call x1, Pallas kernels, shards(): pl.pallas_call(side_band_kernel, out_shape=[shape((2 * WIDE // TB, WIN, T...  3.94 us
    pallas_call x1, Pallas kernels, shards(): pl.pallas_call(mix_kernel, out_shape=[shape((5, 4, FIELDS, TB), BF16), sh...  3.24 us
    pallas_call x1, Pallas kernels, shards(): pl.pallas_call(own_band_kernel, out_shape=[shape((COLS // TB, WIN, TB), B...  2.64 us
    pallas_call x1, Pallas kernels, shards(): pl.pallas_call(begin_kernel, out_shape=[shape(narrow, F32), shape(wide, B...  2.37 us
    ppermute x8, waiting for transfers between devices, paired(): return lax.ppermute(value, 'dom', pairs)  2.32 us
    pallas_call x1, Pallas kernels, shards(): pl.pallas_call(remap_kernel, out_shape=[shape((FIELDS, COLS), F32), shape...  1.95 us
  transfers between devices with their start and end apart: 9, of which 2 were waited for; matrix products, arithmetic and copies ran while one was open for 0% of the time, Pallas kernels for 25%

profile of v5, /device:TPU:0, one launch (start us, length us, event | category | flops | bytes accessed | tf_op | source)
XLA Modules:
  0.0 43.8 jit_solution(17851972035024401107)
XLA Ops:
  0.6 3.2 %mix.1 = (bf16[5,4,16,256]{3,2,1,0:T(8,128)(2,1)}, f32[16,2048]{1,0:T(8,128)}, f32[112,2048]{1,0:T(8,128)}, bf16[16,16,256]{2,1,0:T(8,128)(2,1)}, f32[16,2048]{1,0:T(8,128)}) custom-call(f32[1,8,16,2048]{3,2,1,0:T(8,128)} %state_hbm.1, f32[7,1,2048]{2,1,0:T(1,128)} %bitcast.15, s32[5,4,256]{2,1,0:T(4,128)} %bitcast.18, s32[6,1,2048]{2,1,0:T(1,128)} %bitcast.16, ...), custom_call_target="tpu_custom_call" | custom-call | flops 3000000000 | bytes 9000000 | tf_op jit(solution)/shard_map/mix/pallas_call | solution.py:363
  3.9 0.1 collective-permute-start
  4.0 0.0 copy-start.4
  4.0 0.9 %copy-done.4 = bf16[16,16,256]{2,1,0:T(8,128)(2,1)S(1)} copy-done((bf16[16,16,256]{2,1,0:T(8,128)(2,1)S(1)}, bf16[16,16,256]{2,1,0:T(8,128)(2,1)}, u32[]{:S(2)}) %copy-start.4) | copy-done | bytes 131096
  4.9 0.0 copy-start
  4.9 0.7 %collective-permute-done.swapped = bf16[5,4,16,256]{3,2,1,0:T(8,128)(2,1)S(1)} collective-permute-done((bf16[5,4,16,256]{3,2,1,0:T(8,128)(2,1)}, bf16[5,4,16,256]{3,2,1,0:T(8,128)(2,1)S(1)}, u32[]{:S(2)}, u32[]{:S(2)}) %collective-permute-start) | collective-permute-done | bytes 163872 | tf_op jit(solution)/shard_map/ppermute | solution.py:332
  5.6 3.2 %collective-permute-start.3 = (bf16[4,16,256]{2,1,0:T(8,128)(2,1)S(1)}, bf16[4,16,256]{2,1,0:T(8,128)(2,1)S(1)}, u32[]{:S(2)}, u32[]{:S(2)}) collective-permute-start(bf16[4,16,256]{2,1,0:T(8,128)(2,1)S(1)} %get-tuple-element.30), channel_id=1, source_target_pairs={{0,2},{1,3},{2,0},{3,1},{4,6},{5,7},{6,4},{7,5},{8,10},{9,11},{10,... | collective-permute-start | bytes 98312 | tf_op jit(solution)/shard_map/ppermute | solution.py:338
  8.8 6.4 %collective-permute-start.4 = (bf16[4,16,256]{2,1,0:T(8,128)(2,1)S(1)}, bf16[4,16,256]{2,1,0:T(8,128)(2,1)S(1)}, u32[]{:S(2)}, u32[]{:S(2)}) collective-permute-start(bf16[4,16,256]{2,1,0:T(8,128)(2,1)S(1)} %get-tuple-element.32), channel_id=1, source_target_pairs={{0,62},{1,63},{2,4},{3,5},{4,2},{5,3},{6,8},{7,9},{8,6},{9,7},{10,... | collective-permute-start | bytes 98312 | tf_op jit(solution)/shard_map/ppermute | solution.py:338
  15.2 1.1 %collective-permute-start.2 = (bf16[16,16,256]{2,1,0:T(8,128)(2,1)S(1)}, bf16[16,16,256]{2,1,0:T(8,128)(2,1)S(1)}, u32[]{:S(2)}, u32[]{:S(2)}) collective-permute-start(bf16[16,16,256]{2,1,0:T(8,128)(2,1)S(1)} %get-tuple-element.28), channel_id=1, source_target_pairs={{0,63},{1,2},{2,1},{3,4},{4,3},{5,6},{6,5},{7,8},{8,7},{9,10},{10,... | collective-permute-start | bytes 393224 | tf_op jit(solution)/shard_map/ppermute | solution.py:338
  16.3 0.4 %collective-permute-start.1 = (bf16[16,16,256]{2,1,0:T(8,128)(2,1)S(1)}, bf16[16,16,256]{2,1,0:T(8,128)(2,1)S(1)}, u32[]{:S(2)}, u32[]{:S(2)}) collective-permute-start(bf16[16,16,256]{2,1,0:T(8,128)(2,1)S(1)} %get-tuple-element.26.after), channel_id=1, source_target_pairs={{0,1},{1,0},{2,3},{3,2},{4,5},{5,4},{6,7},{7,6},{8,9},{9,8},{10,11... | collective-permute-start | bytes 393224 | tf_op jit(solution)/shard_map/ppermute | solution.py:338
  16.7 0.0 copy-done
  16.7 0.0 copy-start.5
  16.7 0.0 copy-start.6
  16.7 2.6 %own_band.1 = (bf16[8,1280,256]{2,1,0:T(8,128)(2,1)S(1)}, bf16[112,2048]{1,0:T(8,128)(2,1)S(1)}) custom-call(bf16[16,16,256]{2,1,0:T(8,128)(2,1)S(1)} %hold.1.tabs, f32[112,2048]{1,0:T(8,128)S(1)} %copy-done, bf16[16,16,256]{2,1,0:T(8,128)(2,1)S(1)} %get-tuple-element.26.after), custom_call_target="tpu_custom_call" | custom-call | flops 3000000000 | bytes 9000000 | tf_op jit(solution)/shard_map/own_band/pallas_call | solution.py:418
  19.4 0.0 collective-permute-done.3.e2
  19.4 1.7 %collective-permute-start.7 = (bf16[112,2048]{1,0:T(8,128)(2,1)S(1)}, bf16[112,2048]{1,0:T(8,128)(2,1)S(1)}, u32[]{:S(2)}, u32[]{:S(2)}) collective-permute-start(bf16[112,2048]{1,0:T(8,128)(2,1)S(1)} %get-tuple-element.38.bulk), channel_id=1, source_target_pairs={{0,1},{1,0},{2,3},{3,2},{4,5},{5,4},{6,7},{7,6},{8,9},{9,8},{10,11... | collective-permute-start | bytes 1376264 | tf_op jit(solution)/shard_map/ppermute | solution.py:338
  21.1 6.4 %collective-permute-start.5 = (bf16[112,2048]{1,0:T(8,128)(2,1)S(1)}, bf16[112,2048]{1,0:T(8,128)(2,1)S(1)}, u32[]{:S(2)}, u32[]{:S(2)}) collective-permute-start(bf16[112,2048]{1,0:T(8,128)(2,1)S(1)} %get-tuple-element.38.bulk), channel_id=1, source_target_pairs={{0,63},{1,2},{2,1},{3,4},{4,3},{5,6},{6,5},{7,8},{8,7},{9,10},{10,... | collective-permute-start | bytes 1376264 | tf_op jit(solution)/shard_map/ppermute | solution.py:338
  27.5 0.0 collective-permute-done.4.o2
  27.5 0.0 collective-permute-done.2.o1
  27.5 0.0 collective-permute-done.1.e1
  27.5 0.0 copy-done.1
  27.5 0.0 copy-done.2
  27.5 1.9 %remap.1 = (f32[16,2048]{1,0:T(8,128)}, f32[16,2048]{1,0:T(8,128)S(1)}, bf16[16,2048]{1,0:T(8,128)(2,1)S(1)}) custom-call(s32[1,5]{1,0:T(1,128)S(1)} %bitcast.13, s32[2,8]{1,0:T(2,128)S(1)} %bitcast.12, bf16[16,16,256]{2,1,0:T(8,128)(2,1)S(1)} %collective-permute-done.1.e1, bf16[16,16,256]{2,1,0:T(8,128)(2,1)S(1)} %collective-permute-done.2.o1, ...), custom_call_target="tpu_custom_call" | custom-call | flops 20000000000 | bytes 60000000 | tf_op jit(solution)/shard_map/remap/pallas_call | solution.py:431
  29.5 0.0 collective-permute-start.8
  29.5 1.1 %collective-permute-start.6 = (bf16[16,2048]{1,0:T(8,128)(2,1)S(1)}, bf16[16,2048]{1,0:T(8,128)(2,1)S(1)}, u32[]{:S(2)}, u32[]{:S(2)}) collective-permute-start(bf16[16,2048]{1,0:T(8,128)(2,1)S(1)} %get-tuple-element.35.after.top_half), channel_id=1, source_target_pairs={{0,63},{1,2},{2,1},{3,4},{4,3},{5,6},{6,5},{7,8},{8,7},{9,10},{10,... | collective-permute-start | bytes 196616 | tf_op jit(solution)/shard_map/ppermute | solution.py:338
  30.5 3.9 %side_band.1 = (bf16[12,1280,256]{2,1,0:T(8,128)(2,1)S(1)}, f32[1,5120]{1,0:T(1,128)S(1)}) custom-call(bf16[16,16,256]{2,1,0:T(8,128)(2,1)S(1)} %collective-permute-done.1.e1, bf16[16,16,256]{2,1,0:T(8,128)(2,1)S(1)} %hold.1.tabs, bf16[16,16,256]{2,1,0:T(8,128)(2,1)S(1)} %collective-permute-done.2.o1, bf16[16,2048]{1,0:T(8,128)(2,1)S(1)} %get-tuple-element.35.after.top_half), custom_call_target="tpu_custom_call" | custom-call | flops 1000000000 | bytes 3000000 | tf_op jit(solution)/shard_map/side_band/pallas_call | solution.py:445
  34.5 0.0 collective-permute-done.8.top_e
  34.5 0.0 collective-permute-done.7.bulk_e
  34.5 2.4 %begin.1 = (f32[128,5120]{1,0:T(8,128)S(1)}, bf16[128,6144]{1,0:T(8,128)(2,1)S(1)}, bf16[128,6144]{1,0:T(8,128)(2,1)S(1)}) custom-call(bf16[8,1280,256]{2,1,0:T(8,128)(2,1)S(1)} %get-tuple-element.27.after.band_own, bf16[12,1280,256]{2,1,0:T(8,128)(2,1)S(1)} %get-tuple-element.36.band_side, f32[1,5120]{1,0:T(1,128)S(1)} %get-tuple-element.37.keep, ...), custom_call_target="tpu_custom_call" | custom-call | flops 1000000000 | bytes 3000000 | tf_op jit(solution)/shard_map/begin/pallas_call | solution.py:458
  36.9 2.3 %collective-permute-done.6.top_o = bf16[16,2048]{1,0:T(8,128)(2,1)S(1)} collective-permute-done((bf16[16,2048]{1,0:T(8,128)(2,1)S(1)}, bf16[16,2048]{1,0:T(8,128)(2,1)S(1)}, u32[]{:S(2)}, u32[]{:S(2)}) %collective-permute-start.6) | collective-permute-done | bytes 65568 | tf_op jit(solution)/shard_map/ppermute | solution.py:338
  39.2 0.0 collective-permute-done.5.bulk_o
  39.2 4.5 %finish.1 = f32[128,2048]{1,0:T(8,128)} custom-call(bf16[8,1280,256]{2,1,0:T(8,128)(2,1)S(1)} %get-tuple-element.27.after.band_own, bf16[12,1280,256]{2,1,0:T(8,128)(2,1)S(1)} %get-tuple-element.36.band_side, f32[1,5120]{1,0:T(1,128)S(1)} %get-tuple-element.37.keep, f32[112,2048]{1,0:T(8,128)S(1)} %copy-done, bf16[112,2048]{1,0:T(8,128)(2,1)S(1)} %get-tuple-element.38.bulk, ...), custom_call_target="tpu_custom_call" | custom-call | flops 4000000000 | bytes 12000000 | tf_op jit(solution)/shard_map/finish/pallas_call | solution.py:468
  (8 shorter events, 0.0 us)
Async XLA Ops:
  3.9 1.7 %collective-permute-start = (bf16[5,4,16,256]{3,2,1,0:T(8,128)(2,1)}, bf16[5,4,16,256]{3,2,1,0:T(8,128)(2,1)S(1)}, u32[]{:S(2)}, u32[]{:S(2)}) collective-permute-start(bf16[5,4,16,256]{3,2,1,0:T(8,128)(2,1)} %get-tuple-element.25), channel_id=1, source_target_pairs={{0,64},{1,65},{2,66},{3,67},{4,68},{5,69},{6,70},{7,71},{8,72},{9,... | collective-permute-start | bytes 491528 | tf_op jit(solution)/shard_map/ppermute | solution.py:332
  4.0 0.9 %copy-start.4 = (bf16[16,16,256]{2,1,0:T(8,128)(2,1)S(1)}, bf16[16,16,256]{2,1,0:T(8,128)(2,1)}, u32[]{:S(2)}) copy-start(bf16[16,16,256]{2,1,0:T(8,128)(2,1)} %get-tuple-element.23.tabs) | copy-start | bytes 393220
  4.9 11.8 %copy-start = (f32[112,2048]{1,0:T(8,128)S(1)}, f32[112,2048]{1,0:T(8,128)}, u32[]{:S(2)}) copy-start(f32[112,2048]{1,0:T(8,128)} %get-tuple-element.24.mixr) | copy-start | bytes 2752516
  5.6 13.8 %collective-permute-start.3 = (bf16[4,16,256]{2,1,0:T(8,128)(2,1)S(1)}, bf16[4,16,256]{2,1,0:T(8,128)(2,1)S(1)}, u32[]{:S(2)}, u32[]{:S(2)}) collective-permute-start(bf16[4,16,256]{2,1,0:T(8,128)(2,1)S(1)} %get-tuple-element.30), channel_id=1, source_target_pairs={{0,2},{1,3},{2,0},{3,1},{4,6},{5,7},{6,4},{7,5},{8,10},{9,11},{10,... | collective-permute-start | bytes 98312 | tf_op jit(solution)/shard_map/ppermute | solution.py:338
  8.8 18.7 %collective-permute-start.4 = (bf16[4,16,256]{2,1,0:T(8,128)(2,1)S(1)}, bf16[4,16,256]{2,1,0:T(8,128)(2,1)S(1)}, u32[]{:S(2)}, u32[]{:S(2)}) collective-permute-start(bf16[4,16,256]{2,1,0:T(8,128)(2,1)S(1)} %get-tuple-element.32), channel_id=1, source_target_pairs={{0,62},{1,63},{2,4},{3,5},{4,2},{5,3},{6,8},{7,9},{8,6},{9,7},{10,... | collective-permute-start | bytes 98312 | tf_op jit(solution)/shard_map/ppermute | solution.py:338
  15.2 12.3 %collective-permute-start.2 = (bf16[16,16,256]{2,1,0:T(8,128)(2,1)S(1)}, bf16[16,16,256]{2,1,0:T(8,128)(2,1)S(1)}, u32[]{:S(2)}, u32[]{:S(2)}) collective-permute-start(bf16[16,16,256]{2,1,0:T(8,128)(2,1)S(1)} %get-tuple-element.28), channel_id=1, source_target_pairs={{0,63},{1,2},{2,1},{3,4},{4,3},{5,6},{6,5},{7,8},{8,7},{9,10},{10,... | collective-permute-start | bytes 393224 | tf_op jit(solution)/shard_map/ppermute | solution.py:338
  16.3 11.2 %collective-permute-start.1 = (bf16[16,16,256]{2,1,0:T(8,128)(2,1)S(1)}, bf16[16,16,256]{2,1,0:T(8,128)(2,1)S(1)}, u32[]{:S(2)}, u32[]{:S(2)}) collective-permute-start(bf16[16,16,256]{2,1,0:T(8,128)(2,1)S(1)} %get-tuple-element.26.after), channel_id=1, source_target_pairs={{0,1},{1,0},{2,3},{3,2},{4,5},{5,4},{6,7},{7,6},{8,9},{9,8},{10,11... | collective-permute-start | bytes 393224 | tf_op jit(solution)/shard_map/ppermute | solution.py:338
  16.7 10.8 %copy-start.1 = (bf16[1,1,8,2,256,256]{5,4,3,2,1,0:T(8,128)(2,1)S(1)}, bf16[1,1,8,2,256,256]{5,4,3,2,1,0:T(8,128)(2,1)}, u32[]{:S(2)}) copy-start(bf16[1,1,8,2,256,256]{5,4,3,2,1,0:T(8,128)(2,1)} %param.19) | copy-start | bytes 6291460
  16.7 10.8 %copy-start.2 = (s32[1,1,8,2]{2,3,1,0:T(2,128)S(1)}, s32[1,1,8,2]{2,3,1,0:T(2,128)}, u32[]{:S(2)}) copy-start(s32[1,1,8,2]{2,3,1,0:T(2,128)} %param.18) | copy-start | bytes 196
  16.7 10.8 %copy-start.3 = (s32[1,1,5]{2,1,0:T(1,128)S(1)}, s32[1,1,5]{2,1,0:T(1,128)}, u32[]{:S(2)}) copy-start(s32[1,1,5]{2,1,0:T(1,128)} %param.17) | copy-start | bytes 64
  16.7 10.8 %copy-start.5 = (f32[16,2048]{1,0:T(8,128)S(1)}, f32[16,2048]{1,0:T(8,128)}, u32[]{:S(2)}) copy-start(f32[16,2048]{1,0:T(8,128)} %get-tuple-element.33.mix0) | copy-start | bytes 393220
  16.7 10.8 %copy-start.6 = (f32[16,2048]{1,0:T(8,128)S(1)}, f32[16,2048]{1,0:T(8,128)}, u32[]{:S(2)}) copy-start(f32[16,2048]{1,0:T(8,128)} %get-tuple-element.34.gate) | copy-start | bytes 393220
  19.4 15.1 %collective-permute-start.7 = (bf16[112,2048]{1,0:T(8,128)(2,1)S(1)}, bf16[112,2048]{1,0:T(8,128)(2,1)S(1)}, u32[]{:S(2)}, u32[]{:S(2)}) collective-permute-start(bf16[112,2048]{1,0:T(8,128)(2,1)S(1)} %get-tuple-element.38.bulk), channel_id=1, source_target_pairs={{0,1},{1,0},{2,3},{3,2},{4,5},{5,4},{6,7},{7,6},{8,9},{9,8},{10,11... | collective-permute-start | bytes 1376264 | tf_op jit(solution)/shard_map/ppermute | solution.py:338
  21.1 18.1 %collective-permute-start.5 = (bf16[112,2048]{1,0:T(8,128)(2,1)S(1)}, bf16[112,2048]{1,0:T(8,128)(2,1)S(1)}, u32[]{:S(2)}, u32[]{:S(2)}) collective-permute-start(bf16[112,2048]{1,0:T(8,128)(2,1)S(1)} %get-tuple-element.38.bulk), channel_id=1, source_target_pairs={{0,63},{1,2},{2,1},{3,4},{4,3},{5,6},{6,5},{7,8},{8,7},{9,10},{10,... | collective-permute-start | bytes 1376264 | tf_op jit(solution)/shard_map/ppermute | solution.py:338
  29.5 5.0 %collective-permute-start.8 = (bf16[16,2048]{1,0:T(8,128)(2,1)S(1)}, bf16[16,2048]{1,0:T(8,128)(2,1)S(1)}, u32[]{:S(2)}, u32[]{:S(2)}) collective-permute-start(bf16[16,2048]{1,0:T(8,128)(2,1)S(1)} %get-tuple-element.35.after.top_half), channel_id=1, source_target_pairs={{0,1},{1,0},{2,3},{3,2},{4,5},{5,4},{6,7},{7,6},{8,9},{9,8},{10,11... | collective-permute-start | bytes 196616 | tf_op jit(solution)/shard_map/ppermute | solution.py:338
  29.5 9.7 %collective-permute-start.6 = (bf16[16,2048]{1,0:T(8,128)(2,1)S(1)}, bf16[16,2048]{1,0:T(8,128)(2,1)S(1)}, u32[]{:S(2)}, u32[]{:S(2)}) collective-permute-start(bf16[16,2048]{1,0:T(8,128)(2,1)S(1)} %get-tuple-element.35.after.top_half), channel_id=1, source_target_pairs={{0,63},{1,2},{2,1},{3,4},{4,3},{5,6},{6,5},{7,8},{8,7},{9,10},{10,... | collective-permute-start | bytes 196616 | tf_op jit(solution)/shard_map/ppermute | solution.py:338

commit v6 on v5

--- a/solution.py
+++ b/solution.py
@@ -20,7 +20,7 @@
 
 
 def mix_kernel(
-    state_hbm, rate_hbm, send_hbm, offs_hbm, coef_hbm, mask_hbm, couple_hbm, packed, mix0, mixr, tabs, gate,
+    state_hbm, rate_hbm, send_hbm, offs_hbm, coef_hbm, mask_hbm, couple_hbm, packed, mix0, mixr, sent, tabs, gate,
     state, rate, send, offs, coef, mask, couple, sems,
 ):
     pairs = (
@@ -78,6 +78,7 @@
             else:
                 new = mid - flux
             mixr[(l - 1) * FIELDS : l * FIELDS, here] = new
+            sent[(l - 1) * FIELDS : l * FIELDS, here] = new.astype(BF16)
         lane = lax.broadcasted_iota(jnp.int32, (1, TB), 1) + RIM
         off = [offs[j, :, here] for j in range(6)]
         val = [coef[j, :, here] for j in range(6)]
@@ -360,17 +361,18 @@
 ):
     shape = jax.ShapeDtypeStruct
     rate = vert_rate.transpose(1, 0, 2)
-    packed, mix0, mixr, tabs, gate = pl.pallas_call(
+    packed, mix0, mixr, sent, tabs, gate = pl.pallas_call(
         mix_kernel,
         out_shape=[
             shape((5, 4, FIELDS, TB), BF16),
             shape((FIELDS, COLS), F32),
             shape((REST, COLS), F32),
+            shape((REST, COLS), BF16),
             shape((2 * COLS // TB, 16, TB), BF16),
             shape((FIELDS, COLS), F32),
         ],
         in_specs=[pl.BlockSpec(memory_space=pltpu.HBM)] * 7,
-        out_specs=spec(5),
+        out_specs=spec(6),
         scratch_shapes=[
             pltpu.VMEM((LEVELS, FIELDS, COLS), F32),
             pltpu.VMEM((LEVELS - 1, 1, COLS), F32),
@@ -413,6 +415,9 @@
     staged = e1
     e1, e2, o1, o2 = paired(e1, 1, False), paired(e2, 2, False), paired(o1, 1, True), paired(o2, 2, True)
 
+    bulk_later, e2 = lax.optimization_barrier((sent, e2))
+    bulk_e, bulk_o = paired(bulk_later, 1, False), paired(bulk_later, 1, True)
+
     tab = pltpu.VMEM((16, TB), F32)
     rel = pltpu.VMEM((16 * (WIN // LANE), LANE), F32)
     band_own, bulk = pl.pallas_call(
@@ -424,9 +429,7 @@
         compiler_params=params(8),
         cost_estimate=cost(3),
         name="own_band",
-    )(tabs, mixr, staged)
-    bulk_later, e2 = lax.optimization_barrier((bulk, e2))
-    bulk_e, bulk_o = paired(bulk_later, 1, False), paired(bulk_later, 1, True)
+    )(tabs, mixr, e1)
 
     forcing, top, top_half = pl.pallas_call(
         remap_kernel,

time: 44 us -> 45.1 us (1.025)
  waiting for transfers between devices: 2.98 us -> 5.26 us
  starting transfers between devices: 20.3 us -> 19.1 us
    ppermute x8, waiting for transfers between devices: 2.32 us -> 4.61 us  [paired(): return lax.ppermute(value, 'dom', pairs)]
    ppermute x8, starting transfers between devices: 20.2 us -> 19 us  [paired(): return lax.ppermute(value, 'dom', pairs)]
    unnamed x14 -> x16, local copies, waits for them, and re-layouts: 0.93 us -> 0.93 us
  transfers between devices with their start and end apart: 9 -> 9, of which waited for: 2 -> 3; matrix products, arithmetic and copies ran while one was open for 0% -> 0% of each run, Pallas kernels for 25% -> 24%
where the time goes in v6:
time: 45.1 us; the launch traced here: 44.9 us
  starting transfers between devices  19.1 us (42%)
  Pallas kernels  18.7 us (41%)
  waiting for transfers between devices  5.26 us (12%)
  between operations  0.94 us (2%)
  local copies, waits for them, and re-layouts  0.93 us (2%)
    ppermute x8, starting transfers between devices, paired(): return lax.ppermute(value, 'dom', pairs)  19 us
    ppermute x8, waiting for transfers between devices, paired(): return lax.ppermute(value, 'dom', pairs)  4.61 us
    pallas_call x1, Pallas kernels, shards(): pl.pallas_call(finish_kernel, out_shape=shape((LEVELS * FIELDS, COLS), F3...  4.49 us
    pallas_call x1, Pallas kernels, shards(): pl.pallas_call(side_band_kernel, out_shape=[shape((2 * WIDE // TB, WIN, T...  3.94 us
    pallas_call x1, Pallas kernels, shards(): pl.pallas_call(mix_kernel, out_shape=[shape((5, 4, FIELDS, TB), BF16), sh...  3.27 us
    pallas_call x1, Pallas kernels, shards(): pl.pallas_call(own_band_kernel, out_shape=[shape((COLS // TB, WIN, TB), B...  2.64 us
    pallas_call x1, Pallas kernels, shards(): pl.pallas_call(begin_kernel, out_shape=[shape(narrow, F32), shape(wide, B...  2.37 us
    pallas_call x1, Pallas kernels, shards(): pl.pallas_call(remap_kernel, out_shape=[shape((FIELDS, COLS), F32), shape...  1.96 us
  transfers between devices with their start and end apart: 9, of which 3 were waited for; matrix products, arithmetic and copies ran while one was open for 0% of the time, Pallas kernels for 24%

profile of v6, /device:TPU:0, one launch (start us, length us, event | category | flops | bytes accessed | tf_op | source)
XLA Modules:
  0.0 44.9 jit_solution(2498427687409036681)
XLA Ops:
  0.6 3.3 %mix.1 = (bf16[5,4,16,256]{3,2,1,0:T(8,128)(2,1)}, f32[16,2048]{1,0:T(8,128)}, f32[112,2048]{1,0:T(8,128)}, bf16[112,2048]{1,0:T(8,128)(2,1)}, bf16[16,16,256]{2,1,0:T(8,128)(2,1)}, /*index=5*/f32[16,2048]{1,0:T(8,128)}) custom-call(f32[1,8,16,2048]{3,2,1,0:T(8,128)} %state_hbm.1, f32[7,1,2048]{2,1,0:T(1,128)} %bitcast.15, s32[5,4,256]{2,1,0:T(4,128)} %bitcast.18, ...), custom_call_target="tpu_custom_call" | custom-call | flops 3000000000 | bytes 9000000 | tf_op jit(solution)/shard_map/mix/pallas_call | solution.py:364
  3.9 0.1 collective-permute-start
  4.0 0.0 copy-start.4
  4.0 0.9 %copy-done.4 = bf16[16,16,256]{2,1,0:T(8,128)(2,1)S(1)} copy-done((bf16[16,16,256]{2,1,0:T(8,128)(2,1)S(1)}, bf16[16,16,256]{2,1,0:T(8,128)(2,1)}, u32[]{:S(2)}) %copy-start.4) | copy-done | bytes 131096
  4.9 0.0 copy-start.7
  4.9 0.0 copy-start
  4.9 0.7 %collective-permute-done.swapped = bf16[5,4,16,256]{3,2,1,0:T(8,128)(2,1)S(1)} collective-permute-done((bf16[5,4,16,256]{3,2,1,0:T(8,128)(2,1)}, bf16[5,4,16,256]{3,2,1,0:T(8,128)(2,1)S(1)}, u32[]{:S(2)}, u32[]{:S(2)}) %collective-permute-start) | collective-permute-done | bytes 163872 | tf_op jit(solution)/shard_map/ppermute | solution.py:333
  5.6 1.7 %collective-permute-start.1 = (bf16[16,16,256]{2,1,0:T(8,128)(2,1)S(1)}, bf16[16,16,256]{2,1,0:T(8,128)(2,1)S(1)}, u32[]{:S(2)}, u32[]{:S(2)}) collective-permute-start(bf16[16,16,256]{2,1,0:T(8,128)(2,1)S(1)} %get-tuple-element.27), channel_id=1, source_target_pairs={{0,1},{1,0},{2,3},{3,2},{4,5},{5,4},{6,7},{7,6},{8,9},{9,8},{10,11... | collective-permute-start | bytes 393224 | tf_op jit(solution)/shard_map/ppermute | solution.py:339
  7.3 2.7 %collective-permute-start.3 = (bf16[4,16,256]{2,1,0:T(8,128)(2,1)S(1)}, bf16[4,16,256]{2,1,0:T(8,128)(2,1)S(1)}, u32[]{:S(2)}, u32[]{:S(2)}) collective-permute-start(bf16[4,16,256]{2,1,0:T(8,128)(2,1)S(1)} %get-tuple-element.31), channel_id=1, source_target_pairs={{0,2},{1,3},{2,0},{3,1},{4,6},{5,7},{6,4},{7,5},{8,10},{9,11},{10,... | collective-permute-start | bytes 98312 | tf_op jit(solution)/shard_map/ppermute | solution.py:339
  10.0 6.7 %collective-permute-start.4 = (bf16[4,16,256]{2,1,0:T(8,128)(2,1)S(1)}, bf16[4,16,256]{2,1,0:T(8,128)(2,1)S(1)}, u32[]{:S(2)}, u32[]{:S(2)}) collective-permute-start(bf16[4,16,256]{2,1,0:T(8,128)(2,1)S(1)} %get-tuple-element.33), channel_id=1, source_target_pairs={{0,62},{1,63},{2,4},{3,5},{4,2},{5,3},{6,8},{7,9},{8,6},{9,7},{10,... | collective-permute-start | bytes 98312 | tf_op jit(solution)/shard_map/ppermute | solution.py:339
  16.7 0.4 collective-permute-start.2
  17.1 0.0 collective-permute-done.3.e2
  17.1 0.0 copy-done.7
  17.1 0.2 collective-permute-start.7
  17.4 6.9 %collective-permute-start.5 = (bf16[112,2048]{1,0:T(8,128)(2,1)S(1)}, bf16[112,2048]{1,0:T(8,128)(2,1)S(1)}, u32[]{:S(2)}, u32[]{:S(2)}) collective-permute-start(bf16[112,2048]{1,0:T(8,128)(2,1)S(1)} %copy-done.7), channel_id=1, source_target_pairs={{0,63},{1,2},{2,1},{3,4},{4,3},{5,6},{6,5},{7,8},{8,7},{9,10},{10,... | collective-permute-start | bytes 1376264 | tf_op jit(solution)/shard_map/ppermute | solution.py:339
  24.3 0.0 collective-permute-done.1.after.e1
  24.3 0.0 copy-done
  24.3 0.0 copy-start.3
  24.3 0.0 copy-start.5
  24.3 2.6 %own_band.1 = (bf16[8,1280,256]{2,1,0:T(8,128)(2,1)S(1)}, bf16[112,2048]{1,0:T(8,128)(2,1)S(1)}) custom-call(bf16[16,16,256]{2,1,0:T(8,128)(2,1)S(1)} %hold.1.tabs, f32[112,2048]{1,0:T(8,128)S(1)} %copy-done, bf16[16,16,256]{2,1,0:T(8,128)(2,1)S(1)} %collective-permute-done.1.after.e1), custom_call_target="tpu_custom_call" | custom-call | flops 3000000000 | bytes 9000000 | tf_op jit(solution)/shard_map/own_band/pallas_call | solution.py:423
  27.0 0.0 collective-permute-done.4.o2
  27.0 1.6 %collective-permute-done.2.o1 = bf16[16,16,256]{2,1,0:T(8,128)(2,1)S(1)} collective-permute-done((bf16[16,16,256]{2,1,0:T(8,128)(2,1)S(1)}, bf16[16,16,256]{2,1,0:T(8,128)(2,1)S(1)}, u32[]{:S(2)}, u32[]{:S(2)}) %collective-permute-start.2) | collective-permute-done | bytes 131104 | tf_op jit(solution)/shard_map/ppermute | solution.py:339
  28.6 2.0 %remap.1 = (f32[16,2048]{1,0:T(8,128)}, f32[16,2048]{1,0:T(8,128)S(1)}, bf16[16,2048]{1,0:T(8,128)(2,1)S(1)}) custom-call(s32[1,5]{1,0:T(1,128)S(1)} %bitcast.13, s32[2,8]{1,0:T(2,128)S(1)} %bitcast.12, bf16[16,16,256]{2,1,0:T(8,128)(2,1)S(1)} %collective-permute-done.1.after.e1, bf16[16,16,256]{2,1,0:T(8,128)(2,1)S(1)} %collective-permute-done.2.o1, ...), custom_call_target="tpu_custom_call" | custom-call | flops 20000000000 | bytes 60000000 | tf_op jit(solution)/shard_map/remap/pallas_call | solution.py:434
  30.6 0.0 collective-permute-start.8
  30.6 0.4 collective-permute-start.6
  31.0 3.9 %side_band.1 = (bf16[12,1280,256]{2,1,0:T(8,128)(2,1)S(1)}, f32[1,5120]{1,0:T(1,128)S(1)}) custom-call(bf16[16,16,256]{2,1,0:T(8,128)(2,1)S(1)} %collective-permute-done.1.after.e1, bf16[16,16,256]{2,1,0:T(8,128)(2,1)S(1)} %hold.1.tabs, bf16[16,16,256]{2,1,0:T(8,128)(2,1)S(1)} %collective-permute-done.2.o1, bf16[16,2048]{1,0:T(8,128)(2,1)S(1)} %get-tuple-element.36.after.top_half), custom_call_target="tpu_custom_call" | custom-call | flops 1000000000 | bytes 3000000 | tf_op jit(solution)/shard_map/side_band/pallas_call | solution.py:448
  34.9 0.0 collective-permute-done.8.top_e
  34.9 0.0 collective-permute-done.7.bulk_e
  34.9 2.4 %begin.1 = (f32[128,5120]{1,0:T(8,128)S(1)}, bf16[128,6144]{1,0:T(8,128)(2,1)S(1)}, bf16[128,6144]{1,0:T(8,128)(2,1)S(1)}) custom-call(bf16[8,1280,256]{2,1,0:T(8,128)(2,1)S(1)} %get-tuple-element.28.after.band_own, bf16[12,1280,256]{2,1,0:T(8,128)(2,1)S(1)} %get-tuple-element.37.band_side, f32[1,5120]{1,0:T(1,128)S(1)} %get-tuple-element.38.keep, ...), custom_call_target="tpu_custom_call" | custom-call | flops 1000000000 | bytes 3000000 | tf_op jit(solution)/shard_map/begin/pallas_call | solution.py:461
  37.3 3.0 %collective-permute-done.6.top_o = bf16[16,2048]{1,0:T(8,128)(2,1)S(1)} collective-permute-done((bf16[16,2048]{1,0:T(8,128)(2,1)S(1)}, bf16[16,2048]{1,0:T(8,128)(2,1)S(1)}, u32[]{:S(2)}, u32[]{:S(2)}) %collective-permute-start.6) | collective-permute-done | bytes 65568 | tf_op jit(solution)/shard_map/ppermute | solution.py:339
  40.3 0.0 collective-permute-done.5.bulk_o
  40.3 4.5 %finish.1 = f32[128,2048]{1,0:T(8,128)} custom-call(bf16[8,1280,256]{2,1,0:T(8,128)(2,1)S(1)} %get-tuple-element.28.after.band_own, bf16[12,1280,256]{2,1,0:T(8,128)(2,1)S(1)} %get-tuple-element.37.band_side, f32[1,5120]{1,0:T(1,128)S(1)} %get-tuple-element.38.keep, f32[112,2048]{1,0:T(8,128)S(1)} %copy-done, bf16[112,2048]{1,0:T(8,128)(2,1)S(1)} %get-tuple-element.39.bulk, ...), custom_call_target="tpu_custom_call" | custom-call | flops 4000000000 | bytes 12000000 | tf_op jit(solution)/shard_map/finish/pallas_call | solution.py:471
  (10 shorter events, 0.0 us)
Async XLA Ops:
  3.9 1.7 %collective-permute-start = (bf16[5,4,16,256]{3,2,1,0:T(8,128)(2,1)}, bf16[5,4,16,256]{3,2,1,0:T(8,128)(2,1)S(1)}, u32[]{:S(2)}, u32[]{:S(2)}) collective-permute-start(bf16[5,4,16,256]{3,2,1,0:T(8,128)(2,1)} %get-tuple-element.26), channel_id=1, source_target_pairs={{0,64},{1,65},{2,66},{3,67},{4,68},{5,69},{6,70},{7,71},{8,72},{9,... | collective-permute-start | bytes 491528 | tf_op jit(solution)/shard_map/ppermute | solution.py:333
  4.0 0.9 %copy-start.4 = (bf16[16,16,256]{2,1,0:T(8,128)(2,1)S(1)}, bf16[16,16,256]{2,1,0:T(8,128)(2,1)}, u32[]{:S(2)}) copy-start(bf16[16,16,256]{2,1,0:T(8,128)(2,1)} %get-tuple-element.24.tabs) | copy-start | bytes 393220
  4.9 12.2 %copy-start.7 = (bf16[112,2048]{1,0:T(8,128)(2,1)S(1)}, bf16[112,2048]{1,0:T(8,128)(2,1)}, u32[]{:S(2)}) copy-start(bf16[112,2048]{1,0:T(8,128)(2,1)} %get-tuple-element.40) | copy-start | bytes 1376260
  4.9 19.4 %copy-start = (f32[112,2048]{1,0:T(8,128)S(1)}, f32[112,2048]{1,0:T(8,128)}, u32[]{:S(2)}) copy-start(f32[112,2048]{1,0:T(8,128)} %get-tuple-element.25.mixr) | copy-start | bytes 2752516
  5.6 18.7 %collective-permute-start.1 = (bf16[16,16,256]{2,1,0:T(8,128)(2,1)S(1)}, bf16[16,16,256]{2,1,0:T(8,128)(2,1)S(1)}, u32[]{:S(2)}, u32[]{:S(2)}) collective-permute-start(bf16[16,16,256]{2,1,0:T(8,128)(2,1)S(1)} %get-tuple-element.27), channel_id=1, source_target_pairs={{0,1},{1,0},{2,3},{3,2},{4,5},{5,4},{6,7},{7,6},{8,9},{9,8},{10,11... | collective-permute-start | bytes 393224 | tf_op jit(solution)/shard_map/ppermute | solution.py:339
  7.3 9.8 %collective-permute-start.3 = (bf16[4,16,256]{2,1,0:T(8,128)(2,1)S(1)}, bf16[4,16,256]{2,1,0:T(8,128)(2,1)S(1)}, u32[]{:S(2)}, u32[]{:S(2)}) collective-permute-start(bf16[4,16,256]{2,1,0:T(8,128)(2,1)S(1)} %get-tuple-element.31), channel_id=1, source_target_pairs={{0,2},{1,3},{2,0},{3,1},{4,6},{5,7},{6,4},{7,5},{8,10},{9,11},{10,... | collective-permute-start | bytes 98312 | tf_op jit(solution)/shard_map/ppermute | solution.py:339
  10.0 17.0 %collective-permute-start.4 = (bf16[4,16,256]{2,1,0:T(8,128)(2,1)S(1)}, bf16[4,16,256]{2,1,0:T(8,128)(2,1)S(1)}, u32[]{:S(2)}, u32[]{:S(2)}) collective-permute-start(bf16[4,16,256]{2,1,0:T(8,128)(2,1)S(1)} %get-tuple-element.33), channel_id=1, source_target_pairs={{0,62},{1,63},{2,4},{3,5},{4,2},{5,3},{6,8},{7,9},{8,6},{9,7},{10,... | collective-permute-start | bytes 98312 | tf_op jit(solution)/shard_map/ppermute | solution.py:339
  16.7 11.9 %collective-permute-start.2 = (bf16[16,16,256]{2,1,0:T(8,128)(2,1)S(1)}, bf16[16,16,256]{2,1,0:T(8,128)(2,1)S(1)}, u32[]{:S(2)}, u32[]{:S(2)}) collective-permute-start(bf16[16,16,256]{2,1,0:T(8,128)(2,1)S(1)} %get-tuple-element.29), channel_id=1, source_target_pairs={{0,63},{1,2},{2,1},{3,4},{4,3},{5,6},{6,5},{7,8},{8,7},{9,10},{10,... | collective-permute-start | bytes 393224 | tf_op jit(solution)/shard_map/ppermute | solution.py:339
  17.1 17.8 %collective-permute-start.7 = (bf16[112,2048]{1,0:T(8,128)(2,1)S(1)}, bf16[112,2048]{1,0:T(8,128)(2,1)S(1)}, u32[]{:S(2)}, u32[]{:S(2)}) collective-permute-start(bf16[112,2048]{1,0:T(8,128)(2,1)S(1)} %copy-done.7), channel_id=1, source_target_pairs={{0,1},{1,0},{2,3},{3,2},{4,5},{5,4},{6,7},{7,6},{8,9},{9,8},{10,11... | collective-permute-start | bytes 1376264 | tf_op jit(solution)/shard_map/ppermute | solution.py:339
  17.4 22.9 %collective-permute-start.5 = (bf16[112,2048]{1,0:T(8,128)(2,1)S(1)}, bf16[112,2048]{1,0:T(8,128)(2,1)S(1)}, u32[]{:S(2)}, u32[]{:S(2)}) collective-permute-start(bf16[112,2048]{1,0:T(8,128)(2,1)S(1)} %copy-done.7), channel_id=1, source_target_pairs={{0,63},{1,2},{2,1},{3,4},{4,3},{5,6},{6,5},{7,8},{8,7},{9,10},{10,... | collective-permute-start | bytes 1376264 | tf_op jit(solution)/shard_map/ppermute | solution.py:339
  24.3 4.3 %copy-start.1 = (bf16[1,1,8,2,256,256]{5,4,3,2,1,0:T(8,128)(2,1)S(1)}, bf16[1,1,8,2,256,256]{5,4,3,2,1,0:T(8,128)(2,1)}, u32[]{:S(2)}) copy-start(bf16[1,1,8,2,256,256]{5,4,3,2,1,0:T(8,128)(2,1)} %param.19) | copy-start | bytes 6291460
  24.3 4.3 %copy-start.2 = (s32[1,1,8,2]{2,3,1,0:T(2,128)S(1)}, s32[1,1,8,2]{2,3,1,0:T(2,128)}, u32[]{:S(2)}) copy-start(s32[1,1,8,2]{2,3,1,0:T(2,128)} %param.18) | copy-start | bytes 196
  24.3 4.3 %copy-start.3 = (s32[1,1,5]{2,1,0:T(1,128)S(1)}, s32[1,1,5]{2,1,0:T(1,128)}, u32[]{:S(2)}) copy-start(s32[1,1,5]{2,1,0:T(1,128)} %param.17) | copy-start | bytes 64
  24.3 4.3 %copy-start.5 = (f32[16,2048]{1,0:T(8,128)S(1)}, f32[16,2048]{1,0:T(8,128)}, u32[]{:S(2)}) copy-start(f32[16,2048]{1,0:T(8,128)} %get-tuple-element.34.mix0) | copy-start | bytes 393220
  24.3 4.3 %copy-start.6 = (f32[16,2048]{1,0:T(8,128)S(1)}, f32[16,2048]{1,0:T(8,128)}, u32[]{:S(2)}) copy-start(f32[16,2048]{1,0:T(8,128)} %get-tuple-element.35.gate) | copy-start | bytes 393220
  30.6 4.3 %collective-permute-start.8 = (bf16[16,2048]{1,0:T(8,128)(2,1)S(1)}, bf16[16,2048]{1,0:T(8,128)(2,1)S(1)}, u32[]{:S(2)}, u32[]{:S(2)}) collective-permute-start(bf16[16,2048]{1,0:T(8,128)(2,1)S(1)} %get-tuple-element.36.after.top_half), channel_id=1, source_target_pairs={{0,1},{1,0},{2,3},{3,2},{4,5},{5,4},{6,7},{7,6},{8,9},{9,8},{10,11... | collective-permute-start | bytes 196616 | tf_op jit(solution)/shard_map/ppermute | solution.py:339
  30.6 9.7 %collective-permute-start.6 = (bf16[16,2048]{1,0:T(8,128)(2,1)S(1)}, bf16[16,2048]{1,0:T(8,128)(2,1)S(1)}, u32[]{:S(2)}, u32[]{:S(2)}) collective-permute-start(bf16[16,2048]{1,0:T(8,128)(2,1)S(1)} %get-tuple-element.36.after.top_half), channel_id=1, source_target_pairs={{0,63},{1,2},{2,1},{3,4},{4,3},{5,6},{6,5},{7,8},{8,7},{9,10},{10,... | collective-permute-start | bytes 196616 | tf_op jit(solution)/shard_map/ppermute | solution.py:339

commit v7 on v5

--- a/solution.py
+++ b/solution.py
@@ -16,6 +16,7 @@
 REST = (LEVELS - 1) * FIELDS
 WIDE = COLS - RIM
 PICK_MIB = 63
+EARLY = 4
 PAY = 4 + 2 * WIDE // TB
 
 
@@ -156,10 +157,10 @@
     del after
     for c in range(0, COLS, TB):
         bulk[:, c : c + TB] = mixr[:, c : c + TB].astype(BF16)
-    build_bands(tab, rel, band, 0, COLS // TB, tabs, 0)
-
-
-def side_band_kernel(e1, tabs, o1, after, band, keep, tab, rel):
+    build_bands(tab, rel, band, 0, EARLY, tabs, 0)
+
+
+def side_band_kernel(e1, tabs, o1, after, band, late, keep, tab, rel):
     del after
     near, _ = parities()
     side = WIDE // TB
@@ -176,6 +177,7 @@
             keep[:, pl.ds(at, TB)] = 1.0 - jnp.sum(coefs, axis=0, keepdims=True)
     build_bands(tab, rel, band, 0, side, e1, 4)
     build_bands(tab, rel, band, side, side, o1, 4)
+    build_bands(tab, rel, late, 0, COLS // TB - EARLY, tabs, 2 * EARLY)
 
 
 def remap_kernel(live, source, e1, o1, e2, o2, swapped, weights, mix0, gate, after, forcing, top, top_half, got):
@@ -223,6 +225,10 @@
     return [(EDGE + n, ("own", n)) for n in own] + [((EDGE + OWN if on_right else 0) + n, ("side", n)) for n in side]
 
 
+def own_band(early, late, n):
+    return early[n] if n < EARLY else late[n - EARLY]
+
+
 def per_order(run):
     near, _ = parities()
 
@@ -235,7 +241,7 @@
         run(False)
 
 
-def begin_kernel(band_own, band_side, keep, mixr, bulk, bulk_e, top, top_half, top_e, st, xa, xb, x0):
+def begin_kernel(band_own, band_late, band_side, keep, mixr, bulk, bulk_e, top, top_half, top_e, st, xa, xb, x0):
     x0[0:FIELDS, COLS : 2 * COLS] = top_half[...]
     x0[FIELDS:, COLS : 2 * COLS] = bulk[...]
 
@@ -245,7 +251,7 @@
         x0[FIELDS:, there] = bulk_e[...]
 
         def bands(band):
-            return band_own[band[1]] if band[0] == "own" else band_side[band[1]]
+            return own_band(band_own, band_late, band[1]) if band[0] == "own" else band_side[band[1]]
 
         for step in range(1, NSUB):
             count = OWN - 2 * step
@@ -272,7 +278,7 @@
 
 
 def finish_kernel(
-    band_own, band_side, keep, mixr, bulk, bulk_o, top, top_half, top_o, st_in, xa_in, xb_in, out, st, xa, xb, x0, result,
+    band_own, band_late, band_side, keep, mixr, bulk, bulk_o, top, top_half, top_o, st_in, xa_in, xb_in, out, st, xa, xb, x0, result,
     sems,
 ):
     x0[0:FIELDS, COLS : 2 * COLS] = top_half[...]
@@ -284,7 +290,7 @@
         x0[FIELDS:, there] = bulk_o[...]
 
         def bands(band):
-            return band_own[band[1]] if band[0] == "own" else band_side[EDGE + band[1]]
+            return own_band(band_own, band_late, band[1]) if band[0] == "own" else band_side[EDGE + band[1]]
 
         for step in range(1, NSUB):
             first = EDGE + (2 * step if right else OWN - 2 * step - 4)
@@ -417,7 +423,7 @@
     rel = pltpu.VMEM((16 * (WIN // LANE), LANE), F32)
     band_own, bulk = pl.pallas_call(
         own_band_kernel,
-        out_shape=[shape((COLS // TB, WIN, TB), BF16), shape((REST, COLS), BF16)],
+        out_shape=[shape((EARLY, WIN, TB), BF16), shape((REST, COLS), BF16)],
         in_specs=spec(2) + [ANYWHERE],
         out_specs=spec(2),
         scratch_shapes=[tab, rel],
@@ -442,11 +448,11 @@
     )
     top_e, top_o = paired(top_half, 1, False), paired(top_half, 1, True)
 
-    band_side, keep = pl.pallas_call(
+    band_side, band_late, keep = pl.pallas_call(
         side_band_kernel,
-        out_shape=[shape((2 * WIDE // TB, WIN, TB), BF16), shape((1, COLS + 2 * WIDE), F32)],
+        out_shape=[shape((2 * WIDE // TB, WIN, TB), BF16), shape((OWN - EARLY, WIN, TB), BF16), shape((1, COLS + 2 * WIDE), F32)],
         in_specs=spec(3) + [ANYWHERE],
-        out_specs=spec(2),
+        out_specs=spec(3),
         scratch_shapes=[tab, rel],
         compiler_params=params(8),
         cost_estimate=cost(1),
@@ -458,17 +464,17 @@
     st, xa, xb = pl.pallas_call(
         begin_kernel,
         out_shape=[shape(narrow, F32), shape(wide, BF16), shape(wide, BF16)],
-        in_specs=spec(9),
+        in_specs=spec(10),
         out_specs=spec(3),
         scratch_shapes=[pltpu.VMEM(wide, BF16)],
         compiler_params=params(8),
         cost_estimate=cost(1),
         name="begin",
-    )(band_own, band_side, keep, mixr, bulk, bulk_e, top, top_half, top_e)
+    )(band_own, band_late, band_side, keep, mixr, bulk, bulk_e, top, top_half, top_e)
     state = pl.pallas_call(
         finish_kernel,
         out_shape=shape((LEVELS * FIELDS, COLS), F32),
-        in_specs=spec(12),
+        in_specs=spec(13),
         out_specs=ANYWHERE,
         scratch_shapes=[
             pltpu.VMEM(narrow, F32), pltpu.VMEM(wide, BF16), pltpu.VMEM(wide, BF16), pltpu.VMEM(wide, BF16),
@@ -477,7 +483,7 @@
         compiler_params=params(16),
         cost_estimate=cost(4),
         name="finish",
-    )(band_own, band_side, keep, mixr, bulk, bulk_o, top, top_half, top_o, st, xa, xb)
+    )(band_own, band_late, band_side, keep, mixr, bulk, bulk_o, top, top_half, top_o, st, xa, xb)
     return state.reshape(1, LEVELS, FIELDS, COLS), forcing[None]
 
 

time: 44 us -> 43.5 us (0.989)
  waiting for transfers between devices: 2.98 us -> 0.68 us
  starting transfers between devices: 20.3 us -> 22.1 us
    ppermute x8, waiting for transfers between devices: 2.32 us -> 0.02 us  [paired(): return lax.ppermute(value, 'dom', pairs)]
    ppermute x8, starting transfers between devices: 20.2 us -> 22 us  [paired(): return lax.ppermute(value, 'dom', pairs)]
    pallas_call x1, Pallas kernels: 2.64 us -> 1.34 us  [shards(): pl.pallas_call(own_band_kernel, out_shape=[shape((EARLY, WIN, TB), BF16),...]
    pallas_call x1, Pallas kernels: 3.94 us -> 5.23 us  [shards(): pl.pallas_call(side_band_kernel, out_shape=[shape((2 * WIDE // TB, WIN, T...]
  transfers between devices with their start and end apart: 9 -> 9, of which waited for: 2 -> 1; matrix products, arithmetic and copies ran while one was open for 0% -> 0% of each run, Pallas kernels for 25% -> 25%
where the time goes in v7:
time: 43.5 us; the launch traced here: 43.3 us
  starting transfers between devices  22.1 us (51%)
  Pallas kernels  18.7 us (43%)
  between operations  0.96 us (2%)
  local copies, waits for them, and re-layouts  0.93 us (2%)
  waiting for transfers between devices  0.68 us (2%)
    ppermute x8, starting transfers between devices, paired(): return lax.ppermute(value, 'dom', pairs)  22 us
    pallas_call x1, Pallas kernels, shards(): pl.pallas_call(side_band_kernel, out_shape=[shape((2 * WIDE // TB, WIN, T...  5.23 us
    pallas_call x1, Pallas kernels, shards(): pl.pallas_call(finish_kernel, out_shape=shape((LEVELS * FIELDS, COLS), F3...  4.48 us
    pallas_call x1, Pallas kernels, shards(): pl.pallas_call(mix_kernel, out_shape=[shape((5, 4, FIELDS, TB), BF16), sh...  3.24 us
    pallas_call x1, Pallas kernels, shards(): pl.pallas_call(begin_kernel, out_shape=[shape(narrow, F32), shape(wide, B...  2.37 us
    pallas_call x1, Pallas kernels, shards(): pl.pallas_call(remap_kernel, out_shape=[shape((FIELDS, COLS), F32), shape...  1.96 us
    pallas_call x1, Pallas kernels, shards(): pl.pallas_call(own_band_kernel, out_shape=[shape((EARLY, WIN, TB), BF16),...  1.34 us
    unnamed x14, local copies, waits for them, and re-layouts  0.93 us
  transfers between devices with their start and end apart: 9, of which 1 were waited for; matrix products, arithmetic and copies ran while one was open for 0% of the time, Pallas kernels for 25%

profile of v7, /device:TPU:0, one launch (start us, length us, event | category | flops | bytes accessed | tf_op | source)
XLA Modules:
  0.0 43.3 jit_solution(5536842749596444893)
XLA Ops:
  0.6 3.2 %mix.1 = (bf16[5,4,16,256]{3,2,1,0:T(8,128)(2,1)}, f32[16,2048]{1,0:T(8,128)}, f32[112,2048]{1,0:T(8,128)}, bf16[16,16,256]{2,1,0:T(8,128)(2,1)}, f32[16,2048]{1,0:T(8,128)}) custom-call(f32[1,8,16,2048]{3,2,1,0:T(8,128)} %state_hbm.1, f32[7,1,2048]{2,1,0:T(1,128)} %bitcast.15, s32[5,4,256]{2,1,0:T(4,128)} %bitcast.18, s32[6,1,2048]{2,1,0:T(1,128)} %bitcast.16, ...), custom_call_target="tpu_custom_call" | custom-call | flops 3000000000 | bytes 9000000 | tf_op jit(solution)/shard_map/mix/pallas_call | solution.py:369
  3.9 0.1 collective-permute-start
  4.0 0.0 copy-start.4
  4.0 0.9 %copy-done.4 = bf16[16,16,256]{2,1,0:T(8,128)(2,1)S(1)} copy-done((bf16[16,16,256]{2,1,0:T(8,128)(2,1)S(1)}, bf16[16,16,256]{2,1,0:T(8,128)(2,1)}, u32[]{:S(2)}) %copy-start.4) | copy-done | bytes 131096
  4.9 0.0 copy-start
  4.9 0.7 %collective-permute-done.swapped = bf16[5,4,16,256]{3,2,1,0:T(8,128)(2,1)S(1)} collective-permute-done((bf16[5,4,16,256]{3,2,1,0:T(8,128)(2,1)}, bf16[5,4,16,256]{3,2,1,0:T(8,128)(2,1)S(1)}, u32[]{:S(2)}, u32[]{:S(2)}) %collective-permute-start) | collective-permute-done | bytes 163872 | tf_op jit(solution)/shard_map/ppermute | solution.py:338
  5.6 3.2 %collective-permute-start.3 = (bf16[4,16,256]{2,1,0:T(8,128)(2,1)S(1)}, bf16[4,16,256]{2,1,0:T(8,128)(2,1)S(1)}, u32[]{:S(2)}, u32[]{:S(2)}) collective-permute-start(bf16[4,16,256]{2,1,0:T(8,128)(2,1)S(1)} %get-tuple-element.31), channel_id=1, source_target_pairs={{0,2},{1,3},{2,0},{3,1},{4,6},{5,7},{6,4},{7,5},{8,10},{9,11},{10,... | collective-permute-start | bytes 98312 | tf_op jit(solution)/shard_map/ppermute | solution.py:344
  8.8 6.4 %collective-permute-start.4 = (bf16[4,16,256]{2,1,0:T(8,128)(2,1)S(1)}, bf16[4,16,256]{2,1,0:T(8,128)(2,1)S(1)}, u32[]{:S(2)}, u32[]{:S(2)}) collective-permute-start(bf16[4,16,256]{2,1,0:T(8,128)(2,1)S(1)} %get-tuple-element.33), channel_id=1, source_target_pairs={{0,62},{1,63},{2,4},{3,5},{4,2},{5,3},{6,8},{7,9},{8,6},{9,7},{10,... | collective-permute-start | bytes 98312 | tf_op jit(solution)/shard_map/ppermute | solution.py:344
  15.2 1.1 %collective-permute-start.2 = (bf16[16,16,256]{2,1,0:T(8,128)(2,1)S(1)}, bf16[16,16,256]{2,1,0:T(8,128)(2,1)S(1)}, u32[]{:S(2)}, u32[]{:S(2)}) collective-permute-start(bf16[16,16,256]{2,1,0:T(8,128)(2,1)S(1)} %get-tuple-element.29), channel_id=1, source_target_pairs={{0,63},{1,2},{2,1},{3,4},{4,3},{5,6},{6,5},{7,8},{8,7},{9,10},{10,... | collective-permute-start | bytes 393224 | tf_op jit(solution)/shard_map/ppermute | solution.py:344
  16.3 0.4 %collective-permute-start.1 = (bf16[16,16,256]{2,1,0:T(8,128)(2,1)S(1)}, bf16[16,16,256]{2,1,0:T(8,128)(2,1)S(1)}, u32[]{:S(2)}, u32[]{:S(2)}) collective-permute-start(bf16[16,16,256]{2,1,0:T(8,128)(2,1)S(1)} %get-tuple-element.27.after), channel_id=1, source_target_pairs={{0,1},{1,0},{2,3},{3,2},{4,5},{5,4},{6,7},{7,6},{8,9},{9,8},{10,11... | collective-permute-start | bytes 393224 | tf_op jit(solution)/shard_map/ppermute | solution.py:344
  16.7 0.0 copy-done
  16.7 0.0 copy-start.5
  16.7 0.0 copy-start.6
  16.7 1.3 %own_band.1 = (bf16[4,1280,256]{2,1,0:T(8,128)(2,1)S(1)}, bf16[112,2048]{1,0:T(8,128)(2,1)S(1)}) custom-call(bf16[16,16,256]{2,1,0:T(8,128)(2,1)S(1)} %hold.1.tabs, f32[112,2048]{1,0:T(8,128)S(1)} %copy-done, bf16[16,16,256]{2,1,0:T(8,128)(2,1)S(1)} %get-tuple-element.27.after), custom_call_target="tpu_custom_call" | custom-call | flops 3000000000 | bytes 9000000 | tf_op jit(solution)/shard_map/own_band/pallas_call | solution.py:424
  18.1 0.0 collective-permute-done.3.e2
  18.1 1.7 %collective-permute-start.7 = (bf16[112,2048]{1,0:T(8,128)(2,1)S(1)}, bf16[112,2048]{1,0:T(8,128)(2,1)S(1)}, u32[]{:S(2)}, u32[]{:S(2)}) collective-permute-start(bf16[112,2048]{1,0:T(8,128)(2,1)S(1)} %get-tuple-element.40.bulk), channel_id=1, source_target_pairs={{0,1},{1,0},{2,3},{3,2},{4,5},{5,4},{6,7},{7,6},{8,9},{9,8},{10,11... | collective-permute-start | bytes 1376264 | tf_op jit(solution)/shard_map/ppermute | solution.py:344
  19.8 6.4 %collective-permute-start.5 = (bf16[112,2048]{1,0:T(8,128)(2,1)S(1)}, bf16[112,2048]{1,0:T(8,128)(2,1)S(1)}, u32[]{:S(2)}, u32[]{:S(2)}) collective-permute-start(bf16[112,2048]{1,0:T(8,128)(2,1)S(1)} %get-tuple-element.40.bulk), channel_id=1, source_target_pairs={{0,63},{1,2},{2,1},{3,4},{4,3},{5,6},{6,5},{7,8},{8,7},{9,10},{10,... | collective-permute-start | bytes 1376264 | tf_op jit(solution)/shard_map/ppermute | solution.py:344
  26.2 0.0 collective-permute-done.4.o2
  26.2 0.0 collective-permute-done.2.o1
  26.2 0.0 collective-permute-done.1.e1
  26.2 0.0 copy-done.1
  26.2 0.0 copy-done.2
  26.2 2.0 %remap.1 = (f32[16,2048]{1,0:T(8,128)}, f32[16,2048]{1,0:T(8,128)S(1)}, bf16[16,2048]{1,0:T(8,128)(2,1)S(1)}) custom-call(s32[1,5]{1,0:T(1,128)S(1)} %bitcast.13, s32[2,8]{1,0:T(2,128)S(1)} %bitcast.12, bf16[16,16,256]{2,1,0:T(8,128)(2,1)S(1)} %collective-permute-done.1.e1, bf16[16,16,256]{2,1,0:T(8,128)(2,1)S(1)} %collective-permute-done.2.o1, ...), custom_call_target="tpu_custom_call" | custom-call | flops 20000000000 | bytes 60000000 | tf_op jit(solution)/shard_map/remap/pallas_call | solution.py:437
  28.2 0.0 collective-permute-start.8
  28.2 2.8 %collective-permute-start.6 = (bf16[16,2048]{1,0:T(8,128)(2,1)S(1)}, bf16[16,2048]{1,0:T(8,128)(2,1)S(1)}, u32[]{:S(2)}, u32[]{:S(2)}) collective-permute-start(bf16[16,2048]{1,0:T(8,128)(2,1)S(1)} %get-tuple-element.36.after.top_half), channel_id=1, source_target_pairs={{0,63},{1,2},{2,1},{3,4},{4,3},{5,6},{6,5},{7,8},{8,7},{9,10},{10,... | collective-permute-start | bytes 196616 | tf_op jit(solution)/shard_map/ppermute | solution.py:344
  31.0 5.2 %side_band.1 = (bf16[12,1280,256]{2,1,0:T(8,128)(2,1)S(1)}, bf16[4,1280,256]{2,1,0:T(8,128)(2,1)S(1)}, f32[1,5120]{1,0:T(1,128)S(1)}) custom-call(bf16[16,16,256]{2,1,0:T(8,128)(2,1)S(1)} %collective-permute-done.1.e1, bf16[16,16,256]{2,1,0:T(8,128)(2,1)S(1)} %hold.1.tabs, bf16[16,16,256]{2,1,0:T(8,128)(2,1)S(1)} %collective-permute-done.2.o1, ...), custom_call_target="tpu_custom_call" | custom-call | flops 1000000000 | bytes 3000000 | tf_op jit(solution)/shard_map/side_band/pallas_call | solution.py:451
  36.3 0.0 collective-permute-done.8.top_e
  36.3 0.0 collective-permute-done.7.bulk_e
  36.3 2.4 %begin.1 = (f32[128,5120]{1,0:T(8,128)S(1)}, bf16[128,6144]{1,0:T(8,128)(2,1)S(1)}, bf16[128,6144]{1,0:T(8,128)(2,1)S(1)}) custom-call(bf16[4,1280,256]{2,1,0:T(8,128)(2,1)S(1)} %get-tuple-element.28.after.band_own, bf16[4,1280,256]{2,1,0:T(8,128)(2,1)S(1)} %get-tuple-element.37.band_late, bf16[12,1280,256]{2,1,0:T(8,128)(2,1)S(1)} %get-tuple-element.38.band_side, ...), custom_call_target="tpu_custom_call" | custom-call | flops 1000000000 | bytes 3000000 | tf_op jit(solution)/shard_map/begin/pallas_call | solution.py:464
  38.7 0.0 collective-permute-done.6.top_o
  38.7 0.0 collective-permute-done.5.bulk_o
  38.7 4.5 %finish.1 = f32[128,2048]{1,0:T(8,128)} custom-call(bf16[4,1280,256]{2,1,0:T(8,128)(2,1)S(1)} %get-tuple-element.28.after.band_own, bf16[4,1280,256]{2,1,0:T(8,128)(2,1)S(1)} %get-tuple-element.37.band_late, bf16[12,1280,256]{2,1,0:T(8,128)(2,1)S(1)} %get-tuple-element.38.band_side, f32[1,5120]{1,0:T(1,128)S(1)} %get-tuple-element.39.keep, ...), custom_call_target="tpu_custom_call" | custom-call | flops 4000000000 | bytes 12000000 | tf_op jit(solution)/shard_map/finish/pallas_call | solution.py:474
  (8 shorter events, 0.0 us)
Async XLA Ops:
  3.9 1.7 %collective-permute-start = (bf16[5,4,16,256]{3,2,1,0:T(8,128)(2,1)}, bf16[5,4,16,256]{3,2,1,0:T(8,128)(2,1)S(1)}, u32[]{:S(2)}, u32[]{:S(2)}) collective-permute-start(bf16[5,4,16,256]{3,2,1,0:T(8,128)(2,1)} %get-tuple-element.26), channel_id=1, source_target_pairs={{0,64},{1,65},{2,66},{3,67},{4,68},{5,69},{6,70},{7,71},{8,72},{9,... | collective-permute-start | bytes 491528 | tf_op jit(solution)/shard_map/ppermute | solution.py:338
  4.0 0.9 %copy-start.4 = (bf16[16,16,256]{2,1,0:T(8,128)(2,1)S(1)}, bf16[16,16,256]{2,1,0:T(8,128)(2,1)}, u32[]{:S(2)}) copy-start(bf16[16,16,256]{2,1,0:T(8,128)(2,1)} %get-tuple-element.24.tabs) | copy-start | bytes 393220
  4.9 11.8 %copy-start = (f32[112,2048]{1,0:T(8,128)S(1)}, f32[112,2048]{1,0:T(8,128)}, u32[]{:S(2)}) copy-start(f32[112,2048]{1,0:T(8,128)} %get-tuple-element.25.mixr) | copy-start | bytes 2752516
  5.6 12.5 %collective-permute-start.3 = (bf16[4,16,256]{2,1,0:T(8,128)(2,1)S(1)}, bf16[4,16,256]{2,1,0:T(8,128)(2,1)S(1)}, u32[]{:S(2)}, u32[]{:S(2)}) collective-permute-start(bf16[4,16,256]{2,1,0:T(8,128)(2,1)S(1)} %get-tuple-element.31), channel_id=1, source_target_pairs={{0,2},{1,3},{2,0},{3,1},{4,6},{5,7},{6,4},{7,5},{8,10},{9,11},{10,... | collective-permute-start | bytes 98312 | tf_op jit(solution)/shard_map/ppermute | solution.py:344
  8.8 17.4 %collective-permute-start.4 = (bf16[4,16,256]{2,1,0:T(8,128)(2,1)S(1)}, bf16[4,16,256]{2,1,0:T(8,128)(2,1)S(1)}, u32[]{:S(2)}, u32[]{:S(2)}) collective-permute-start(bf16[4,16,256]{2,1,0:T(8,128)(2,1)S(1)} %get-tuple-element.33), channel_id=1, source_target_pairs={{0,62},{1,63},{2,4},{3,5},{4,2},{5,3},{6,8},{7,9},{8,6},{9,7},{10,... | collective-permute-start | bytes 98312 | tf_op jit(solution)/shard_map/ppermute | solution.py:344
  15.2 11.0 %collective-permute-start.2 = (bf16[16,16,256]{2,1,0:T(8,128)(2,1)S(1)}, bf16[16,16,256]{2,1,0:T(8,128)(2,1)S(1)}, u32[]{:S(2)}, u32[]{:S(2)}) collective-permute-start(bf16[16,16,256]{2,1,0:T(8,128)(2,1)S(1)} %get-tuple-element.29), channel_id=1, source_target_pairs={{0,63},{1,2},{2,1},{3,4},{4,3},{5,6},{6,5},{7,8},{8,7},{9,10},{10,... | collective-permute-start | bytes 393224 | tf_op jit(solution)/shard_map/ppermute | solution.py:344
  16.3 9.9 %collective-permute-start.1 = (bf16[16,16,256]{2,1,0:T(8,128)(2,1)S(1)}, bf16[16,16,256]{2,1,0:T(8,128)(2,1)S(1)}, u32[]{:S(2)}, u32[]{:S(2)}) collective-permute-start(bf16[16,16,256]{2,1,0:T(8,128)(2,1)S(1)} %get-tuple-element.27.after), channel_id=1, source_target_pairs={{0,1},{1,0},{2,3},{3,2},{4,5},{5,4},{6,7},{7,6},{8,9},{9,8},{10,11... | collective-permute-start | bytes 393224 | tf_op jit(solution)/shard_map/ppermute | solution.py:344
  16.7 9.5 %copy-start.1 = (bf16[1,1,8,2,256,256]{5,4,3,2,1,0:T(8,128)(2,1)S(1)}, bf16[1,1,8,2,256,256]{5,4,3,2,1,0:T(8,128)(2,1)}, u32[]{:S(2)}) copy-start(bf16[1,1,8,2,256,256]{5,4,3,2,1,0:T(8,128)(2,1)} %param.19) | copy-start | bytes 6291460
  16.7 9.5 %copy-start.2 = (s32[1,1,8,2]{2,3,1,0:T(2,128)S(1)}, s32[1,1,8,2]{2,3,1,0:T(2,128)}, u32[]{:S(2)}) copy-start(s32[1,1,8,2]{2,3,1,0:T(2,128)} %param.18) | copy-start | bytes 196
  16.7 9.5 %copy-start.3 = (s32[1,1,5]{2,1,0:T(1,128)S(1)}, s32[1,1,5]{2,1,0:T(1,128)}, u32[]{:S(2)}) copy-start(s32[1,1,5]{2,1,0:T(1,128)} %param.17) | copy-start | bytes 64
  16.7 9.5 %copy-start.5 = (f32[16,2048]{1,0:T(8,128)S(1)}, f32[16,2048]{1,0:T(8,128)}, u32[]{:S(2)}) copy-start(f32[16,2048]{1,0:T(8,128)} %get-tuple-element.34.mix0) | copy-start | bytes 393220
  16.7 9.5 %copy-start.6 = (f32[16,2048]{1,0:T(8,128)S(1)}, f32[16,2048]{1,0:T(8,128)}, u32[]{:S(2)}) copy-start(f32[16,2048]{1,0:T(8,128)} %get-tuple-element.35.gate) | copy-start | bytes 393220
  18.1 18.2 %collective-permute-start.7 = (bf16[112,2048]{1,0:T(8,128)(2,1)S(1)}, bf16[112,2048]{1,0:T(8,128)(2,1)S(1)}, u32[]{:S(2)}, u32[]{:S(2)}) collective-permute-start(bf16[112,2048]{1,0:T(8,128)(2,1)S(1)} %get-tuple-element.40.bulk), channel_id=1, source_target_pairs={{0,1},{1,0},{2,3},{3,2},{4,5},{5,4},{6,7},{7,6},{8,9},{9,8},{10,11... | collective-permute-start | bytes 1376264 | tf_op jit(solution)/shard_map/ppermute | solution.py:344
  19.8 18.9 %collective-permute-start.5 = (bf16[112,2048]{1,0:T(8,128)(2,1)S(1)}, bf16[112,2048]{1,0:T(8,128)(2,1)S(1)}, u32[]{:S(2)}, u32[]{:S(2)}) collective-permute-start(bf16[112,2048]{1,0:T(8,128)(2,1)S(1)} %get-tuple-element.40.bulk), channel_id=1, source_target_pairs={{0,63},{1,2},{2,1},{3,4},{4,3},{5,6},{6,5},{7,8},{8,7},{9,10},{10,... | collective-permute-start | bytes 1376264 | tf_op jit(solution)/shard_map/ppermute | solution.py:344
  28.2 8.1 %collective-permute-start.8 = (bf16[16,2048]{1,0:T(8,128)(2,1)S(1)}, bf16[16,2048]{1,0:T(8,128)(2,1)S(1)}, u32[]{:S(2)}, u32[]{:S(2)}) collective-permute-start(bf16[16,2048]{1,0:T(8,128)(2,1)S(1)} %get-tuple-element.36.after.top_half), channel_id=1, source_target_pairs={{0,1},{1,0},{2,3},{3,2},{4,5},{5,4},{6,7},{7,6},{8,9},{9,8},{10,11... | collective-permute-start | bytes 196616 | tf_op jit(solution)/shard_map/ppermute | solution.py:344
  28.2 10.5 %collective-permute-start.6 = (bf16[16,2048]{1,0:T(8,128)(2,1)S(1)}, bf16[16,2048]{1,0:T(8,128)(2,1)S(1)}, u32[]{:S(2)}, u32[]{:S(2)}) collective-permute-start(bf16[16,2048]{1,0:T(8,128)(2,1)S(1)} %get-tuple-element.36.after.top_half), channel_id=1, source_target_pairs={{0,63},{1,2},{2,1},{3,4},{4,3},{5,6},{6,5},{7,8},{8,7},{9,10},{10,... | collective-permute-start | bytes 196616 | tf_op jit(solution)/shard_map/ppermute | solution.py:344

commit v8 on v7

--- a/solution.py
+++ b/solution.py
@@ -431,8 +431,10 @@
         cost_estimate=cost(3),
         name="own_band",
     )(tabs, mixr, staged)
-    bulk_later, e2 = lax.optimization_barrier((bulk, e2))
-    bulk_e, bulk_o = paired(bulk_later, 1, False), paired(bulk_later, 1, True)
+    bulk_first, e2 = lax.optimization_barrier((bulk, e2))
+    bulk_o = paired(bulk_first, 1, True)
+    bulk_then, e1 = lax.optimization_barrier((bulk, e1))
+    bulk_e = paired(bulk_then, 1, False)
 
     forcing, top, top_half = pl.pallas_call(
         remap_kernel,

time: 43.5 us -> 44.2 us (1.016)
  waiting for transfers between devices: 0.68 us -> 2.32 us
  starting transfers between devices: 22.1 us -> 21.2 us
    ppermute x8, waiting for transfers between devices: 0.02 us -> 1.65 us  [paired(): return lax.ppermute(value, 'dom', pairs)]
    ppermute x8, starting transfers between devices: 22 us -> 21.1 us  [paired(): return lax.ppermute(value, 'dom', pairs)]
  transfers between devices with their start and end apart: 9 -> 9, of which waited for: 1 -> 3; matrix products, arithmetic and copies ran while one was open for 0% -> 0% of each run, Pallas kernels for 25% -> 25%
where the time goes in v8:
time: 44.2 us; the launch traced here: 44.1 us
  starting transfers between devices  21.2 us (48%)
  Pallas kernels  18.7 us (42%)
  waiting for transfers between devices  2.32 us (5%)
  local copies, waits for them, and re-layouts  0.93 us (2%)
  between operations  0.93 us (2%)
    ppermute x8, starting transfers between devices, paired(): return lax.ppermute(value, 'dom', pairs)  21.1 us
    pallas_call x1, Pallas kernels, shards(): pl.pallas_call(side_band_kernel, out_shape=[shape((2 * WIDE // TB, WIN, T...  5.23 us
    pallas_call x1, Pallas kernels, shards(): pl.pallas_call(finish_kernel, out_shape=shape((LEVELS * FIELDS, COLS), F3...  4.5 us
    pallas_call x1, Pallas kernels, shards(): pl.pallas_call(mix_kernel, out_shape=[shape((5, 4, FIELDS, TB), BF16), sh...  3.24 us
    pallas_call x1, Pallas kernels, shards(): pl.pallas_call(begin_kernel, out_shape=[shape(narrow, F32), shape(wide, B...  2.37 us
    pallas_call x1, Pallas kernels, shards(): pl.pallas_call(remap_kernel, out_shape=[shape((FIELDS, COLS), F32), shape...  1.96 us
    ppermute x8, waiting for transfers between devices, paired(): return lax.ppermute(value, 'dom', pairs)  1.65 us
    pallas_call x1, Pallas kernels, shards(): pl.pallas_call(own_band_kernel, out_shape=[shape((EARLY, WIN, TB), BF16),...  1.34 us
  transfers between devices with their start and end apart: 9, of which 3 were waited for; matrix products, arithmetic and copies ran while one was open for 0% of the time, Pallas kernels for 25%

profile of v8, /device:TPU:0, one launch (start us, length us, event | category | flops | bytes accessed | tf_op | source)
XLA Modules:
  0.0 44.1 jit_solution(3812984956439896509)
XLA Ops:
  0.6 3.2 %mix.1 = (bf16[5,4,16,256]{3,2,1,0:T(8,128)(2,1)}, f32[16,2048]{1,0:T(8,128)}, f32[112,2048]{1,0:T(8,128)}, bf16[16,16,256]{2,1,0:T(8,128)(2,1)}, f32[16,2048]{1,0:T(8,128)}) custom-call(f32[1,8,16,2048]{3,2,1,0:T(8,128)} %state_hbm.1, f32[7,1,2048]{2,1,0:T(1,128)} %bitcast.15, s32[5,4,256]{2,1,0:T(4,128)} %bitcast.18, s32[6,1,2048]{2,1,0:T(1,128)} %bitcast.16, ...), custom_call_target="tpu_custom_call" | custom-call | flops 3000000000 | bytes 9000000 | tf_op jit(solution)/shard_map/mix/pallas_call | solution.py:369
  3.9 0.1 collective-permute-start
  4.0 0.0 copy-start.4
  4.0 0.9 %copy-done.4 = bf16[16,16,256]{2,1,0:T(8,128)(2,1)S(1)} copy-done((bf16[16,16,256]{2,1,0:T(8,128)(2,1)S(1)}, bf16[16,16,256]{2,1,0:T(8,128)(2,1)}, u32[]{:S(2)}) %copy-start.4) | copy-done | bytes 131096
  4.9 0.0 copy-start
  4.9 0.7 %collective-permute-done.swapped = bf16[5,4,16,256]{3,2,1,0:T(8,128)(2,1)S(1)} collective-permute-done((bf16[5,4,16,256]{3,2,1,0:T(8,128)(2,1)}, bf16[5,4,16,256]{3,2,1,0:T(8,128)(2,1)S(1)}, u32[]{:S(2)}, u32[]{:S(2)}) %collective-permute-start) | collective-permute-done | bytes 163872 | tf_op jit(solution)/shard_map/ppermute | solution.py:338
  5.6 3.2 %collective-permute-start.3 = (bf16[4,16,256]{2,1,0:T(8,128)(2,1)S(1)}, bf16[4,16,256]{2,1,0:T(8,128)(2,1)S(1)}, u32[]{:S(2)}, u32[]{:S(2)}) collective-permute-start(bf16[4,16,256]{2,1,0:T(8,128)(2,1)S(1)} %get-tuple-element.34), channel_id=1, source_target_pairs={{0,2},{1,3},{2,0},{3,1},{4,6},{5,7},{6,4},{7,5},{8,10},{9,11},{10,... | collective-permute-start | bytes 98312 | tf_op jit(solution)/shard_map/ppermute | solution.py:344
  8.8 6.4 %collective-permute-start.4 = (bf16[4,16,256]{2,1,0:T(8,128)(2,1)S(1)}, bf16[4,16,256]{2,1,0:T(8,128)(2,1)S(1)}, u32[]{:S(2)}, u32[]{:S(2)}) collective-permute-start(bf16[4,16,256]{2,1,0:T(8,128)(2,1)S(1)} %get-tuple-element.36), channel_id=1, source_target_pairs={{0,62},{1,63},{2,4},{3,5},{4,2},{5,3},{6,8},{7,9},{8,6},{9,7},{10,... | collective-permute-start | bytes 98312 | tf_op jit(solution)/shard_map/ppermute | solution.py:344
  15.2 1.1 %collective-permute-start.2 = (bf16[16,16,256]{2,1,0:T(8,128)(2,1)S(1)}, bf16[16,16,256]{2,1,0:T(8,128)(2,1)S(1)}, u32[]{:S(2)}, u32[]{:S(2)}) collective-permute-start(bf16[16,16,256]{2,1,0:T(8,128)(2,1)S(1)} %get-tuple-element.33), channel_id=1, source_target_pairs={{0,63},{1,2},{2,1},{3,4},{4,3},{5,6},{6,5},{7,8},{8,7},{9,10},{10,... | collective-permute-start | bytes 393224 | tf_op jit(solution)/shard_map/ppermute | solution.py:344
  16.3 0.4 collective-permute-start.1
  16.7 0.0 copy-done
  16.7 0.0 copy-start.5
  16.7 0.0 copy-start.6
  16.7 1.3 %own_band.1 = (bf16[4,1280,256]{2,1,0:T(8,128)(2,1)S(1)}, bf16[112,2048]{1,0:T(8,128)(2,1)S(1)}) custom-call(bf16[16,16,256]{2,1,0:T(8,128)(2,1)S(1)} %hold.1.tabs, f32[112,2048]{1,0:T(8,128)S(1)} %copy-done, bf16[16,16,256]{2,1,0:T(8,128)(2,1)S(1)} %get-tuple-element.29.after), custom_call_target="tpu_custom_call" | custom-call | flops 3000000000 | bytes 9000000 | tf_op jit(solution)/shard_map/own_band/pallas_call | solution.py:424
  18.1 0.0 collective-permute-done.3.e2
  18.1 6.1 %collective-permute-start.5 = (bf16[112,2048]{1,0:T(8,128)(2,1)S(1)}, bf16[112,2048]{1,0:T(8,128)(2,1)S(1)}, u32[]{:S(2)}, u32[]{:S(2)}) collective-permute-start(bf16[112,2048]{1,0:T(8,128)(2,1)S(1)} %get-tuple-element.45.bulk), channel_id=1, source_target_pairs={{0,63},{1,2},{2,1},{3,4},{4,3},{5,6},{6,5},{7,8},{8,7},{9,10},{10,... | collective-permute-start | bytes 1376264 | tf_op jit(solution)/shard_map/ppermute | solution.py:344
  24.2 0.0 collective-permute-done.1.e1
  24.2 0.0 collective-permute-start.7
  24.2 0.0 collective-permute-done.4.o2
  24.2 1.5 %collective-permute-done.2.o1 = bf16[16,16,256]{2,1,0:T(8,128)(2,1)S(1)} collective-permute-done((bf16[16,16,256]{2,1,0:T(8,128)(2,1)S(1)}, bf16[16,16,256]{2,1,0:T(8,128)(2,1)S(1)}, u32[]{:S(2)}, u32[]{:S(2)}) %collective-permute-start.2) | collective-permute-done | bytes 131104 | tf_op jit(solution)/shard_map/ppermute | solution.py:344
  25.7 0.0 copy-done.5
  25.7 0.0 copy-done.6
  25.7 2.0 %remap.1 = (f32[16,2048]{1,0:T(8,128)}, f32[16,2048]{1,0:T(8,128)S(1)}, bf16[16,2048]{1,0:T(8,128)(2,1)S(1)}) custom-call(s32[1,5]{1,0:T(1,128)S(1)} %bitcast.13, s32[2,8]{1,0:T(2,128)S(1)} %bitcast.12, bf16[16,16,256]{2,1,0:T(8,128)(2,1)S(1)} %collective-permute-done.1.e1, bf16[16,16,256]{2,1,0:T(8,128)(2,1)S(1)} %collective-permute-done.2.o1, ...), custom_call_target="tpu_custom_call" | custom-call | flops 20000000000 | bytes 60000000 | tf_op jit(solution)/shard_map/remap/pallas_call | solution.py:439
  27.7 0.5 %collective-permute-start.8 = (bf16[16,2048]{1,0:T(8,128)(2,1)S(1)}, bf16[16,2048]{1,0:T(8,128)(2,1)S(1)}, u32[]{:S(2)}, u32[]{:S(2)}) collective-permute-start(bf16[16,2048]{1,0:T(8,128)(2,1)S(1)} %get-tuple-element.39.after.top_half), channel_id=1, source_target_pairs={{0,1},{1,0},{2,3},{3,2},{4,5},{5,4},{6,7},{7,6},{8,9},{9,8},{10,11... | collective-permute-start | bytes 196616 | tf_op jit(solution)/shard_map/ppermute | solution.py:344
  28.2 3.5 %collective-permute-start.6 = (bf16[16,2048]{1,0:T(8,128)(2,1)S(1)}, bf16[16,2048]{1,0:T(8,128)(2,1)S(1)}, u32[]{:S(2)}, u32[]{:S(2)}) collective-permute-start(bf16[16,2048]{1,0:T(8,128)(2,1)S(1)} %get-tuple-element.39.after.top_half), channel_id=1, source_target_pairs={{0,63},{1,2},{2,1},{3,4},{4,3},{5,6},{6,5},{7,8},{8,7},{9,10},{10,... | collective-permute-start | bytes 196616 | tf_op jit(solution)/shard_map/ppermute | solution.py:344
  31.7 5.2 %side_band.1 = (bf16[12,1280,256]{2,1,0:T(8,128)(2,1)S(1)}, bf16[4,1280,256]{2,1,0:T(8,128)(2,1)S(1)}, f32[1,5120]{1,0:T(1,128)S(1)}) custom-call(bf16[16,16,256]{2,1,0:T(8,128)(2,1)S(1)} %collective-permute-done.1.e1, bf16[16,16,256]{2,1,0:T(8,128)(2,1)S(1)} %hold.1.tabs, bf16[16,16,256]{2,1,0:T(8,128)(2,1)S(1)} %collective-permute-done.2.o1, ...), custom_call_target="tpu_custom_call" | custom-call | flops 1000000000 | bytes 3000000 | tf_op jit(solution)/shard_map/side_band/pallas_call | solution.py:453
  36.9 0.1 collective-permute-done.8.top_e
  37.0 0.0 collective-permute-done.7.bulk_e
  37.0 2.4 %begin.1 = (f32[128,5120]{1,0:T(8,128)S(1)}, bf16[128,6144]{1,0:T(8,128)(2,1)S(1)}, bf16[128,6144]{1,0:T(8,128)(2,1)S(1)}) custom-call(bf16[4,1280,256]{2,1,0:T(8,128)(2,1)S(1)} %get-tuple-element.30.after.band_own, bf16[4,1280,256]{2,1,0:T(8,128)(2,1)S(1)} %get-tuple-element.40.band_late, bf16[12,1280,256]{2,1,0:T(8,128)(2,1)S(1)} %get-tuple-element.41.band_side, ...), custom_call_target="tpu_custom_call" | custom-call | flops 1000000000 | bytes 3000000 | tf_op jit(solution)/shard_map/begin/pallas_call | solution.py:466
  39.4 0.0 collective-permute-done.6.top_o
  39.4 0.0 collective-permute-done.5.bulk_o
  39.4 4.5 %finish.1 = f32[128,2048]{1,0:T(8,128)} custom-call(bf16[4,1280,256]{2,1,0:T(8,128)(2,1)S(1)} %get-tuple-element.30.after.band_own, bf16[4,1280,256]{2,1,0:T(8,128)(2,1)S(1)} %get-tuple-element.40.band_late, bf16[12,1280,256]{2,1,0:T(8,128)(2,1)S(1)} %get-tuple-element.41.band_side, f32[1,5120]{1,0:T(1,128)S(1)} %get-tuple-element.42.keep, ...), custom_call_target="tpu_custom_call" | custom-call | flops 4000000000 | bytes 12000000 | tf_op jit(solution)/shard_map/finish/pallas_call | solution.py:476
  (8 shorter events, 0.0 us)
Async XLA Ops:
  3.9 1.7 %collective-permute-start = (bf16[5,4,16,256]{3,2,1,0:T(8,128)(2,1)}, bf16[5,4,16,256]{3,2,1,0:T(8,128)(2,1)S(1)}, u32[]{:S(2)}, u32[]{:S(2)}) collective-permute-start(bf16[5,4,16,256]{3,2,1,0:T(8,128)(2,1)} %get-tuple-element.28), channel_id=1, source_target_pairs={{0,64},{1,65},{2,66},{3,67},{4,68},{5,69},{6,70},{7,71},{8,72},{9,... | collective-permute-start | bytes 491528 | tf_op jit(solution)/shard_map/ppermute | solution.py:338
  4.0 0.9 %copy-start.4 = (bf16[16,16,256]{2,1,0:T(8,128)(2,1)S(1)}, bf16[16,16,256]{2,1,0:T(8,128)(2,1)}, u32[]{:S(2)}) copy-start(bf16[16,16,256]{2,1,0:T(8,128)(2,1)} %get-tuple-element.26.tabs) | copy-start | bytes 393220
  4.9 11.8 %copy-start = (f32[112,2048]{1,0:T(8,128)S(1)}, f32[112,2048]{1,0:T(8,128)}, u32[]{:S(2)}) copy-start(f32[112,2048]{1,0:T(8,128)} %get-tuple-element.27.mixr) | copy-start | bytes 2752516
  5.6 12.5 %collective-permute-start.3 = (bf16[4,16,256]{2,1,0:T(8,128)(2,1)S(1)}, bf16[4,16,256]{2,1,0:T(8,128)(2,1)S(1)}, u32[]{:S(2)}, u32[]{:S(2)}) collective-permute-start(bf16[4,16,256]{2,1,0:T(8,128)(2,1)S(1)} %get-tuple-element.34), channel_id=1, source_target_pairs={{0,2},{1,3},{2,0},{3,1},{4,6},{5,7},{6,4},{7,5},{8,10},{9,11},{10,... | collective-permute-start | bytes 98312 | tf_op jit(solution)/shard_map/ppermute | solution.py:344
  8.8 15.4 %collective-permute-start.4 = (bf16[4,16,256]{2,1,0:T(8,128)(2,1)S(1)}, bf16[4,16,256]{2,1,0:T(8,128)(2,1)S(1)}, u32[]{:S(2)}, u32[]{:S(2)}) collective-permute-start(bf16[4,16,256]{2,1,0:T(8,128)(2,1)S(1)} %get-tuple-element.36), channel_id=1, source_target_pairs={{0,62},{1,63},{2,4},{3,5},{4,2},{5,3},{6,8},{7,9},{8,6},{9,7},{10,... | collective-permute-start | bytes 98312 | tf_op jit(solution)/shard_map/ppermute | solution.py:344
  15.2 10.5 %collective-permute-start.2 = (bf16[16,16,256]{2,1,0:T(8,128)(2,1)S(1)}, bf16[16,16,256]{2,1,0:T(8,128)(2,1)S(1)}, u32[]{:S(2)}, u32[]{:S(2)}) collective-permute-start(bf16[16,16,256]{2,1,0:T(8,128)(2,1)S(1)} %get-tuple-element.33), channel_id=1, source_target_pairs={{0,63},{1,2},{2,1},{3,4},{4,3},{5,6},{6,5},{7,8},{8,7},{9,10},{10,... | collective-permute-start | bytes 393224 | tf_op jit(solution)/shard_map/ppermute | solution.py:344
  16.3 7.9 %collective-permute-start.1 = (bf16[16,16,256]{2,1,0:T(8,128)(2,1)S(1)}, bf16[16,16,256]{2,1,0:T(8,128)(2,1)S(1)}, u32[]{:S(2)}, u32[]{:S(2)}) collective-permute-start(bf16[16,16,256]{2,1,0:T(8,128)(2,1)S(1)} %get-tuple-element.29.after), channel_id=1, source_target_pairs={{0,1},{1,0},{2,3},{3,2},{4,5},{5,4},{6,7},{7,6},{8,9},{9,8},{10,11... | collective-permute-start | bytes 393224 | tf_op jit(solution)/shard_map/ppermute | solution.py:344
  16.7 9.0 %copy-start.1 = (bf16[1,1,8,2,256,256]{5,4,3,2,1,0:T(8,128)(2,1)S(1)}, bf16[1,1,8,2,256,256]{5,4,3,2,1,0:T(8,128)(2,1)}, u32[]{:S(2)}) copy-start(bf16[1,1,8,2,256,256]{5,4,3,2,1,0:T(8,128)(2,1)} %param.19) | copy-start | bytes 6291460
  16.7 9.0 %copy-start.2 = (s32[1,1,8,2]{2,3,1,0:T(2,128)S(1)}, s32[1,1,8,2]{2,3,1,0:T(2,128)}, u32[]{:S(2)}) copy-start(s32[1,1,8,2]{2,3,1,0:T(2,128)} %param.18) | copy-start | bytes 196
  16.7 9.0 %copy-start.3 = (s32[1,1,5]{2,1,0:T(1,128)S(1)}, s32[1,1,5]{2,1,0:T(1,128)}, u32[]{:S(2)}) copy-start(s32[1,1,5]{2,1,0:T(1,128)} %param.17) | copy-start | bytes 64
  16.7 9.0 %copy-start.5 = (f32[16,2048]{1,0:T(8,128)S(1)}, f32[16,2048]{1,0:T(8,128)}, u32[]{:S(2)}) copy-start(f32[16,2048]{1,0:T(8,128)} %get-tuple-element.37.mix0) | copy-start | bytes 393220
  16.7 9.0 %copy-start.6 = (f32[16,2048]{1,0:T(8,128)S(1)}, f32[16,2048]{1,0:T(8,128)}, u32[]{:S(2)}) copy-start(f32[16,2048]{1,0:T(8,128)} %get-tuple-element.38.gate) | copy-start | bytes 393220
  18.1 21.3 %collective-permute-start.5 = (bf16[112,2048]{1,0:T(8,128)(2,1)S(1)}, bf16[112,2048]{1,0:T(8,128)(2,1)S(1)}, u32[]{:S(2)}, u32[]{:S(2)}) collective-permute-start(bf16[112,2048]{1,0:T(8,128)(2,1)S(1)} %get-tuple-element.45.bulk), channel_id=1, source_target_pairs={{0,63},{1,2},{2,1},{3,4},{4,3},{5,6},{6,5},{7,8},{8,7},{9,10},{10,... | collective-permute-start | bytes 1376264 | tf_op jit(solution)/shard_map/ppermute | solution.py:344
  24.2 12.9 %collective-permute-start.7 = (bf16[112,2048]{1,0:T(8,128)(2,1)S(1)}, bf16[112,2048]{1,0:T(8,128)(2,1)S(1)}, u32[]{:S(2)}, u32[]{:S(2)}) collective-permute-start(bf16[112,2048]{1,0:T(8,128)(2,1)S(1)} %get-tuple-element.45.bulk), channel_id=1, source_target_pairs={{0,1},{1,0},{2,3},{3,2},{4,5},{5,4},{6,7},{7,6},{8,9},{9,8},{10,11... | collective-permute-start | bytes 1376264 | tf_op jit(solution)/shard_map/ppermute | solution.py:344
  27.7 9.3 %collective-permute-start.8 = (bf16[16,2048]{1,0:T(8,128)(2,1)S(1)}, bf16[16,2048]{1,0:T(8,128)(2,1)S(1)}, u32[]{:S(2)}, u32[]{:S(2)}) collective-permute-start(bf16[16,2048]{1,0:T(8,128)(2,1)S(1)} %get-tuple-element.39.after.top_half), channel_id=1, source_target_pairs={{0,1},{1,0},{2,3},{3,2},{4,5},{5,4},{6,7},{7,6},{8,9},{9,8},{10,11... | collective-permute-start | bytes 196616 | tf_op jit(solution)/shard_map/ppermute | solution.py:344
  28.2 11.2 %collective-permute-start.6 = (bf16[16,2048]{1,0:T(8,128)(2,1)S(1)}, bf16[16,2048]{1,0:T(8,128)(2,1)S(1)}, u32[]{:S(2)}, u32[]{:S(2)}) collective-permute-start(bf16[16,2048]{1,0:T(8,128)(2,1)S(1)} %get-tuple-element.39.after.top_half), channel_id=1, source_target_pairs={{0,63},{1,2},{2,1},{3,4},{4,3},{5,6},{6,5},{7,8},{8,7},{9,10},{10,... | collective-permute-start | bytes 196616 | tf_op jit(solution)/shard_map/ppermute | solution.py:344

commit v9 on v7

--- a/solution.py
+++ b/solution.py
@@ -16,7 +16,7 @@
 REST = (LEVELS - 1) * FIELDS
 WIDE = COLS - RIM
 PICK_MIB = 63
-EARLY = 4
+EARLY = 6
 PAY = 4 + 2 * WIDE // TB
 
 

time: 43.5 us -> 43.3 us (level)
  starting transfers between devices: 22.1 us -> 21.1 us
  waiting for transfers between devices: 0.68 us -> 1.57 us
    ppermute x8, starting transfers between devices: 22 us -> 21 us  [paired(): return lax.ppermute(value, 'dom', pairs)]
    ppermute x8, waiting for transfers between devices: 0.02 us -> 0.91 us  [paired(): return lax.ppermute(value, 'dom', pairs)]
    pallas_call x1, Pallas kernels: 5.23 us -> 4.59 us  [shards(): pl.pallas_call(side_band_kernel, out_shape=[shape((2 * WIDE // TB, WIN, T...]
    pallas_call x1, Pallas kernels: 1.34 us -> 1.99 us  [shards(): pl.pallas_call(own_band_kernel, out_shape=[shape((EARLY, WIN, TB), BF16),...]
  transfers between devices with their start and end apart: 9 -> 9, of which waited for: 1 -> 2; matrix products, arithmetic and copies ran while one was open for 0% -> 0% of each run, Pallas kernels for 25% -> 25%
where the time goes in v9:
time: 43.3 us; the launch traced here: 43.2 us
  starting transfers between devices  21.1 us (49%)
  Pallas kernels  18.7 us (43%)
  waiting for transfers between devices  1.57 us (4%)
  between operations  0.94 us (2%)
  local copies, waits for them, and re-layouts  0.93 us (2%)
    ppermute x8, starting transfers between devices, paired(): return lax.ppermute(value, 'dom', pairs)  21 us
    pallas_call x1, Pallas kernels, shards(): pl.pallas_call(side_band_kernel, out_shape=[shape((2 * WIDE // TB, WIN, T...  4.59 us
    pallas_call x1, Pallas kernels, shards(): pl.pallas_call(finish_kernel, out_shape=shape((LEVELS * FIELDS, COLS), F3...  4.5 us
    pallas_call x1, Pallas kernels, shards(): pl.pallas_call(mix_kernel, out_shape=[shape((5, 4, FIELDS, TB), BF16), sh...  3.24 us
    pallas_call x1, Pallas kernels, shards(): pl.pallas_call(begin_kernel, out_shape=[shape(narrow, F32), shape(wide, B...  2.38 us
    pallas_call x1, Pallas kernels, shards(): pl.pallas_call(own_band_kernel, out_shape=[shape((EARLY, WIN, TB), BF16),...  1.99 us
    pallas_call x1, Pallas kernels, shards(): pl.pallas_call(remap_kernel, out_shape=[shape((FIELDS, COLS), F32), shape...  1.96 us
    unnamed x14, local copies, waits for them, and re-layouts  0.93 us
  transfers between devices with their start and end apart: 9, of which 2 were waited for; matrix products, arithmetic and copies ran while one was open for 0% of the time, Pallas kernels for 25%

profile of v9, /device:TPU:0, one launch (start us, length us, event | category | flops | bytes accessed | tf_op | source)
XLA Modules:
  0.0 43.2 jit_solution(6072767067937802588)
XLA Ops:
  0.6 3.2 %mix.1 = (bf16[5,4,16,256]{3,2,1,0:T(8,128)(2,1)}, f32[16,2048]{1,0:T(8,128)}, f32[112,2048]{1,0:T(8,128)}, bf16[16,16,256]{2,1,0:T(8,128)(2,1)}, f32[16,2048]{1,0:T(8,128)}) custom-call(f32[1,8,16,2048]{3,2,1,0:T(8,128)} %state_hbm.1, f32[7,1,2048]{2,1,0:T(1,128)} %bitcast.15, s32[5,4,256]{2,1,0:T(4,128)} %bitcast.18, s32[6,1,2048]{2,1,0:T(1,128)} %bitcast.16, ...), custom_call_target="tpu_custom_call" | custom-call | flops 3000000000 | bytes 9000000 | tf_op jit(solution)/shard_map/mix/pallas_call | solution.py:369
  3.9 0.1 collective-permute-start
  4.0 0.0 copy-start.4
  4.0 0.9 %copy-done.4 = bf16[16,16,256]{2,1,0:T(8,128)(2,1)S(1)} copy-done((bf16[16,16,256]{2,1,0:T(8,128)(2,1)S(1)}, bf16[16,16,256]{2,1,0:T(8,128)(2,1)}, u32[]{:S(2)}) %copy-start.4) | copy-done | bytes 131096
  4.9 0.0 copy-start
  4.9 0.7 %collective-permute-done.swapped = bf16[5,4,16,256]{3,2,1,0:T(8,128)(2,1)S(1)} collective-permute-done((bf16[5,4,16,256]{3,2,1,0:T(8,128)(2,1)}, bf16[5,4,16,256]{3,2,1,0:T(8,128)(2,1)S(1)}, u32[]{:S(2)}, u32[]{:S(2)}) %collective-permute-start) | collective-permute-done | bytes 163872 | tf_op jit(solution)/shard_map/ppermute | solution.py:338
  5.6 3.2 %collective-permute-start.3 = (bf16[4,16,256]{2,1,0:T(8,128)(2,1)S(1)}, bf16[4,16,256]{2,1,0:T(8,128)(2,1)S(1)}, u32[]{:S(2)}, u32[]{:S(2)}) collective-permute-start(bf16[4,16,256]{2,1,0:T(8,128)(2,1)S(1)} %get-tuple-element.31), channel_id=1, source_target_pairs={{0,2},{1,3},{2,0},{3,1},{4,6},{5,7},{6,4},{7,5},{8,10},{9,11},{10,... | collective-permute-start | bytes 98312 | tf_op jit(solution)/shard_map/ppermute | solution.py:344
  8.8 6.4 %collective-permute-start.4 = (bf16[4,16,256]{2,1,0:T(8,128)(2,1)S(1)}, bf16[4,16,256]{2,1,0:T(8,128)(2,1)S(1)}, u32[]{:S(2)}, u32[]{:S(2)}) collective-permute-start(bf16[4,16,256]{2,1,0:T(8,128)(2,1)S(1)} %get-tuple-element.33), channel_id=1, source_target_pairs={{0,62},{1,63},{2,4},{3,5},{4,2},{5,3},{6,8},{7,9},{8,6},{9,7},{10,... | collective-permute-start | bytes 98312 | tf_op jit(solution)/shard_map/ppermute | solution.py:344
  15.2 1.1 %collective-permute-start.2 = (bf16[16,16,256]{2,1,0:T(8,128)(2,1)S(1)}, bf16[16,16,256]{2,1,0:T(8,128)(2,1)S(1)}, u32[]{:S(2)}, u32[]{:S(2)}) collective-permute-start(bf16[16,16,256]{2,1,0:T(8,128)(2,1)S(1)} %get-tuple-element.29), channel_id=1, source_target_pairs={{0,63},{1,2},{2,1},{3,4},{4,3},{5,6},{6,5},{7,8},{8,7},{9,10},{10,... | collective-permute-start | bytes 393224 | tf_op jit(solution)/shard_map/ppermute | solution.py:344
  16.3 0.4 %collective-permute-start.1 = (bf16[16,16,256]{2,1,0:T(8,128)(2,1)S(1)}, bf16[16,16,256]{2,1,0:T(8,128)(2,1)S(1)}, u32[]{:S(2)}, u32[]{:S(2)}) collective-permute-start(bf16[16,16,256]{2,1,0:T(8,128)(2,1)S(1)} %get-tuple-element.27.after), channel_id=1, source_target_pairs={{0,1},{1,0},{2,3},{3,2},{4,5},{5,4},{6,7},{7,6},{8,9},{9,8},{10,11... | collective-permute-start | bytes 393224 | tf_op jit(solution)/shard_map/ppermute | solution.py:344
  16.7 0.0 copy-done
  16.7 0.0 copy-start.5
  16.7 0.0 copy-start.6
  16.7 2.0 %own_band.1 = (bf16[6,1280,256]{2,1,0:T(8,128)(2,1)S(1)}, bf16[112,2048]{1,0:T(8,128)(2,1)S(1)}) custom-call(bf16[16,16,256]{2,1,0:T(8,128)(2,1)S(1)} %hold.1.tabs, f32[112,2048]{1,0:T(8,128)S(1)} %copy-done, bf16[16,16,256]{2,1,0:T(8,128)(2,1)S(1)} %get-tuple-element.27.after), custom_call_target="tpu_custom_call" | custom-call | flops 3000000000 | bytes 9000000 | tf_op jit(solution)/shard_map/own_band/pallas_call | solution.py:424
  18.7 0.0 collective-permute-done.3.e2
  18.7 1.7 %collective-permute-start.7 = (bf16[112,2048]{1,0:T(8,128)(2,1)S(1)}, bf16[112,2048]{1,0:T(8,128)(2,1)S(1)}, u32[]{:S(2)}, u32[]{:S(2)}) collective-permute-start(bf16[112,2048]{1,0:T(8,128)(2,1)S(1)} %get-tuple-element.40.bulk), channel_id=1, source_target_pairs={{0,1},{1,0},{2,3},{3,2},{4,5},{5,4},{6,7},{7,6},{8,9},{9,8},{10,11... | collective-permute-start | bytes 1376264 | tf_op jit(solution)/shard_map/ppermute | solution.py:344
  20.4 6.4 %collective-permute-start.5 = (bf16[112,2048]{1,0:T(8,128)(2,1)S(1)}, bf16[112,2048]{1,0:T(8,128)(2,1)S(1)}, u32[]{:S(2)}, u32[]{:S(2)}) collective-permute-start(bf16[112,2048]{1,0:T(8,128)(2,1)S(1)} %get-tuple-element.40.bulk), channel_id=1, source_target_pairs={{0,63},{1,2},{2,1},{3,4},{4,3},{5,6},{6,5},{7,8},{8,7},{9,10},{10,... | collective-permute-start | bytes 1376264 | tf_op jit(solution)/shard_map/ppermute | solution.py:344
  26.8 0.0 collective-permute-done.4.o2
  26.8 0.0 collective-permute-done.2.o1
  26.8 0.0 collective-permute-done.1.e1
  26.8 0.0 copy-done.1
  26.8 0.0 copy-done.2
  26.9 2.0 %remap.1 = (f32[16,2048]{1,0:T(8,128)}, f32[16,2048]{1,0:T(8,128)S(1)}, bf16[16,2048]{1,0:T(8,128)(2,1)S(1)}) custom-call(s32[1,5]{1,0:T(1,128)S(1)} %bitcast.13, s32[2,8]{1,0:T(2,128)S(1)} %bitcast.12, bf16[16,16,256]{2,1,0:T(8,128)(2,1)S(1)} %collective-permute-done.1.e1, bf16[16,16,256]{2,1,0:T(8,128)(2,1)S(1)} %collective-permute-done.2.o1, ...), custom_call_target="tpu_custom_call" | custom-call | flops 20000000000 | bytes 60000000 | tf_op jit(solution)/shard_map/remap/pallas_call | solution.py:437
  28.8 0.0 collective-permute-start.8
  28.8 1.8 %collective-permute-start.6 = (bf16[16,2048]{1,0:T(8,128)(2,1)S(1)}, bf16[16,2048]{1,0:T(8,128)(2,1)S(1)}, u32[]{:S(2)}, u32[]{:S(2)}) collective-permute-start(bf16[16,2048]{1,0:T(8,128)(2,1)S(1)} %get-tuple-element.36.after.top_half), channel_id=1, source_target_pairs={{0,63},{1,2},{2,1},{3,4},{4,3},{5,6},{6,5},{7,8},{8,7},{9,10},{10,... | collective-permute-start | bytes 196616 | tf_op jit(solution)/shard_map/ppermute | solution.py:344
  30.6 4.6 %side_band.1 = (bf16[12,1280,256]{2,1,0:T(8,128)(2,1)S(1)}, bf16[2,1280,256]{2,1,0:T(8,128)(2,1)S(1)}, f32[1,5120]{1,0:T(1,128)S(1)}) custom-call(bf16[16,16,256]{2,1,0:T(8,128)(2,1)S(1)} %collective-permute-done.1.e1, bf16[16,16,256]{2,1,0:T(8,128)(2,1)S(1)} %hold.1.tabs, bf16[16,16,256]{2,1,0:T(8,128)(2,1)S(1)} %collective-permute-done.2.o1, ...), custom_call_target="tpu_custom_call" | custom-call | flops 1000000000 | bytes 3000000 | tf_op jit(solution)/shard_map/side_band/pallas_call | solution.py:451
  35.2 0.0 collective-permute-done.8.top_e
  35.2 0.0 collective-permute-done.7.bulk_e
  35.2 2.4 %begin.1 = (f32[128,5120]{1,0:T(8,128)S(1)}, bf16[128,6144]{1,0:T(8,128)(2,1)S(1)}, bf16[128,6144]{1,0:T(8,128)(2,1)S(1)}) custom-call(bf16[6,1280,256]{2,1,0:T(8,128)(2,1)S(1)} %get-tuple-element.28.after.band_own, bf16[2,1280,256]{2,1,0:T(8,128)(2,1)S(1)} %get-tuple-element.37.band_late, bf16[12,1280,256]{2,1,0:T(8,128)(2,1)S(1)} %get-tuple-element.38.band_side, ...), custom_call_target="tpu_custom_call" | custom-call | flops 1000000000 | bytes 3000000 | tf_op jit(solution)/shard_map/begin/pallas_call | solution.py:464
  37.6 0.9 %collective-permute-done.6.top_o = bf16[16,2048]{1,0:T(8,128)(2,1)S(1)} collective-permute-done((bf16[16,2048]{1,0:T(8,128)(2,1)S(1)}, bf16[16,2048]{1,0:T(8,128)(2,1)S(1)}, u32[]{:S(2)}, u32[]{:S(2)}) %collective-permute-start.6) | collective-permute-done | bytes 65568 | tf_op jit(solution)/shard_map/ppermute | solution.py:344
  38.5 0.0 collective-permute-done.5.bulk_o
  38.5 4.5 %finish.1 = f32[128,2048]{1,0:T(8,128)} custom-call(bf16[6,1280,256]{2,1,0:T(8,128)(2,1)S(1)} %get-tuple-element.28.after.band_own, bf16[2,1280,256]{2,1,0:T(8,128)(2,1)S(1)} %get-tuple-element.37.band_late, bf16[12,1280,256]{2,1,0:T(8,128)(2,1)S(1)} %get-tuple-element.38.band_side, f32[1,5120]{1,0:T(1,128)S(1)} %get-tuple-element.39.keep, ...), custom_call_target="tpu_custom_call" | custom-call | flops 4000000000 | bytes 12000000 | tf_op jit(solution)/shard_map/finish/pallas_call | solution.py:474
  (8 shorter events, 0.0 us)
Async XLA Ops:
  3.9 1.7 %collective-permute-start = (bf16[5,4,16,256]{3,2,1,0:T(8,128)(2,1)}, bf16[5,4,16,256]{3,2,1,0:T(8,128)(2,1)S(1)}, u32[]{:S(2)}, u32[]{:S(2)}) collective-permute-start(bf16[5,4,16,256]{3,2,1,0:T(8,128)(2,1)} %get-tuple-element.26), channel_id=1, source_target_pairs={{0,64},{1,65},{2,66},{3,67},{4,68},{5,69},{6,70},{7,71},{8,72},{9,... | collective-permute-start | bytes 491528 | tf_op jit(solution)/shard_map/ppermute | solution.py:338
  4.0 0.9 %copy-start.4 = (bf16[16,16,256]{2,1,0:T(8,128)(2,1)S(1)}, bf16[16,16,256]{2,1,0:T(8,128)(2,1)}, u32[]{:S(2)}) copy-start(bf16[16,16,256]{2,1,0:T(8,128)(2,1)} %get-tuple-element.24.tabs) | copy-start | bytes 393220
  4.9 11.8 %copy-start = (f32[112,2048]{1,0:T(8,128)S(1)}, f32[112,2048]{1,0:T(8,128)}, u32[]{:S(2)}) copy-start(f32[112,2048]{1,0:T(8,128)} %get-tuple-element.25.mixr) | copy-start | bytes 2752516
  5.6 13.1 %collective-permute-start.3 = (bf16[4,16,256]{2,1,0:T(8,128)(2,1)S(1)}, bf16[4,16,256]{2,1,0:T(8,128)(2,1)S(1)}, u32[]{:S(2)}, u32[]{:S(2)}) collective-permute-start(bf16[4,16,256]{2,1,0:T(8,128)(2,1)S(1)} %get-tuple-element.31), channel_id=1, source_target_pairs={{0,2},{1,3},{2,0},{3,1},{4,6},{5,7},{6,4},{7,5},{8,10},{9,11},{10,... | collective-permute-start | bytes 98312 | tf_op jit(solution)/shard_map/ppermute | solution.py:344
  8.8 18.0 %collective-permute-start.4 = (bf16[4,16,256]{2,1,0:T(8,128)(2,1)S(1)}, bf16[4,16,256]{2,1,0:T(8,128)(2,1)S(1)}, u32[]{:S(2)}, u32[]{:S(2)}) collective-permute-start(bf16[4,16,256]{2,1,0:T(8,128)(2,1)S(1)} %get-tuple-element.33), channel_id=1, source_target_pairs={{0,62},{1,63},{2,4},{3,5},{4,2},{5,3},{6,8},{7,9},{8,6},{9,7},{10,... | collective-permute-start | bytes 98312 | tf_op jit(solution)/shard_map/ppermute | solution.py:344
  15.2 11.6 %collective-permute-start.2 = (bf16[16,16,256]{2,1,0:T(8,128)(2,1)S(1)}, bf16[16,16,256]{2,1,0:T(8,128)(2,1)S(1)}, u32[]{:S(2)}, u32[]{:S(2)}) collective-permute-start(bf16[16,16,256]{2,1,0:T(8,128)(2,1)S(1)} %get-tuple-element.29), channel_id=1, source_target_pairs={{0,63},{1,2},{2,1},{3,4},{4,3},{5,6},{6,5},{7,8},{8,7},{9,10},{10,... | collective-permute-start | bytes 393224 | tf_op jit(solution)/shard_map/ppermute | solution.py:344
  16.3 10.6 %collective-permute-start.1 = (bf16[16,16,256]{2,1,0:T(8,128)(2,1)S(1)}, bf16[16,16,256]{2,1,0:T(8,128)(2,1)S(1)}, u32[]{:S(2)}, u32[]{:S(2)}) collective-permute-start(bf16[16,16,256]{2,1,0:T(8,128)(2,1)S(1)} %get-tuple-element.27.after), channel_id=1, source_target_pairs={{0,1},{1,0},{2,3},{3,2},{4,5},{5,4},{6,7},{7,6},{8,9},{9,8},{10,11... | collective-permute-start | bytes 393224 | tf_op jit(solution)/shard_map/ppermute | solution.py:344
  16.7 10.1 %copy-start.1 = (bf16[1,1,8,2,256,256]{5,4,3,2,1,0:T(8,128)(2,1)S(1)}, bf16[1,1,8,2,256,256]{5,4,3,2,1,0:T(8,128)(2,1)}, u32[]{:S(2)}) copy-start(bf16[1,1,8,2,256,256]{5,4,3,2,1,0:T(8,128)(2,1)} %param.19) | copy-start | bytes 6291460
  16.7 10.1 %copy-start.2 = (s32[1,1,8,2]{2,3,1,0:T(2,128)S(1)}, s32[1,1,8,2]{2,3,1,0:T(2,128)}, u32[]{:S(2)}) copy-start(s32[1,1,8,2]{2,3,1,0:T(2,128)} %param.18) | copy-start | bytes 196
  16.7 10.1 %copy-start.3 = (s32[1,1,5]{2,1,0:T(1,128)S(1)}, s32[1,1,5]{2,1,0:T(1,128)}, u32[]{:S(2)}) copy-start(s32[1,1,5]{2,1,0:T(1,128)} %param.17) | copy-start | bytes 64
  16.7 10.1 %copy-start.5 = (f32[16,2048]{1,0:T(8,128)S(1)}, f32[16,2048]{1,0:T(8,128)}, u32[]{:S(2)}) copy-start(f32[16,2048]{1,0:T(8,128)} %get-tuple-element.34.mix0) | copy-start | bytes 393220
  16.7 10.1 %copy-start.6 = (f32[16,2048]{1,0:T(8,128)S(1)}, f32[16,2048]{1,0:T(8,128)}, u32[]{:S(2)}) copy-start(f32[16,2048]{1,0:T(8,128)} %get-tuple-element.35.gate) | copy-start | bytes 393220
  18.7 16.5 %collective-permute-start.7 = (bf16[112,2048]{1,0:T(8,128)(2,1)S(1)}, bf16[112,2048]{1,0:T(8,128)(2,1)S(1)}, u32[]{:S(2)}, u32[]{:S(2)}) collective-permute-start(bf16[112,2048]{1,0:T(8,128)(2,1)S(1)} %get-tuple-element.40.bulk), channel_id=1, source_target_pairs={{0,1},{1,0},{2,3},{3,2},{4,5},{5,4},{6,7},{7,6},{8,9},{9,8},{10,11... | collective-permute-start | bytes 1376264 | tf_op jit(solution)/shard_map/ppermute | solution.py:344
  20.4 18.1 %collective-permute-start.5 = (bf16[112,2048]{1,0:T(8,128)(2,1)S(1)}, bf16[112,2048]{1,0:T(8,128)(2,1)S(1)}, u32[]{:S(2)}, u32[]{:S(2)}) collective-permute-start(bf16[112,2048]{1,0:T(8,128)(2,1)S(1)} %get-tuple-element.40.bulk), channel_id=1, source_target_pairs={{0,63},{1,2},{2,1},{3,4},{4,3},{5,6},{6,5},{7,8},{8,7},{9,10},{10,... | collective-permute-start | bytes 1376264 | tf_op jit(solution)/shard_map/ppermute | solution.py:344
  28.8 6.4 %collective-permute-start.8 = (bf16[16,2048]{1,0:T(8,128)(2,1)S(1)}, bf16[16,2048]{1,0:T(8,128)(2,1)S(1)}, u32[]{:S(2)}, u32[]{:S(2)}) collective-permute-start(bf16[16,2048]{1,0:T(8,128)(2,1)S(1)} %get-tuple-element.36.after.top_half), channel_id=1, source_target_pairs={{0,1},{1,0},{2,3},{3,2},{4,5},{5,4},{6,7},{7,6},{8,9},{9,8},{10,11... | collective-permute-start | bytes 196616 | tf_op jit(solution)/shard_map/ppermute | solution.py:344
  28.8 9.7 %collective-permute-start.6 = (bf16[16,2048]{1,0:T(8,128)(2,1)S(1)}, bf16[16,2048]{1,0:T(8,128)(2,1)S(1)}, u32[]{:S(2)}, u32[]{:S(2)}) collective-permute-start(bf16[16,2048]{1,0:T(8,128)(2,1)S(1)} %get-tuple-element.36.after.top_half), channel_id=1, source_target_pairs={{0,63},{1,2},{2,1},{3,4},{4,3},{5,6},{6,5},{7,8},{8,7},{9,10},{10,... | collective-permute-start | bytes 196616 | tf_op jit(solution)/shard_map/ppermute | solution.py:344
